TPU v7x, 32 devices: a whole 2x2x4 slice. The times are simulated.
32 devices in a mesh: dp: 4 (over z), fsdp: 8 (over y, x, core).
Axes of the slice: x: 2, y: 2, z: 4, core: 2. Of those that a mesh axis runs over, the one named last changes fastest.
Arguments:
- tokens: bfloat16 [64, 640, 768], P(('dp', 'fsdp')), may hold values from -6 to 6
- cotangent: bfloat16 [64, 640, 768], P(('dp', 'fsdp')), may hold values from -6 to 6
- seg_lengths: int32 [64], P(('dp', 'fsdp')), may hold values from 5 to 128, as said below
- alignment: int32 [64, 512], P(('dp', 'fsdp')), may hold values from 0 to 127, as said below
- query_weight: bfloat16 [768, 768], P(('dp', 'fsdp')), may hold values from -0.3125 to 0.3125
- query_bias: bfloat16 [768], P(('dp', 'fsdp')), may hold values from -3 to 3
- key_weight: bfloat16 [768, 768], P(('dp', 'fsdp')), may hold values from -0.21875 to 0.21875
- value_weight: bfloat16 [768, 768], P(('dp', 'fsdp')), may hold values from -0.21875 to 0.21875
- value_bias: bfloat16 [768], P(('dp', 'fsdp')), may hold values from -3 to 3
- out_weight: bfloat16 [768, 768], P(('dp', 'fsdp')), may hold values from -0.625 to 0.625
- out_bias: bfloat16 [768], P(('dp', 'fsdp')), may hold values from -3 to 3
- first_gain: bfloat16 [768], P(('dp', 'fsdp')), may hold values from 0.25 to 1.75
- first_shift: bfloat16 [768], P(('dp', 'fsdp')), may hold values from -2 to 2
- inner_weight: bfloat16 [768, 3072], P(('dp', 'fsdp')), may hold values from -0.21875 to 0.21875
- inner_bias: bfloat16 [3072], P(('dp', 'fsdp')), may hold values from -3 to 3
- outer_weight: bfloat16 [3072, 768], P(('dp', 'fsdp')), may hold values from -0.21875 to 0.21875
- outer_bias: bfloat16 [768], P(('dp', 'fsdp')), may hold values from -3 to 3
- second_gain: bfloat16 [768], P(('dp', 'fsdp')), may hold values from 0.25 to 1.75
- second_shift: bfloat16 [768], P(('dp', 'fsdp')), may hold values from -2 to 2
Outputs:
- encoded: bfloat16 [64, 640, 768], P(('dp', 'fsdp'))
- grad_tokens: bfloat16 [64, 640, 768], P(('dp', 'fsdp'))
- grad_query_weight: float32 [768, 768], P(('dp', 'fsdp'))
- grad_query_bias: float32 [768], P(('dp', 'fsdp'))
- grad_key_weight: float32 [768, 768], P(('dp', 'fsdp'))
- grad_value_weight: float32 [768, 768], P(('dp', 'fsdp'))
- grad_value_bias: float32 [768], P(('dp', 'fsdp'))
- grad_out_weight: float32 [768, 768], P(('dp', 'fsdp'))
- grad_out_bias: float32 [768], P(('dp', 'fsdp'))
- grad_first_gain: float32 [768], P(('dp', 'fsdp'))
- grad_first_shift: float32 [768], P(('dp', 'fsdp'))
- grad_inner_weight: float32 [768, 3072], P(('dp', 'fsdp'))
- grad_inner_bias: float32 [3072], P(('dp', 'fsdp'))
- grad_outer_weight: float32 [3072, 768], P(('dp', 'fsdp'))
- grad_outer_bias: float32 [768], P(('dp', 'fsdp'))
- grad_second_gain: float32 [768], P(('dp', 'fsdp'))
- grad_second_shift: float32 [768], P(('dp', 'fsdp'))
Inputs may be any that keep to these rules, and one draw needn't show every extreme that they name: `seg_lengths`: one document has exactly 128 segment tokens and another exactly 5. `alignment`: each text token names a segment below its document's segment count.
All inputs are finite; a program needn't handle non-finite values.
Results may differ from a plain program's by a relative error of at most 0.017.
Values may be sent and summed in bfloat16 or wider, within the bound.
A program may use at most 192 MiB of HBM per device.

v0:
```python
import jax
import jax.numpy as jnp
from jax import lax
from jax.sharding import PartitionSpec as P

HEADS = 12
HEAD_DIM = 64


norm_eps = 1e-05
masked_score = -1000000000.0
half_root = 0.7071067811865476
density_scale = 0.3989422804014327


def norm_parts(values_in):
    centred = values_in - jnp.mean(values_in, axis=-1, keepdims=True)
    inverse = lax.rsqrt(jnp.mean(centred * centred, axis=-1, keepdims=True) + norm_eps)
    return (centred * inverse, inverse)


def norm_back(grad_hat, normed_hat, inverse):
    return inverse * (
        grad_hat
        - jnp.mean(grad_hat, axis=-1, keepdims=True)
        - normed_hat * jnp.mean(grad_hat * normed_hat, axis=-1, keepdims=True)
    )


def gelu_slope(pre_act):
    return (
        0.5 * (1.0 + lax.erf(pre_act * half_root))
        + pre_act * jnp.exp(-0.5 * pre_act * pre_act) * density_scale
    )


def apply_weight(left_rows, weight_mat):
    return jnp.einsum("bsd,de->bse", left_rows, weight_mat, preferred_element_type=jnp.float32)


def apply_transposed(left_rows, weight_mat):
    return jnp.einsum("bse,de->bsd", left_rows, weight_mat, preferred_element_type=jnp.float32)


def weight_grad(left_rows, right_rows):
    return jnp.einsum("bsd,bse->de", left_rows, right_rows, preferred_element_type=jnp.float32)


def column_sum(rows_low):
    return jnp.sum(rows_low, axis=(0, 1), dtype=jnp.float32)


def split_heads(rows_in):
    return rows_in.reshape(rows_in.shape[0], HEADS, HEAD_DIM)


def score_block(query_rows, key_rows, valid_keys):
    scores = jnp.einsum(
        "qhd,khd->hqk",
        split_heads(query_rows),
        split_heads(key_rows),
        preferred_element_type=jnp.float32,
    ) * HEAD_DIM ** (-0.5)
    return jnp.where(valid_keys[None, None, :], scores, masked_score)


def attend_forward(packed):
    query_rows, key_rows, value_rows, valid_keys = packed
    scores = score_block(query_rows, key_rows, valid_keys)
    row_top = jnp.max(scores, axis=-1, keepdims=True)
    expo = jnp.exp(scores - row_top)
    total = jnp.sum(expo, axis=-1, keepdims=True)
    probs_low = (expo / total).astype(jnp.bfloat16)
    mixed = jnp.einsum(
        "hqk,khd->qhd", probs_low, split_heads(value_rows), preferred_element_type=jnp.float32
    )
    return (mixed.reshape(query_rows.shape[0], HEADS * HEAD_DIM), row_top + jnp.log(total))


def attend_backward(packed):
    query_rows, key_rows, value_rows, valid_keys, log_total, grad_mixed = packed
    slot_count = query_rows.shape[0]
    scores = score_block(query_rows, key_rows, valid_keys)
    probs = jnp.exp(scores - log_total)
    grad_heads = split_heads(grad_mixed)
    grad_probs = jnp.einsum(
        "qhd,khd->hqk", grad_heads, split_heads(value_rows), preferred_element_type=jnp.float32
    )
    grad_value = jnp.einsum(
        "hqk,qhd->khd", probs.astype(jnp.bfloat16), grad_heads, preferred_element_type=jnp.float32
    )
    grad_scores = probs * (grad_probs - jnp.sum(probs * grad_probs, axis=-1, keepdims=True))
    grad_scores_low = grad_scores.astype(jnp.bfloat16)
    grad_query = jnp.einsum(
        "hqk,khd->qhd", grad_scores_low, split_heads(key_rows), preferred_element_type=jnp.float32
    ) * HEAD_DIM ** (-0.5)
    grad_key = jnp.einsum(
        "hqk,qhd->khd", grad_scores_low, split_heads(query_rows), preferred_element_type=jnp.float32
    ) * HEAD_DIM ** (-0.5)
    width = HEADS * HEAD_DIM
    return (
        grad_query.reshape(slot_count, width).astype(jnp.bfloat16),
        grad_key.reshape(slot_count, width).astype(jnp.bfloat16),
        grad_value.reshape(slot_count, width).astype(jnp.bfloat16),
    )


def shards(
    tokens,
    cotangent,
    seg_lengths,
    alignment,
    query_weight,
    query_bias,
    key_weight,
    value_weight,
    value_bias,
    out_weight,
    out_bias,
    first_gain,
    first_shift,
    inner_weight,
    inner_bias,
    outer_weight,
    outer_bias,
    second_gain,
    second_shift,
):
    gathered = (
        lax.all_gather(query_weight, ("dp", "fsdp"), axis=0, tiled=True),
        lax.all_gather(query_bias, ("dp", "fsdp"), axis=0, tiled=True),
        lax.all_gather(key_weight, ("dp", "fsdp"), axis=0, tiled=True),
        lax.all_gather(value_weight, ("dp", "fsdp"), axis=0, tiled=True),
        lax.all_gather(value_bias, ("dp", "fsdp"), axis=0, tiled=True),
        lax.all_gather(out_weight, ("dp", "fsdp"), axis=0, tiled=True),
        lax.all_gather(out_bias, ("dp", "fsdp"), axis=0, tiled=True),
        lax.all_gather(first_gain, ("dp", "fsdp"), axis=0, tiled=True),
        lax.all_gather(first_shift, ("dp", "fsdp"), axis=0, tiled=True),
        lax.all_gather(inner_weight, ("dp", "fsdp"), axis=0, tiled=True),
        lax.all_gather(inner_bias, ("dp", "fsdp"), axis=0, tiled=True),
        lax.all_gather(outer_weight, ("dp", "fsdp"), axis=0, tiled=True),
        lax.all_gather(outer_bias, ("dp", "fsdp"), axis=0, tiled=True),
        lax.all_gather(second_gain, ("dp", "fsdp"), axis=0, tiled=True),
        lax.all_gather(second_shift, ("dp", "fsdp"), axis=0, tiled=True),
    )
    (
        w_query,
        b_query,
        w_key,
        w_value,
        b_value,
        w_out,
        b_out,
        g_first,
        s_first,
        w_inner,
        b_inner,
        w_outer,
        b_outer,
        g_second,
        s_second,
    ) = gathered
    text_count = alignment.shape[1]
    slot_count = tokens.shape[1]
    seg_count = slot_count - text_count
    member = alignment[:, None, :] == jnp.arange(seg_count, dtype=jnp.int32)[None, :, None]
    member_float = member.astype(jnp.float32)
    counts = jnp.maximum(jnp.sum(member_float, axis=-1), 1.0)
    pooled = (
        jnp.einsum(
            "bst,btd->bsd",
            member.astype(jnp.bfloat16),
            tokens[:, :text_count],
            preferred_element_type=jnp.float32,
        )
        / counts[:, :, None]
    )
    text_zeros = jnp.zeros((tokens.shape[0], text_count, tokens.shape[2]), jnp.float32)
    base = tokens.astype(jnp.float32) + jnp.concatenate([text_zeros, pooled], axis=1)
    valid_keys = (
        jnp.arange(slot_count, dtype=jnp.int32)[None, :] < text_count + seg_lengths[:, None]
    )
    base_low = base.astype(jnp.bfloat16)
    query_rows = (apply_weight(base_low, w_query) + b_query).astype(jnp.bfloat16)
    key_rows = apply_weight(base_low, w_key).astype(jnp.bfloat16)
    value_rows = (apply_weight(base_low, w_value) + b_value).astype(jnp.bfloat16)
    attended, log_total = lax.map(attend_forward, (query_rows, key_rows, value_rows, valid_keys))
    attended_low = attended.astype(jnp.bfloat16)
    first_sum = base + apply_weight(attended_low, w_out) + b_out
    first_hat, first_inv = norm_parts(first_sum)
    normed = first_hat * g_first + s_first
    normed_low = normed.astype(jnp.bfloat16)
    pre_act = apply_weight(normed_low, w_inner) + b_inner
    act_low = jax.nn.gelu(pre_act, approximate=False).astype(jnp.bfloat16)
    second_sum = normed + apply_weight(act_low, w_outer) + b_outer
    second_hat, second_inv = norm_parts(second_sum)
    encoded = (second_hat * g_second + s_second).astype(jnp.bfloat16)
    regathered = (
        lax.all_gather(query_weight, ("dp", "fsdp"), axis=0, tiled=True),
        lax.all_gather(query_bias, ("dp", "fsdp"), axis=0, tiled=True),
        lax.all_gather(key_weight, ("dp", "fsdp"), axis=0, tiled=True),
        lax.all_gather(value_weight, ("dp", "fsdp"), axis=0, tiled=True),
        lax.all_gather(value_bias, ("dp", "fsdp"), axis=0, tiled=True),
        lax.all_gather(out_weight, ("dp", "fsdp"), axis=0, tiled=True),
        lax.all_gather(out_bias, ("dp", "fsdp"), axis=0, tiled=True),
        lax.all_gather(first_gain, ("dp", "fsdp"), axis=0, tiled=True),
        lax.all_gather(first_shift, ("dp", "fsdp"), axis=0, tiled=True),
        lax.all_gather(inner_weight, ("dp", "fsdp"), axis=0, tiled=True),
        lax.all_gather(inner_bias, ("dp", "fsdp"), axis=0, tiled=True),
        lax.all_gather(outer_weight, ("dp", "fsdp"), axis=0, tiled=True),
        lax.all_gather(outer_bias, ("dp", "fsdp"), axis=0, tiled=True),
        lax.all_gather(second_gain, ("dp", "fsdp"), axis=0, tiled=True),
        lax.all_gather(second_shift, ("dp", "fsdp"), axis=0, tiled=True),
    )
    (
        back_query,
        unused_qb,
        back_key,
        back_value,
        unused_vb,
        back_out,
        unused_ob,
        back_first,
        unused_fs,
        back_inner,
        unused_ib,
        back_outer,
        unused_xb,
        back_second,
        unused_ss,
    ) = regathered
    grad_y = cotangent.astype(jnp.float32)
    grad_second_gain = jnp.sum(grad_y * second_hat, axis=(0, 1))
    grad_second_shift = jnp.sum(grad_y, axis=(0, 1))
    grad_second = norm_back(grad_y * back_second, second_hat, second_inv)
    grad_mlp_low = grad_second.astype(jnp.bfloat16)
    grad_outer_weight = weight_grad(act_low, grad_mlp_low)
    grad_outer_bias = column_sum(grad_mlp_low)
    grad_pre_low = (apply_transposed(grad_mlp_low, back_outer) * gelu_slope(pre_act)).astype(
        jnp.bfloat16
    )
    grad_inner_weight = weight_grad(normed_low, grad_pre_low)
    grad_inner_bias = column_sum(grad_pre_low)
    grad_normed = grad_second + apply_transposed(grad_pre_low, back_inner)
    grad_first_gain = jnp.sum(grad_normed * first_hat, axis=(0, 1))
    grad_first_shift = jnp.sum(grad_normed, axis=(0, 1))
    grad_first = norm_back(grad_normed * back_first, first_hat, first_inv)
    grad_branch_low = grad_first.astype(jnp.bfloat16)
    grad_out_weight = weight_grad(attended_low, grad_branch_low)
    grad_out_bias = column_sum(grad_branch_low)
    grad_attended_low = apply_transposed(grad_branch_low, back_out).astype(jnp.bfloat16)
    grad_query, grad_key, grad_value = lax.map(
        attend_backward,
        (query_rows, key_rows, value_rows, valid_keys, log_total, grad_attended_low),
    )
    grad_query_weight = weight_grad(base_low, grad_query)
    grad_query_bias = column_sum(grad_query)
    grad_key_weight = weight_grad(base_low, grad_key)
    grad_value_weight = weight_grad(base_low, grad_value)
    grad_value_bias = column_sum(grad_value)
    grad_base = (
        grad_first
        + apply_transposed(grad_query, back_query)
        + apply_transposed(grad_key, back_key)
        + apply_transposed(grad_value, back_value)
    )
    spread_back = jnp.einsum(
        "bst,bsd->btd",
        member_float,
        grad_base[:, text_count:] / counts[:, :, None],
        precision=lax.Precision.HIGHEST,
    )
    grad_tokens = jnp.concatenate(
        [grad_base[:, :text_count] + spread_back, grad_base[:, text_count:]], axis=1
    ).astype(jnp.bfloat16)
    owned = (
        lax.psum_scatter(grad_query_weight, ("dp", "fsdp"), scatter_dimension=0, tiled=True),
        lax.psum_scatter(grad_query_bias, ("dp", "fsdp"), scatter_dimension=0, tiled=True),
        lax.psum_scatter(grad_key_weight, ("dp", "fsdp"), scatter_dimension=0, tiled=True),
        lax.psum_scatter(grad_value_weight, ("dp", "fsdp"), scatter_dimension=0, tiled=True),
        lax.psum_scatter(grad_value_bias, ("dp", "fsdp"), scatter_dimension=0, tiled=True),
        lax.psum_scatter(grad_out_weight, ("dp", "fsdp"), scatter_dimension=0, tiled=True),
        lax.psum_scatter(grad_out_bias, ("dp", "fsdp"), scatter_dimension=0, tiled=True),
        lax.psum_scatter(grad_first_gain, ("dp", "fsdp"), scatter_dimension=0, tiled=True),
        lax.psum_scatter(grad_first_shift, ("dp", "fsdp"), scatter_dimension=0, tiled=True),
        lax.psum_scatter(grad_inner_weight, ("dp", "fsdp"), scatter_dimension=0, tiled=True),
        lax.psum_scatter(grad_inner_bias, ("dp", "fsdp"), scatter_dimension=0, tiled=True),
        lax.psum_scatter(grad_outer_weight, ("dp", "fsdp"), scatter_dimension=0, tiled=True),
        lax.psum_scatter(grad_outer_bias, ("dp", "fsdp"), scatter_dimension=0, tiled=True),
        lax.psum_scatter(grad_second_gain, ("dp", "fsdp"), scatter_dimension=0, tiled=True),
        lax.psum_scatter(grad_second_shift, ("dp", "fsdp"), scatter_dimension=0, tiled=True),
    )
    return (
        encoded,
        grad_tokens,
        owned[0],
        owned[1],
        owned[2],
        owned[3],
        owned[4],
        owned[5],
        owned[6],
        owned[7],
        owned[8],
        owned[9],
        owned[10],
        owned[11],
        owned[12],
        owned[13],
        owned[14],
    )


def solution(mesh):
    in_specs = (
        P(("dp", "fsdp"), None, None),
        P(("dp", "fsdp"), None, None),
        P(("dp", "fsdp")),
        P(("dp", "fsdp"), None),
        P(("dp", "fsdp"), None),
        P(("dp", "fsdp")),
        P(("dp", "fsdp"), None),
        P(("dp", "fsdp"), None),
        P(("dp", "fsdp")),
        P(("dp", "fsdp"), None),
        P(("dp", "fsdp")),
        P(("dp", "fsdp")),
        P(("dp", "fsdp")),
        P(("dp", "fsdp"), None),
        P(("dp", "fsdp")),
        P(("dp", "fsdp"), None),
        P(("dp", "fsdp")),
        P(("dp", "fsdp")),
        P(("dp", "fsdp")),
    )
    out_specs = (
        P(("dp", "fsdp"), None, None),
        P(("dp", "fsdp"), None, None),
        P(("dp", "fsdp"), None),
        P(("dp", "fsdp")),
        P(("dp", "fsdp"), None),
        P(("dp", "fsdp"), None),
        P(("dp", "fsdp")),
        P(("dp", "fsdp"), None),
        P(("dp", "fsdp")),
        P(("dp", "fsdp")),
        P(("dp", "fsdp")),
        P(("dp", "fsdp"), None),
        P(("dp", "fsdp")),
        P(("dp", "fsdp"), None),
        P(("dp", "fsdp")),
        P(("dp", "fsdp")),
        P(("dp", "fsdp")),
    )
    return jax.shard_map(shards, mesh=mesh, in_specs=in_specs, out_specs=out_specs, check_vma=False)
```

profile of v0, /device:TPU:0, one launch (start us, length us, event | category | flops | bytes accessed | tf_op | source)
XLA Modules:
  0.0 1158.2 jit_solution(16809535199130521690)
XLA Ops:
  18.8 42.4 %all-reduce.20 = (bf16[768]{0:T(1024)(128)(2,1)S(1)}, bf16[768]{0:T(1024)(128)(2,1)S(1)}, bf16[768]{0:T(1024)(128)(2,1)S(1)}, bf16[768]{0:T(1024)(128)(2,1)S(1)}...) all-reduce(bf16[768]{0:T(1024)(128)(2,1)S(1)} %dynamic-update-slice, ...), channel_id=1, replica_groups=mesh['dp'=4,'fsdp'=8] {'dp','fsdp'}, use_global_device_ids=true, to_apply=%add.3 | all-reduce | flops 9216 | bytes 36864
  67.1 2.0 fusion.56
  69.1 3.8 add_convert_fusion.2
  73.0 2.3 copy.65
  75.3 48.7 %all-gather.9.cloned.1.call-done = bf16[768,768]{1,0:T(8,128)(2,1)} async-done(((bf16[24,768]{1,0:T(8,128)(2,1)}), bf16[768,768]{1,0:T(8,128)(2,1)}) %all-gather.9.cloned.1.call-update) | async-done | bytes 1179664 | tf_op jit(solution)/shard_map/all_gather | solution.py:130
  124.0 3.6 add_convert_fusion.1
  127.6 2.3 copy.66
  129.9 50.0 %all-gather.11.cloned.1.call-done = bf16[768,768]{1,0:T(8,128)(2,1)} async-done(((bf16[24,768]{1,0:T(8,128)(2,1)}), bf16[768,768]{1,0:T(8,128)(2,1)}) %all-gather.11.cloned.1.call-update) | async-done | bytes 1179664 | tf_op jit(solution)/shard_map/all_gather | solution.py:132
  179.9 3.6 convolution_convert_fusion.1
  183.5 2.3 copy.67
  185.8 66.9 %while.26 = (s32[]{:T(128)}, bf16[2,640,768]{1,2,0:T(8,128)(2,1)}, f32[2,12,640,1]{2,1,3,0:T(8,128)S(1)}, bf16[2,640,768]{1,2,0:T(8,128)(2,1)}, pred[2,640]{1,0:...) while((s32[]{:T(128)}, bf16[2,640,768]{1,2,0:T(8,128)(2,1)}, ...), condition=%wide.region_4.5_spmd, body=%wide.region_1.4_spmd.sunk | while | flops 1317265920 | bytes 71059176 | solution.py:187
  186.3 1.8 constant_dynamic-slice_fusion.14
  188.1 8.9 fusion.139
  197.0 10.6 fusion.140
  209.0 9.4 fusion.141
  219.4 1.7 constant_dynamic-slice_fusion.14
  221.1 8.9 fusion.139
  230.0 10.7 fusion.140
  242.1 9.5 fusion.141
  252.8 4.2 fusion.87
  257.1 1.9 copy-done.3
  259.5 41.5 %all-gather.15.cloned.1.call-done = bf16[768,3072]{1,0:T(8,128)(2,1)} async-done(((bf16[24,3072]{1,0:T(8,128)(2,1)}), bf16[768,3072]{1,0:T(8,128)(2,1)}) %all-gather.15.cloned.1.call-update) | async-done | bytes 4718608 | tf_op jit(solution)/shard_map/all_gather | solution.py:139
  301.1 18.7 %fusion.45 = (u8[640,3072]{1,0:T(8,128)(4,1)S(1)}, u8[640,3072]{1,0:T(8,128)(4,1)S(1)}, f32[2,640,3072]{2,1,0:T(8,128)}) fusion(f32[3072]{0:T(1024)S(1)} %copy-done.24, bf16[768,3072]{1,0:T(8,128)(2,1)} %all-gather.15.cloned.1.call-done, f32[2,640,768]{2,1,0:T(8,128)} %copy-done.3, f32[768]{0:T(1024)S(1)} %copy-done.33, f32[768]{0:T(1024)S(1)} %copy-done.22, ...), kind=kOutput, calls=%fused_computation.102 | convolution fusion | flops 6095831040 | bytes 28340224 | tf_op jit(solution)/shard_map/bsd,de->bse/dot_general | solution.py:38
  319.8 39.1 %fusion.16 = bf16[2,640,3072]{2,1,0:T(8,128)(2,1)} fusion(f32[2,640,3072]{2,1,0:T(8,128)} %get-tuple-element.225, f32[3072]{0:T(1024)S(1)} %copy-done.24, u8[640,3072]{1,0:T(8,128)(4,1)S(1)} %get-tuple-element.149, u8[640,3072]{1,0:T(8,128)(4,1)S(1)} %get-tuple-element.148), kind=kLoop, calls=%fused_computation.38 | loop fusion | flops 279183360 | bytes 27537408 | tf_op jit(solution)/shard_map/convert_element_type | solution.py:194
  358.9 7.4 all-gather.17.cloned.1.call-done
  366.3 11.6 fusion.88
  379.4 2.5 fusion.42
  382.0 3.4 convert_reduce_fusion.2
  385.4 15.0 %convert_reduce_fusion = (f32[3072]{0:T(1024)}, bf16[2,640,3072]{2,1,0:T(8,128)(2,1)}) fusion(f32[2,640,3072]{2,1,0:T(8,128)S(1)} %bitcast.172, f32[3072]{0:T(1024)S(1)} %copy-done.24, bf16[2,640,768]{2,1,0:T(8,128)(2,1)S(1)} %get-tuple-element.211, bf16[3072,768]{1,0:T(8,128)(2,1)} %all-gather.17.cloned.1.call-done), kind=kOutput, calls=%fused_computation.50 | convolution fusion | flops 6090912768 | bytes 30302208 | tf_op jit(solution)/shard_map/bse,de->bsd/dot_general | solution.py:42
  400.4 12.4 %multiply_reduce_fusion.1 = (f32[768]{0:T(1024)}, f32[2,640]{1,0:T(2,128)S(1)}, f32[2,640]{1,0:T(2,128)S(1)}, f32[768]{0:T(1024)}, f32[2,640,768]{2,1,0:T(8,128)S(1)}) fusion(f32[2,640,768]{2,1,0:T(8,128)S(1)} %copy-done.4, f32[2,640]{1,0:T(2,128)S(1)} %add_rsqrt_fusion.1, f32[2,640]{1,0:T(2,128)S(1)} %broadcast_multiply_fusion.5, f32[768]{0:T(1024)S(1)} %copy-done.22, ...), kind=kOutput, calls=%fused_computation.84 | convolution fusion | flops 6057488384 | bytes 26398720 | tf_op jit(solution)/shard_map/bse,de->bsd/dot_general | solution.py:42
  412.9 1.9 convert_reduce_fusion.3
  414.8 4.6 convolution_bitcast_fusion.2
  419.5 4.3 convolution_convert_fusion
  423.8 131.8 %while.27 = (s32[]{:T(128)}, bf16[2,640,768]{1,2,0:T(8,128)(2,1)}, bf16[2,640,768]{1,2,0:T(8,128)(2,1)}, bf16[2,640,768]{1,2,0:T(8,128)(2,1)}, bf16[2,640,768]{1...) while((s32[]{:T(128)}, bf16[2,640,768]{1,2,0:T(8,128)(2,1)}, ...), condition=%wide.region_15.16_spmd, body=%wide.region_13.15_spmd.sunk | while | flops 3221905920 | bytes 192895376 | solution.py:252
  426.6 8.4 fusion.152
  439.3 13.9 %multiply_reduce_fusion.7 = (f32[12,640]{1,0:T(8,128)S(1)}, f32[12,640,640]{1,2,0:T(8,128)}) fusion(f32[12,640,640]{1,2,0:T(8,128)} %fusion.152, f32[12,640]{1,0:T(8,128)S(1)} %dynamic-slice_bitcast_fusion.2, pred[640]{0:T(1024)(128)(4,1)S(1)} %dynamic-slice_reduce_fusion.5, bf16[640,12,64]{0,2,1:T(8,128)(2,1)S(1)} %bitcast.162, ...), kind=kOutput, calls=%fused_computation.15.clone.1 | convolution fusion | flops 653713920 | bytes 41349760 | tf_op jit(solution)/shard_map/while/body/eval_jaxpr/qhd,khd->hqk/dot_general | solution.py:86
  453.3 14.1 %multiply_convert_fusion.6 = bf16[12,640,640]{1,2,0:T(8,128)(2,1)S(1)} fusion(f32[12,640,640]{1,2,0:T(8,128)} %get-tuple-element.349, f32[12,640,640]{1,2,0:T(8,128)} %fusion.152, f32[12,640]{1,0:T(8,128)S(1)} %get-tuple-element.350, f32[12,640]{1,0:T(8,128)S(1)} %dynamic-slice_bitcast_fusion.2, pred[640]{0:T(1024)(128)(4,1)S(1)} %dynamic-slice_reduce_fusion.5), kind=kLoop, calls=%fused_computation.14.clone.1 | loop fusion | flops 29491200 | bytes 49214080 | tf_op jit(solution)/shard_map/while/body/eval_jaxpr/convert_element_type | solution.py:93
  467.4 4.2 multiply_convert_fusion.8
  471.6 12.7 %fusion.153 = bf16[12,64,640]{2,1,0:T(8,128)(2,1)} fusion(bf16[640,12,64]{0,2,1:T(8,128)(2,1)} %bitcast.163, f32[12,640,640]{1,2,0:T(8,128)} %fusion.152, f32[12,640]{1,0:T(8,128)S(1)} %dynamic-slice_bitcast_fusion.2, pred[640]{0:T(1024)(128)(4,1)S(1)} %dynamic-slice_reduce_fusion.5), kind=kOutput, calls=%fused_computation.22.clone.1 | convolution fusion | flops 649297920 | bytes 21658240 | tf_op jit(solution)/shard_map/while/body/eval_jaxpr/hqk,qhd->khd/dot_general | solution.py:89
  484.2 3.0 constant_dynamic-update-slice_fusion.9
  487.3 1.7 multiply_convert_fusion.7
  492.6 8.3 fusion.152
  503.5 1.7 constant_dynamic-slice_fusion.18
  505.2 13.7 %multiply_reduce_fusion.7 = (f32[12,640]{1,0:T(8,128)S(1)}, f32[12,640,640]{1,2,0:T(8,128)}) fusion(f32[12,640,640]{1,2,0:T(8,128)} %fusion.152, f32[12,640]{1,0:T(8,128)S(1)} %dynamic-slice_bitcast_fusion.2, pred[640]{0:T(1024)(128)(4,1)S(1)} %dynamic-slice_reduce_fusion.5, bf16[640,12,64]{0,2,1:T(8,128)(2,1)S(1)} %bitcast.162, ...), kind=kOutput, calls=%fused_computation.15.clone.1 | convolution fusion | flops 653713920 | bytes 41349760 | tf_op jit(solution)/shard_map/while/body/eval_jaxpr/qhd,khd->hqk/dot_general | solution.py:86
  518.9 14.0 %multiply_convert_fusion.6 = bf16[12,640,640]{1,2,0:T(8,128)(2,1)S(1)} fusion(f32[12,640,640]{1,2,0:T(8,128)} %get-tuple-element.349, f32[12,640,640]{1,2,0:T(8,128)} %fusion.152, f32[12,640]{1,0:T(8,128)S(1)} %get-tuple-element.350, f32[12,640]{1,0:T(8,128)S(1)} %dynamic-slice_bitcast_fusion.2, pred[640]{0:T(1024)(128)(4,1)S(1)} %dynamic-slice_reduce_fusion.5), kind=kLoop, calls=%fused_computation.14.clone.1 | loop fusion | flops 29491200 | bytes 49214080 | tf_op jit(solution)/shard_map/while/body/eval_jaxpr/convert_element_type | solution.py:93
  532.9 4.2 multiply_convert_fusion.8
  537.1 12.5 %fusion.153 = bf16[12,64,640]{2,1,0:T(8,128)(2,1)} fusion(bf16[640,12,64]{0,2,1:T(8,128)(2,1)} %bitcast.163, f32[12,640,640]{1,2,0:T(8,128)} %fusion.152, f32[12,640]{1,0:T(8,128)S(1)} %dynamic-slice_bitcast_fusion.2, pred[640]{0:T(1024)(128)(4,1)S(1)} %dynamic-slice_reduce_fusion.5), kind=kOutput, calls=%fused_computation.22.clone.1 | convolution fusion | flops 649297920 | bytes 21658240 | tf_op jit(solution)/shard_map/while/body/eval_jaxpr/hqk,qhd->khd/dot_general | solution.py:89
  549.6 2.9 constant_dynamic-update-slice_fusion.9
  552.5 1.7 multiply_convert_fusion.7
  555.7 5.6 convolution_bitcast_fusion.3
  561.4 4.8 convolution_bitcast_fusion.5
  566.3 5.4 convolution_bitcast_fusion.4
  571.8 12.9 %convolution_bitcast_fusion.1 = f32[768,3072]{1,0:T(8,128)} fusion(bf16[2,640,3072]{2,1,0:T(8,128)(2,1)} %get-tuple-element.230, f32[2,640,768]{2,1,0:T(8,128)} %copy-done.3, f32[768]{0:T(1024)S(1)} %copy-done.34, f32[768]{0:T(1024)S(1)} %copy-done.23, f32[2,640]{1,0:T(2,128)S(1)} %copy-done.17, f32[2,640]{1,0:T(2,128)S(1)} %copy-done.15), kind=kOutput, calls=%fused_computation.68 | convolution fusion | flops 6044712960 | bytes 21250048 | tf_op jit(solution)/shard_map/bsd,bse->de/dot_general | solution.py:46
  586.3 10.9 convolution_bitcast_fusion
  599.1 1.9 convert_reduce_fusion.5
  601.1 41.0 %all-reduce.19 = (f32[768]{0:T(1024)S(1)}, f32[768]{0:T(1024)S(1)}, f32[768]{0:T(1024)S(1)}, f32[768]{0:T(1024)S(1)}, f32[768]{0:T(1024)S(1)}, /*index=5*/f32[30...) all-reduce(f32[768]{0:T(1024)S(1)} %convert_reduce_fusion.5, ...), channel_id=3, replica_groups=mesh['dp'=4,'fsdp'=8] {'dp','fsdp'}, use_global_device_ids=true, to_apply=%region_18.19.clone | all-reduce | flops 9216 | bytes 73728
  646.8 3.5 fusion.64
  650.3 1.7 fusion.61
  653.9 3.5 add_add_fusion
  658.0 1.8 fusion.47
  661.2 102.4 %reduce-scatter.7.cloned.1.call-done = f32[24,768]{1,0:T(8,128)} async-done(((f32[768,768]{1,0:T(8,128)}), f32[24,768]{1,0:T(8,128)}) %reduce-scatter.7.cloned.1.call-update) | async-done | bytes 73744 | tf_op jit(solution)/shard_map/reduce_scatter | solution.py:277
  763.6 104.6 %reduce-scatter.9.cloned.1.call-done = f32[24,768]{1,0:T(8,128)} async-done(((f32[768,768]{1,0:T(8,128)}), f32[24,768]{1,0:T(8,128)}) %reduce-scatter.9.cloned.1.call-update) | async-done | bytes 73744 | tf_op jit(solution)/shard_map/reduce_scatter | solution.py:279
  868.2 141.1 %reduce-scatter.15.cloned.1.call-done = f32[24,3072]{1,0:T(8,128)} async-done(((f32[768,3072]{1,0:T(8,128)}), f32[24,3072]{1,0:T(8,128)}) %reduce-scatter.15.cloned.1.call-update) | async-done | bytes 294928 | tf_op jit(solution)/shard_map/reduce_scatter | solution.py:286
  1009.4 141.8 %reduce-scatter.17.cloned.1.call-done = f32[96,768]{1,0:T(8,128)} async-done(((f32[3072,768]{1,0:T(8,128)}), f32[96,768]{1,0:T(8,128)}) %reduce-scatter.17.cloned.1.call-update) | async-done | bytes 294928 | tf_op jit(solution)/shard_map/reduce_scatter | solution.py:288
  (220 shorter events, 50.6 us)
Async XLA Ops:
  7.2 62.0 %all-gather.7.cloned.1.call-start = ((), (), s32[]{:S(2)}) async-start(), calls=%async_computation.6 | async-start | bytes 1216512 | tf_op jit(solution)/shard_map/all_gather | solution.py:133
  7.9 116.1 %all-gather.9.cloned.1.call-start = ((), (), s32[]{:S(2)}) async-start(), calls=%async_computation.7 | async-start | bytes 1216512 | tf_op jit(solution)/shard_map/all_gather | solution.py:130
  8.7 171.3 %all-gather.11.cloned.1.call-start = ((), (), s32[]{:S(2)}) async-start(), calls=%async_computation.8 | async-start | bytes 1216512 | tf_op jit(solution)/shard_map/all_gather | solution.py:132
  9.4 243.4 %all-gather.13.cloned.1.call-start = ((), (), s32[]{:S(2)}) async-start(), calls=%async_computation.9 | async-start | bytes 1216512 | tf_op jit(solution)/shard_map/all_gather | solution.py:135
  10.0 291.1 %all-gather.15.cloned.1.call-start = ((), (), s32[]{:S(2)}) async-start(), calls=%async_computation.10 | async-start | bytes 4866048 | tf_op jit(solution)/shard_map/all_gather | solution.py:139
  10.6 355.7 %all-gather.17.cloned.1.call-start = ((), (), s32[]{:S(2)}) async-start(), calls=%async_computation.11 | async-start | bytes 4866048 | tf_op jit(solution)/shard_map/all_gather | solution.py:141
  11.1 650.0 %reduce-scatter.13.cloned.1.call-start = ((), (), s32[]{:S(2)}) async-start(), calls=%async_computation.15 | async-start | bytes 2433024 | tf_op jit(solution)/shard_map/reduce_scatter | solution.py:282
  62.2 7.0 copy-start.39
  69.1 110.8 %copy-start.46 = (f32[2,128,768]{2,1,0:T(8,128)}, f32[2,128,768]{2,1,0:T(8,128)S(1)}, u32[]{:S(2)}) copy-start(f32[2,128,768]{2,1,0:T(8,128)S(1)} %fusion.56) | copy-start | bytes 2359300
  185.8 67.0 %copy-start.36 = (f32[768]{0:T(1024)S(1)}, f32[768]{0:T(1024)}, u32[]{:S(2)}) copy-start(f32[768]{0:T(1024)} %convert_element_type.157) | copy-start | bytes 9220
  185.8 67.0 %copy-start.41 = (bf16[2,640,768]{2,1,0:T(8,128)(2,1)S(1)}, bf16[2,640,768]{2,1,0:T(8,128)(2,1)}, u32[]{:S(2)}) copy-start(bf16[2,640,768]{2,1,0:T(8,128)(2,1)} %param.23) | copy-start | bytes 5898244
  257.0 1.9 copy-start.3
  257.0 44.1 %copy-start.22 = (f32[768]{0:T(1024)S(1)}, f32[768]{0:T(1024)}, u32[]{:S(2)}) copy-start(f32[768]{0:T(1024)} %convert_element_type.158) | copy-start | bytes 9220
  257.0 44.1 %copy-start.24 = (f32[3072]{0:T(1024)S(1)}, f32[3072]{0:T(1024)}, u32[]{:S(2)}) copy-start(f32[3072]{0:T(1024)} %convert_element_type.161) | copy-start | bytes 36868
  257.0 44.0 %copy-start.33 = (f32[768]{0:T(1024)S(1)}, f32[768]{0:T(1024)}, u32[]{:S(2)}) copy-start(f32[768]{0:T(1024)} %convert_element_type.159) | copy-start | bytes 9220
  257.0 155.8 %copy-start.14 = (f32[2,640]{1,0:T(2,128)}, f32[2,640]{1,0:T(2,128)S(1)}, u32[]{:S(2)}) copy-start(f32[2,640]{1,0:T(2,128)S(1)} %broadcast_multiply_fusion.5) | copy-start | bytes 15364
  259.5 153.3 %copy-start.16 = (f32[2,640]{1,0:T(2,128)}, f32[2,640]{1,0:T(2,128)S(1)}, u32[]{:S(2)}) copy-start(f32[2,640]{1,0:T(2,128)S(1)} %add_rsqrt_fusion.1) | copy-start | bytes 15364
  319.8 46.5 %copy-start.35 = (f32[768]{0:T(1024)S(1)}, f32[768]{0:T(1024)}, u32[]{:S(2)}) copy-start(f32[768]{0:T(1024)} %convert_element_type.163) | copy-start | bytes 9220
  366.3 19.1 %slice-start = ((s8[15728640]{0:T(1024)(128)(4,1)}), s8[4194304]{0:T(1024)(128)(4,1)S(1)}, s32[]{:S(2)}) async-start(s8[15728640]{0:T(1024)(128)(4,1)} %bitcast.171), calls=%async_computation.18 | async-start | bytes 8388608
  366.3 19.1 %slice-start.1 = ((s8[15728640]{0:T(1024)(128)(4,1)}), s8[4194304]{0:T(1024)(128)(4,1)S(1)}, s32[]{:S(2)}) async-start(s8[15728640]{0:T(1024)(128)(4,1)} %bitcast.171), calls=%async_computation.19 | async-start | bytes 8388608
  366.3 19.1 %slice-start.2 = ((s8[15728640]{0:T(1024)(128)(4,1)}), s8[4194304]{0:T(1024)(128)(4,1)S(1)}, s32[]{:S(2)}) async-start(s8[15728640]{0:T(1024)(128)(4,1)} %bitcast.171), calls=%async_computation.20 | async-start | bytes 8388608
  377.9 7.5 slice-start.3
  378.5 3.5 copy-start.26
  385.4 15.1 %copy-start.11 = (bf16[2,640,768]{2,1,0:T(8,128)(2,1)}, bf16[2,640,768]{2,1,0:T(8,128)(2,1)S(1)}, u32[]{:S(2)}) copy-start(bf16[2,640,768]{2,1,0:T(8,128)(2,1)S(1)} %get-tuple-element.211) | copy-start | bytes 5898244
  385.4 15.0 %copy-start.4 = (f32[2,640,768]{2,1,0:T(8,128)S(1)}, f32[2,640,768]{2,1,0:T(8,128)}, u32[]{:S(2)}) copy-start(f32[2,640,768]{2,1,0:T(8,128)} %copy-done.3) | copy-start | bytes 11796484
  412.8 2.0 copy-start.6
  412.8 2.0 copy-start.18
  412.8 2.0 copy-start.20
  419.5 241.7 %reduce-scatter.11.cloned.1.call-start = ((), (), s32[]{:S(2)}) async-start(), calls=%async_computation.14 | async-start | bytes 2433024 | tf_op jit(solution)/shard_map/reduce_scatter | solution.py:280
  426.6 8.4 copy-start
  426.6 8.5 copy-start.8
  437.6 15.6 %copy-start.2 = (bf16[1,640,768]{1,2,0:T(8,128)(2,1)}, bf16[1,640,768]{1,2,0:T(8,128)(2,1)S(1)}, u32[]{:S(2)}) copy-start(bf16[1,640,768]{1,2,0:T(8,128)(2,1)S(1)} %copy.103) | copy-start | bytes 2949124 | tf_op jit(solution)/shard_map/while
  453.3 14.1 %copy-start.1 = (bf16[1,640,768]{1,2,0:T(8,128)(2,1)S(1)}, bf16[1,640,768]{1,2,0:T(8,128)(2,1)}, u32[]{:S(2)}) copy-start(bf16[1,640,768]{1,2,0:T(8,128)(2,1)} %copy-done) | copy-start | bytes 2949124 | tf_op jit(solution)/shard_map/while
  492.6 8.3 copy-start
  492.6 8.3 copy-start.8
  503.5 15.4 %copy-start.2 = (bf16[1,640,768]{1,2,0:T(8,128)(2,1)}, bf16[1,640,768]{1,2,0:T(8,128)(2,1)S(1)}, u32[]{:S(2)}) copy-start(bf16[1,640,768]{1,2,0:T(8,128)(2,1)S(1)} %copy.103) | copy-start | bytes 2949124 | tf_op jit(solution)/shard_map/while
  518.9 14.0 %copy-start.1 = (bf16[1,640,768]{1,2,0:T(8,128)(2,1)S(1)}, bf16[1,640,768]{1,2,0:T(8,128)(2,1)}, u32[]{:S(2)}) copy-start(bf16[1,640,768]{1,2,0:T(8,128)(2,1)} %copy-done) | copy-start | bytes 2949124 | tf_op jit(solution)/shard_map/while
  555.7 5.7 copy-start.42
  555.7 5.7 copy-start.47
  561.4 202.2 %reduce-scatter.7.cloned.1.call-start = ((), (), s32[]{:S(2)}) async-start(), calls=%async_computation.12 | async-start | bytes 2433024 | tf_op jit(solution)/shard_map/reduce_scatter | solution.py:277
  566.2 302.0 %reduce-scatter.9.cloned.1.call-start = ((), (), s32[]{:S(2)}) async-start(), calls=%async_computation.13 | async-start | bytes 2433024 | tf_op jit(solution)/shard_map/reduce_scatter | solution.py:279
  566.3 5.5 copy-start.15
  566.3 5.5 copy-start.17
  566.3 5.5 copy-start.23
  566.3 5.5 copy-start.34
  571.7 437.6 %reduce-scatter.15.cloned.1.call-start = ((), (), s32[]{:S(2)}) async-start(), calls=%async_computation.16 | async-start | bytes 9732096 | tf_op jit(solution)/shard_map/reduce_scatter | solution.py:286
  584.8 566.4 %reduce-scatter.17.cloned.1.call-start = ((), (), s32[]{:S(2)}) async-start(), calls=%async_computation.17 | async-start | bytes 9732096 | tf_op jit(solution)/shard_map/reduce_scatter | solution.py:288
  597.2 3.8 copy-start.27
  597.2 3.8 copy-start.28
  597.2 3.8 copy-start.29
  597.3 3.8 copy-start.30
  597.3 3.8 copy-start.31
  597.3 3.8 copy-start.37
  597.3 3.8 copy-start.38
  597.3 49.5 %copy-start.44 = (bf16[768,768]{1,0:T(8,128)(2,1)S(1)}, bf16[768,768]{1,0:T(8,128)(2,1)}, u32[]{:S(2)}) copy-start(bf16[768,768]{1,0:T(8,128)(2,1)} %all-gather.9.cloned.1.call-done) | copy-start | bytes 3538948
  646.8 3.5 copy-start.43
  646.8 3.5 copy-start.45
  650.3 2.1 copy-start.5
  650.3 3.3 copy-start.7
  650.3 3.6 copy-start.13
  650.3 3.6 copy-start.19
  650.3 3.6 copy-start.21
  653.9 4.1 copy-start.32
  653.9 4.1 copy-start.40
  (4 other events, 6.2 us)
Sparse Core Ops, SparseCore 0:
  10.9 56.9 all-gather.6
  70.9 53.1 all-gather.8
  126.9 52.9 all-gather.10
  182.7 52.9 all-gather.12
  238.4 62.5 all-gather.14
  303.8 62.4 all-gather.16
  419.6 97.8 reduce-scatter.12
  561.5 98.2 reduce-scatter.10
  665.6 97.9 reduce-scatter.6
  770.2 98.0 reduce-scatter.8
  874.7 134.6 reduce-scatter.14
  1016.7 134.4 reduce-scatter.16
where the time goes:
time: 1170 us; the launch traced here: 1160 us
  waiting for transfers between devices  641 us (55%)
  matrix products  252 us (22%)
  other arithmetic  107 us (9%)
  blocking collectives  83.5 us (7%)
  local copies, waits for them, and re-layouts  57.4 us (5%)
  between operations  15.2 us (1%)
    reduce_scatter x1, waiting for transfers between devices, shards(): lax.psum_scatter(grad_outer_weight, ('dp', 'fsdp'), scatter_dimension=0,...  142 us
    reduce_scatter x1, waiting for transfers between devices, shards(): lax.psum_scatter(grad_inner_weight, ('dp', 'fsdp'), scatter_dimension=0,...  141 us
    reduce_scatter x1, waiting for transfers between devices, shards(): lax.psum_scatter(grad_key_weight, ('dp', 'fsdp'), scatter_dimension=0, ti...  105 us
    reduce_scatter x1, waiting for transfers between devices, shards(): lax.psum_scatter(grad_query_weight, ('dp', 'fsdp'), scatter_dimension=0,...  102 us
    unnamed x2, blocking collectives  83.5 us
    all_gather x1, waiting for transfers between devices, shards(): lax.all_gather(key_weight, ('dp', 'fsdp'), axis=0, tiled=True)  50 us
    all_gather x1, waiting for transfers between devices, shards(): lax.all_gather(query_weight, ('dp', 'fsdp'), axis=0, tiled=True)  48.7 us
    dot_general x6, matrix products, apply_weight(): jnp.einsum('bsd,de->bse', left_rows, weight_mat, preferred_element_type=j...  45.4 us
  transfers between devices with their start and end apart: 12, of which 8 were waited for; matrix products, arithmetic and copies ran while one was open for 31% of the time, Pallas kernels for 0%

commit v1 on v0

--- a/solution.py
+++ b/solution.py
@@ -1,7 +1,423 @@
+import functools
 import jax
 import jax.numpy as jnp
 from jax import lax
+from jax.experimental import pallas as pl
+from jax.experimental.pallas import tpu as pltpu
 from jax.sharding import PartitionSpec as P
+
+MESH = pl.DeviceIdType.MESH
+ANY = pl.BlockSpec(memory_space=pl.ANY)
+VMEM = pl.BlockSpec(memory_space=pltpu.VMEM)
+PLANES = 4
+CHIPS = 16
+
+
+class Place:
+    def __init__(self):
+        self.z = lax.axis_index("dp")
+        self.f = lax.axis_index("fsdp")
+        self.core = self.f % 2
+        self.x = (self.f // 2) % 2
+        self.y = self.f // 4
+        self.sib = self.f + 1 - 2 * self.core
+        self.xn = self.f + 2 - 4 * self.x
+        self.yn = self.f + 4 - 8 * self.y
+        self.spot = self.f // 2
+        self.spot_x = self.xn // 2
+        self.spot_y = self.yn // 2
+        self.spot_d = 3 - self.spot
+
+    def plane(self, back):
+        return (self.z + PLANES - back) % PLANES
+
+    def ahead(self, step):
+        return (self.z + step) % PLANES
+
+    def barrier(self):
+        bar = pltpu.get_barrier_semaphore()
+        for other in self.partners():
+            pl.semaphore_signal(bar, inc=1, device_id=other, device_id_type=MESH)
+        pl.semaphore_wait(bar, 3 + PLANES - 1)
+
+    def partners(self):
+        return [(self.z, self.sib), (self.z, self.xn), (self.z, self.yn)] + [
+            (self.ahead(k), self.f) for k in range(1, PLANES)
+        ]
+
+
+def remote(src, dst, send, recv, dev):
+    return pltpu.make_async_remote_copy(
+        src_ref=src, dst_ref=dst, send_sem=send, recv_sem=recv, device_id=dev, device_id_type=MESH
+    )
+
+
+class Gather:
+    SEMS = 3 + 4 + 4 + 4 + 4 + 4
+
+    def __init__(self, place, full, own, send, recv, local, width=None):
+        self.p, self.full, self.own = place, full, own
+        self.send, self.recv, self.local = send, recv, local
+        self.half = None if width is None else width // 2
+        self.rows = own.shape[0]
+        self.started = []
+
+    def view(self, chip, r0=0, r1=None, core=None):
+        core = self.p.core if core is None else core
+        r1 = self.rows if r1 is None else r1
+        if self.half is None:
+            return self.full.at[chip, core, pl.ds(r0, r1 - r0), :]
+        cols = pl.ds(pl.multiple_of(core * self.half, 128), self.half)
+        return self.full.at[chip, pl.ds(r0, r1 - r0), cols]
+
+    def block(self, plane, core):
+        if self.half is None:
+            return self.full.at[pl.ds(4 * plane, 4), core]
+        cols = pl.ds(pl.multiple_of(core * self.half, 128), self.half)
+        return self.full.at[pl.ds(4 * plane, 4), :, cols]
+
+    def cut(self, back):
+        if self.rows == 96:
+            return 48
+        return 32 if back % 2 == 0 else 16
+
+    def copy(self, src, dst, index, dev):
+        c = remote(src, dst, self.send.at[index], self.recv.at[index], dev)
+        return c
+
+    def start(self, src, dst, index, dev):
+        c = self.copy(src, dst, index, dev)
+        c.start()
+        self.started.append(c)
+
+    def chip(self, back, spot):
+        return 4 * self.p.plane(back) + spot
+
+    def along_z(self):
+        p = self.p
+        mine = self.view(self.chip(0, p.spot))
+        c = pltpu.make_async_copy(self.own, mine, self.local)
+        c.start()
+        self.own_copy = c
+        for k in range(1, PLANES):
+            self.start(self.own, mine, k - 1, (p.ahead(k), p.f))
+
+    def to_neighbours(self, back):
+        p = self.p
+        piece = self.view(self.chip(back, p.spot))
+        if back:
+            self.copy(piece, piece, back - 1, (p.z, p.f)).wait_recv()
+        src = piece if back else self.own
+        self.start(src, piece, 3 + back, (p.z, p.xn))
+        self.start(src, piece, 7 + back, (p.z, p.yn))
+
+    def to_diagonal(self, back):
+        p, cut = self.p, self.cut(back)
+        cx, cy = self.chip(back, p.spot_x), self.chip(back, p.spot_y)
+        full_x, full_y = self.view(cx), self.view(cy)
+        self.copy(full_x, full_x, 3 + back, (p.z, p.xn)).wait_recv()
+        part = self.view(cx, 0, cut)
+        self.start(part, part, 11 + back, (p.z, p.yn))
+        self.copy(full_y, full_y, 7 + back, (p.z, p.yn)).wait_recv()
+        part = self.view(cy, cut, self.rows)
+        self.start(part, part, 15 + back, (p.z, p.xn))
+
+    def to_core(self, back):
+        p, cut = self.p, self.cut(back)
+        cd = self.chip(back, p.spot_d)
+        a, b = self.view(cd, 0, cut), self.view(cd, cut, self.rows)
+        self.copy(a, a, 11 + back, (p.z, p.yn)).wait_recv()
+        self.copy(b, b, 15 + back, (p.z, p.xn)).wait_recv()
+        if back == 0:
+            self.own_copy.wait()
+        blk = self.block(p.plane(back), p.core)
+        self.start(blk, blk, 19 + back, (p.z, p.sib))
+
+    def finish(self):
+        p = self.p
+        for back in range(PLANES):
+            blk = self.block(p.plane(back), 1 - p.core)
+            self.copy(blk, blk, 19 + back, (p.z, p.sib)).wait_recv()
+
+    def drain(self):
+        for c in self.started:
+            c.wait_send()
+
+
+def build_own(place, shard, land, own):
+    half = own.shape[1]
+    first = place.core == 0
+    for c0 in range(0, half, 128):
+        mine = shard[:, pl.ds(pl.multiple_of(place.core * half + c0, 128), 128)]
+        other = land[:, c0 : c0 + 128]
+        top = jnp.where(first, mine, other)
+        bottom = jnp.where(first, other, mine)
+        own[:, c0 : c0 + 128] = jnp.concatenate([top, bottom], axis=0).astype(own.dtype)
+
+
+class Pair:
+    def __init__(self, place, shard, land, own, send, recv):
+        half = own.shape[1]
+        src = shard.at[:, pl.ds(pl.multiple_of((1 - place.core) * half, 128), half)]
+        self.c = remote(src, land, send, recv, (place.z, place.sib))
+        self.args = (place, shard, land, own)
+
+    def start(self):
+        self.c.start()
+
+    def done(self):
+        self.c.wait()
+        build_own(*self.args)
+
+
+def gather_steps(groups, pairs):
+    g0, g1, g2 = groups
+    steps = []
+
+    def begin():
+        for pr in pairs:
+            pr.start()
+        pairs[0].done()
+        g0.along_z()
+        g0.to_neighbours(0)
+        pairs[1].done()
+        g1.along_z()
+
+    steps.append(begin)
+    for k in (1, 2, 3):
+        steps.append(functools.partial(g0.to_neighbours, k))
+    steps.append(functools.partial(g1.to_neighbours, 0))
+    steps.append(g2.along_z)
+    for k in range(4):
+        steps.append(functools.partial(g0.to_diagonal, k))
+    for k in (1, 2, 3):
+        steps.append(functools.partial(g1.to_neighbours, k))
+    for k in range(4):
+        steps.append(functools.partial(g0.to_core, k))
+    steps.append(functools.partial(g2.to_neighbours, 0))
+    steps.append(g0.finish)
+    for k in range(4):
+        steps.append(functools.partial(g1.to_diagonal, k))
+    for k in (1, 2, 3):
+        steps.append(functools.partial(g2.to_neighbours, k))
+    for k in range(4):
+        steps.append(functools.partial(g1.to_core, k))
+    for k in range(4):
+        steps.append(functools.partial(g2.to_diagonal, k))
+    for k in range(4):
+        steps.append(functools.partial(g2.to_core, k))
+    steps.append(g1.finish)
+    steps.append(g2.finish)
+    for g in groups:
+        steps.append(g.drain)
+    return steps
+
+
+def gather_kernel(s0, s1, s2, w0, w1, w2, land0, land1, own0, own1, pair_sem, local, send, recv):
+    place = Place()
+    place.barrier()
+    pairs = [
+        Pair(place, s0, land0, own0, pair_sem.at[0], pair_sem.at[1]),
+        Pair(place, s1, land1, own1, pair_sem.at[2], pair_sem.at[3]),
+    ]
+    groups = [
+        Gather(place, w0, own0, send.at[0], recv.at[0], local.at[0], w0.shape[2]),
+        Gather(place, w1, own1, send.at[1], recv.at[1], local.at[1], w1.shape[2]),
+        Gather(place, w2, s2, send.at[2], recv.at[2], local.at[2]),
+    ]
+    for step in gather_steps(groups, pairs):
+        step()
+
+
+def gather_all(s0, s1, s2):
+    n0, n1 = s0.shape[1], s1.shape[1]
+    bf = jnp.bfloat16
+    return pl.pallas_call(
+        gather_kernel,
+        out_shape=(
+            jax.ShapeDtypeStruct((CHIPS, 48, n0), bf),
+            jax.ShapeDtypeStruct((CHIPS, 48, n1), bf),
+            jax.ShapeDtypeStruct((CHIPS, 2, 96, s2.shape[1]), bf),
+        ),
+        in_specs=[VMEM] * 3,
+        out_specs=[ANY] * 3,
+        scratch_shapes=[
+            pltpu.VMEM((24, n0 // 2), jnp.float32),
+            pltpu.VMEM((24, n1 // 2), jnp.float32),
+            pltpu.VMEM((48, n0 // 2), bf),
+            pltpu.VMEM((48, n1 // 2), bf),
+            pltpu.SemaphoreType.DMA((4,)),
+            pltpu.SemaphoreType.DMA((3,)),
+            pltpu.SemaphoreType.DMA((3, Gather.SEMS)),
+            pltpu.SemaphoreType.DMA((3, Gather.SEMS)),
+        ],
+        compiler_params=pltpu.CompilerParams(
+            collective_id=0, has_side_effects=True, vmem_limit_bytes=56 * 2**20
+        ),
+    )(s0, s1, s2)
+
+
+class Scatter:
+    SEMS = 4 + 4 + 4 + 4 + 4 + 3 + 1
+
+    def __init__(self, place, full, bufs, out, send, recv, local, width=None):
+        self.p, self.full, self.out = place, full, out
+        self.sums, self.from_core, self.la, self.lb, self.lx, self.ly, self.lz = bufs[:7]
+        if width is not None:
+            self.total, self.last = bufs[7:]
+        self.send, self.recv, self.local = send, recv, local
+        self.half = None if width is None else width // 2
+        self.rows = self.sums.shape[1]
+        self.started = []
+
+    @staticmethod
+    def scratch(rows, cols, two_rows):
+        bf = jnp.bfloat16
+        shapes = [
+            pltpu.VMEM((CHIPS, rows, cols), bf),
+            pltpu.VMEM((CHIPS, rows, cols), bf),
+            pltpu.VMEM((4, rows - 16, cols), bf),
+            pltpu.VMEM((4, rows - 16, cols), bf),
+            pltpu.VMEM((4, rows, cols), bf),
+            pltpu.VMEM((4, rows, cols), bf),
+            pltpu.VMEM((3, rows, cols), bf),
+        ]
+        if two_rows:
+            shapes += [pltpu.VMEM((rows, cols), jnp.float32), pltpu.VMEM((rows // 2, cols), jnp.float32)]
+        return shapes
+
+    cut = Gather.cut
+    chip = Gather.chip
+    copy = Gather.copy
+    start = Gather.start
+    drain = Gather.drain
+    block = Gather.block
+
+    def from_sibling(self, back):
+        p = self.p
+        blk = pl.ds(4 * p.plane(back), 4)
+        c = pltpu.make_async_copy(self.block(p.plane(back), p.core), self.sums.at[blk], self.local.at[back])
+        c.start()
+        self.start(self.block(p.plane(back), 1 - p.core), self.from_core.at[blk], back, (p.z, p.sib))
+
+    def to_diagonal(self, back):
+        p, cut, rows = self.p, self.cut(back), self.rows
+        blk = pl.ds(4 * p.plane(back), 4)
+        pltpu.make_async_copy(self.block(p.plane(back), p.core), self.sums.at[blk], self.local.at[back]).wait()
+        self.copy(self.from_core.at[blk], self.from_core.at[blk], back, (p.z, p.sib)).wait_recv()
+        for j in range(4):
+            at = 4 * p.plane(back) + j
+            self.sums[at] = self.sums[at] + self.from_core[at]
+        cd = self.chip(back, p.spot_d)
+        self.start(self.sums.at[cd, pl.ds(0, cut)], self.la.at[back, pl.ds(0, cut)], 4 + back, (p.z, p.xn))
+        self.start(self.sums.at[cd, pl.ds(cut, rows - cut)], self.lb.at[back, pl.ds(0, rows - cut)], 8 + back, (p.z, p.yn))
+
+    def to_neighbours(self, back):
+        p, cut, rows = self.p, self.cut(back), self.rows
+        cx, cy = self.chip(back, p.spot_x), self.chip(back, p.spot_y)
+        a, b = self.la.at[back, pl.ds(0, cut)], self.lb.at[back, pl.ds(0, rows - cut)]
+        self.copy(a, a, 4 + back, (p.z, p.xn)).wait_recv()
+        self.sums[cy, 0:cut] = self.sums[cy, 0:cut] + a[...]
+        self.start(self.sums.at[cy], self.ly.at[back], 16 + back, (p.z, p.yn))
+        self.copy(b, b, 8 + back, (p.z, p.yn)).wait_recv()
+        self.sums[cx, cut:rows] = self.sums[cx, cut:rows] + b[...]
+        self.start(self.sums.at[cx], self.lx.at[back], 12 + back, (p.z, p.xn))
+
+    def along_z(self, back):
+        p = self.p
+        c0 = self.chip(back, p.spot)
+        lx, ly = self.lx.at[back], self.ly.at[back]
+        self.copy(lx, lx, 12 + back, (p.z, p.xn)).wait_recv()
+        self.copy(ly, ly, 16 + back, (p.z, p.yn)).wait_recv()
+        f = jnp.float32
+        got = self.sums[c0].astype(f) + lx[...].astype(f) + ly[...].astype(f)
+        self.sums[c0] = got.astype(jnp.bfloat16)
+        if back:
+            self.start(self.sums.at[c0], self.lz.at[back - 1], 20 + back - 1, (p.plane(back), p.f))
+
+    def owner(self):
+        p = self.p
+        f = jnp.float32
+        for k in range(3):
+            self.copy(self.lz.at[k], self.lz.at[k], 20 + k, (p.z, p.f)).wait_recv()
+        c0 = self.chip(0, p.spot)
+        total = self.sums[c0].astype(f)
+        for k in range(3):
+            total = total + self.lz[k].astype(f)
+        if self.half is None:
+            self.out[...] = total
+            return
+        self.total[...] = total
+        rows = self.rows // 2
+        theirs = pl.ds(pl.multiple_of((1 - p.core) * rows, 8), rows)
+        self.start(self.total.at[theirs], self.last, 23, (p.z, p.sib))
+
+    def finish(self):
+        if self.half is None:
+            return
+        p, half = self.p, self.half
+        rows = self.rows // 2
+        self.copy(self.last, self.last, 23, (p.z, p.sib)).wait_recv()
+        mine = pl.ds(pl.multiple_of(p.core * rows, 8), rows)
+        self.out[:, pl.ds(pl.multiple_of(p.core * half, 128), half)] = self.total[mine]
+        self.out[:, pl.ds(pl.multiple_of((1 - p.core) * half, 128), half)] = self.last[...]
+
+
+def scatter_steps(groups):
+    stages = [[], [], [], [], []]
+    seq = []
+    for i, g in enumerate(groups):
+        for s, fn in enumerate((g.from_sibling, g.to_diagonal, g.to_neighbours, g.along_z)):
+            for k in (3, 2, 1, 0):
+                seq.append((i + s, i, s, functools.partial(fn, k)))
+        seq.append((i + 4, i, 4, g.owner))
+        seq.append((i + 5, i, 5, g.finish))
+    seq.sort(key=lambda t: (t[0], -t[2] if t[2] < 1 else 0, t[1]))
+    steps = [t[3] for t in seq]
+    for g in groups:
+        steps.append(g.drain)
+    return steps
+
+
+def scatter_kernel(kinds, *refs):
+    n = len(kinds)
+    fulls, outs, rest = refs[:n], refs[n : 2 * n], list(refs[2 * n :])
+    local, send, recv = rest[-3:]
+    place = Place()
+    place.barrier()
+    groups, at = [], 0
+    for i, width in enumerate(kinds):
+        count = 7 if width is None else 9
+        groups.append(Scatter(place, fulls[i], rest[at : at + count], outs[i], send.at[i], recv.at[i], local.at[i], width))
+        at += count
+    for step in scatter_steps(groups):
+        step()
+
+
+def scatter_all(grads, cid):
+    kinds, outs, scratch = [], [], []
+    for g in grads:
+        if g.ndim == 3:
+            kinds.append(g.shape[2])
+            outs.append(jax.ShapeDtypeStruct((24, g.shape[2]), jnp.float32))
+            scratch += Scatter.scratch(48, g.shape[2] // 2, True)
+        else:
+            kinds.append(None)
+            outs.append(jax.ShapeDtypeStruct((96, g.shape[3]), jnp.float32))
+            scratch += Scatter.scratch(96, g.shape[3], False)
+    n = len(kinds)
+    return pl.pallas_call(
+        functools.partial(scatter_kernel, tuple(kinds)),
+        out_shape=tuple(outs),
+        in_specs=[ANY] * n,
+        out_specs=tuple([VMEM] * n),
+        scratch_shapes=scratch
+        + [pltpu.SemaphoreType.DMA((n, 4)), pltpu.SemaphoreType.DMA((n, Scatter.SEMS)), pltpu.SemaphoreType.DMA((n, Scatter.SEMS))],
+        compiler_params=pltpu.CompilerParams(
+            collective_id=cid, has_side_effects=True, vmem_limit_bytes=56 * 2**20
+        ),
+    )(*grads)
+
 
 HEADS = 12
 HEAD_DIM = 64
@@ -102,6 +518,74 @@
         grad_query.reshape(slot_count, width).astype(jnp.bfloat16),
         grad_key.reshape(slot_count, width).astype(jnp.bfloat16),
         grad_value.reshape(slot_count, width).astype(jnp.bfloat16),
+    )
+
+
+def own_kernels(shard_rows):
+    return lax.axis_size("dp") == PLANES and lax.axis_size("fsdp") == 8 and shard_rows == 24
+
+
+def gather_params(qkv, rest, outer, vectors, inner_bias):
+    rows = outer.shape[0] // 4
+    columns = [v[:, None] for v in vectors] + [inner_bias.reshape(rows, 4)]
+    pad = jnp.zeros((rows, 256 - len(vectors) - 4), jnp.bfloat16)
+    s0 = jnp.concatenate(list(qkv) + columns + [pad], axis=1)
+    s1 = jnp.concatenate(list(rest), axis=1)
+    if own_kernels(rows):
+        w0, w1, w2 = gather_all(s0.astype(jnp.float32), s1.astype(jnp.float32), outer)
+    else:
+        w0, w1, w2 = (lax.all_gather(s, ("dp", "fsdp"), axis=0, tiled=True) for s in (s0, s1, outer))
+    width = outer.shape[1]
+    w0, w1, w2 = w0.reshape(width, -1), w1.reshape(width, -1), w2.reshape(-1, width)
+    vec = w0[:, 3 * width :]
+    return (
+        *(w0[:, i * width : (i + 1) * width] for i in range(3)),
+        w1[:, :width],
+        w1[:, width:],
+        w2,
+        *(vec[:, i] for i in range(8)),
+        vec[:, 8:12].reshape(-1),
+    )
+
+
+def scatter_grads(qkv, rest, outer, vectors, inner_bias):
+    width = outer.shape[1]
+    columns = [v[:, None] for v in vectors] + [inner_bias.reshape(width, 4)]
+    pad = jnp.zeros((width, 256 - len(vectors) - 4), jnp.float32)
+    g0 = jnp.concatenate(list(qkv) + columns + [pad], axis=1)
+    g1 = jnp.concatenate(list(rest), axis=1)
+    devices = lax.axis_size("dp") * lax.axis_size("fsdp")
+    if own_kernels(width // devices):
+        low = jnp.bfloat16
+        o2, o1, o0 = scatter_all(
+            (
+                outer.astype(low).reshape(CHIPS, 2, 96, width),
+                g1.astype(low).reshape(CHIPS, 48, -1),
+                g0.astype(low).reshape(CHIPS, 48, -1),
+            ),
+            1,
+        )
+    else:
+        o2, o1, o0 = (
+            lax.psum_scatter(g, ("dp", "fsdp"), scatter_dimension=0, tiled=True) for g in (outer, g1, g0)
+        )
+    vec = o0[:, 3 * width :]
+    return (
+        o0[:, :width],
+        vec[:, 0],
+        o0[:, width : 2 * width],
+        o0[:, 2 * width : 3 * width],
+        vec[:, 1],
+        o1[:, :width],
+        vec[:, 2],
+        vec[:, 3],
+        vec[:, 4],
+        o1[:, width:],
+        vec[:, 8:12].reshape(-1),
+        o2,
+        vec[:, 5],
+        vec[:, 6],
+        vec[:, 7],
     )
 
 
@@ -126,40 +610,30 @@
     second_gain,
     second_shift,
 ):
-    gathered = (
-        lax.all_gather(query_weight, ("dp", "fsdp"), axis=0, tiled=True),
-        lax.all_gather(query_bias, ("dp", "fsdp"), axis=0, tiled=True),
-        lax.all_gather(key_weight, ("dp", "fsdp"), axis=0, tiled=True),
-        lax.all_gather(value_weight, ("dp", "fsdp"), axis=0, tiled=True),
-        lax.all_gather(value_bias, ("dp", "fsdp"), axis=0, tiled=True),
-        lax.all_gather(out_weight, ("dp", "fsdp"), axis=0, tiled=True),
-        lax.all_gather(out_bias, ("dp", "fsdp"), axis=0, tiled=True),
-        lax.all_gather(first_gain, ("dp", "fsdp"), axis=0, tiled=True),
-        lax.all_gather(first_shift, ("dp", "fsdp"), axis=0, tiled=True),
-        lax.all_gather(inner_weight, ("dp", "fsdp"), axis=0, tiled=True),
-        lax.all_gather(inner_bias, ("dp", "fsdp"), axis=0, tiled=True),
-        lax.all_gather(outer_weight, ("dp", "fsdp"), axis=0, tiled=True),
-        lax.all_gather(outer_bias, ("dp", "fsdp"), axis=0, tiled=True),
-        lax.all_gather(second_gain, ("dp", "fsdp"), axis=0, tiled=True),
-        lax.all_gather(second_shift, ("dp", "fsdp"), axis=0, tiled=True),
+    w_all = gather_params(
+        (query_weight, key_weight, value_weight), (out_weight, inner_weight), outer_weight,
+        (query_bias, value_bias, out_bias, first_gain, first_shift, outer_bias, second_gain, second_shift),
+        inner_bias,
     )
     (
         w_query,
-        b_query,
         w_key,
         w_value,
+        w_out,
+        w_inner,
+        w_outer,
+        b_query,
         b_value,
-        w_out,
         b_out,
         g_first,
         s_first,
-        w_inner,
-        b_inner,
-        w_outer,
         b_outer,
         g_second,
         s_second,
-    ) = gathered
+        b_inner,
+    ) = w_all
+    back_query, back_key, back_value, back_out = w_query, w_key, w_value, w_out
+    back_first, back_inner, back_outer, back_second = g_first, w_inner, w_outer, g_second
     text_count = alignment.shape[1]
     slot_count = tokens.shape[1]
     seg_count = slot_count - text_count
@@ -195,40 +669,6 @@
     second_sum = normed + apply_weight(act_low, w_outer) + b_outer
     second_hat, second_inv = norm_parts(second_sum)
     encoded = (second_hat * g_second + s_second).astype(jnp.bfloat16)
-    regathered = (
-        lax.all_gather(query_weight, ("dp", "fsdp"), axis=0, tiled=True),
-        lax.all_gather(query_bias, ("dp", "fsdp"), axis=0, tiled=True),
-        lax.all_gather(key_weight, ("dp", "fsdp"), axis=0, tiled=True),
-        lax.all_gather(value_weight, ("dp", "fsdp"), axis=0, tiled=True),
-        lax.all_gather(value_bias, ("dp", "fsdp"), axis=0, tiled=True),
-        lax.all_gather(out_weight, ("dp", "fsdp"), axis=0, tiled=True),
-        lax.all_gather(out_bias, ("dp", "fsdp"), axis=0, tiled=True),
-        lax.all_gather(first_gain, ("dp", "fsdp"), axis=0, tiled=True),
-        lax.all_gather(first_shift, ("dp", "fsdp"), axis=0, tiled=True),
-        lax.all_gather(inner_weight, ("dp", "fsdp"), axis=0, tiled=True),
-        lax.all_gather(inner_bias, ("dp", "fsdp"), axis=0, tiled=True),
-        lax.all_gather(outer_weight, ("dp", "fsdp"), axis=0, tiled=True),
-        lax.all_gather(outer_bias, ("dp", "fsdp"), axis=0, tiled=True),
-        lax.all_gather(second_gain, ("dp", "fsdp"), axis=0, tiled=True),
-        lax.all_gather(second_shift, ("dp", "fsdp"), axis=0, tiled=True),
-    )
-    (
-        back_query,
-        unused_qb,
-        back_key,
-        back_value,
-        unused_vb,
-        back_out,
-        unused_ob,
-        back_first,
-        unused_fs,
-        back_inner,
-        unused_ib,
-        back_outer,
-        unused_xb,
-        back_second,
-        unused_ss,
-    ) = regathered
     grad_y = cotangent.astype(jnp.float32)
     grad_second_gain = jnp.sum(grad_y * second_hat, axis=(0, 1))
     grad_second_shift = jnp.sum(grad_y, axis=(0, 1))
@@ -273,22 +713,13 @@
     grad_tokens = jnp.concatenate(
         [grad_base[:, :text_count] + spread_back, grad_base[:, text_count:]], axis=1
     ).astype(jnp.bfloat16)
-    owned = (
-        lax.psum_scatter(grad_query_weight, ("dp", "fsdp"), scatter_dimension=0, tiled=True),
-        lax.psum_scatter(grad_query_bias, ("dp", "fsdp"), scatter_dimension=0, tiled=True),
-        lax.psum_scatter(grad_key_weight, ("dp", "fsdp"), scatter_dimension=0, tiled=True),
-        lax.psum_scatter(grad_value_weight, ("dp", "fsdp"), scatter_dimension=0, tiled=True),
-        lax.psum_scatter(grad_value_bias, ("dp", "fsdp"), scatter_dimension=0, tiled=True),
-        lax.psum_scatter(grad_out_weight, ("dp", "fsdp"), scatter_dimension=0, tiled=True),
-        lax.psum_scatter(grad_out_bias, ("dp", "fsdp"), scatter_dimension=0, tiled=True),
-        lax.psum_scatter(grad_first_gain, ("dp", "fsdp"), scatter_dimension=0, tiled=True),
-        lax.psum_scatter(grad_first_shift, ("dp", "fsdp"), scatter_dimension=0, tiled=True),
-        lax.psum_scatter(grad_inner_weight, ("dp", "fsdp"), scatter_dimension=0, tiled=True),
-        lax.psum_scatter(grad_inner_bias, ("dp", "fsdp"), scatter_dimension=0, tiled=True),
-        lax.psum_scatter(grad_outer_weight, ("dp", "fsdp"), scatter_dimension=0, tiled=True),
-        lax.psum_scatter(grad_outer_bias, ("dp", "fsdp"), scatter_dimension=0, tiled=True),
-        lax.psum_scatter(grad_second_gain, ("dp", "fsdp"), scatter_dimension=0, tiled=True),
-        lax.psum_scatter(grad_second_shift, ("dp", "fsdp"), scatter_dimension=0, tiled=True),
+    owned = scatter_grads(
+        (grad_query_weight, grad_key_weight, grad_value_weight),
+        (grad_out_weight, grad_inner_weight),
+        grad_outer_weight,
+        (grad_query_bias, grad_value_bias, grad_out_bias, grad_first_gain, grad_first_shift, grad_outer_bias,
+         grad_second_gain, grad_second_shift),
+        grad_inner_bias,
     )
     return (
         encoded,

time: 1170 us -> 599 us (0.51)
  waiting for transfers between devices: 641 us -> 0 us
  Pallas kernels: 0 us -> 155 us
  blocking collectives: 83.5 us -> 0 us
  local copies, waits for them, and re-layouts: 57.4 us -> 74.2 us
  between operations: 15.2 us -> 1.74 us
  matrix products: 252 us -> 240 us
    reduce_scatter x6 -> x0, waiting for transfers between devices: 490 us -> none  [the longest x1 142 us: shards(): lax.psum_scatter(grad_outer_weight, ('dp', 'fsdp'), scatter_dimension=0,...]
    pallas_call x0 -> x2, Pallas kernels: none -> 155 us  [the longest x1 78.7 us: gather_all(): pl.pallas_call(gather_kernel, out_shape=(jax.ShapeDtypeStruct((CHIPS, 48,...]
    all_gather x6 -> x0, waiting for transfers between devices: 148 us -> none  [the longest x1 50 us: shards(): lax.all_gather(key_weight, ('dp', 'fsdp'), axis=0, tiled=True)]
    unnamed x2 -> x0, blocking collectives: 83.5 us -> none
    concatenate x0 -> x11, local copies, waits for them, and re-layouts: none -> 18 us  [the longest x10 17.1 us: scatter_grads(): g0 = jnp.concatenate(list(qkv) + columns + [pad], axis=1)]
    dot_general x6, matrix products: 44.3 us -> 29.9 us  [weight_grad(): jnp.einsum('bsd,bse->de', left_rows, right_rows, preferred_element_type=j...]
    unnamed x123 -> x87, local copies, waits for them, and re-layouts: 20.5 us -> 6.48 us
  transfers between devices with their start and end apart: 12 -> 0, of which waited for: 8 -> 0; matrix products, arithmetic and copies ran while one was open for 31% -> 0% of each run, Pallas kernels for 0% -> 0%
where the time goes in v1:
time: 599 us; the launch traced here: 590 us
  matrix products  240 us (40%)
  Pallas kernels  155 us (26%)
  other arithmetic  118 us (20%)
  local copies, waits for them, and re-layouts  74.2 us (12%)
    pallas_call x1, Pallas kernels, gather_all(): pl.pallas_call(gather_kernel, out_shape=(jax.ShapeDtypeStruct((CHIPS, 48,...  78.7 us
    pallas_call x1, Pallas kernels, scatter_all(): pl.pallas_call(functools.partial(scatter_kernel, tuple(kinds)), out_shape...  76.6 us
    dot_general x6, matrix products, apply_weight(): jnp.einsum('bsd,de->bse', left_rows, weight_mat, preferred_element_type=j...  50.4 us
    dot_general x6, matrix products, apply_transposed(): jnp.einsum('bse,de->bsd', left_rows, weight_mat, preferred_element_type=j...  43.3 us
    convert_element_type x1, other arithmetic, shards(): act_low = jax.nn.gelu(pre_act, approximate=False).astype(jnp.bfloat16)  38.6 us
    dot_general x4, matrix products, score_block(): jnp.einsum('qhd,khd->hqk', split_heads(query_rows), split_heads(key_rows)...  34.2 us
    dot_general x6, matrix products, weight_grad(): jnp.einsum('bsd,bse->de', left_rows, right_rows, preferred_element_type=j...  29.9 us
    convert_element_type x2, other arithmetic, attend_backward(): grad_scores_low = grad_scores.astype(jnp.bfloat16)  27.5 us

profile of v1, /device:TPU:0, one launch (start us, length us, event | category | flops | bytes accessed | tf_op | source)
XLA Modules:
  0.0 590.5 jit_solution(14321362915146767467)
XLA Ops:
  10.7 1.7 maximum_convert_fusion.s1
  12.4 2.0 fusion.47
  14.4 78.7 %shard_map.314 = (bf16[16,48,2560]{2,1,0:T(8,128)(2,1)}, bf16[16,48,3840]{2,1,0:T(8,128)(2,1)}, bf16[16,2,96,768]{3,2,1,0:T(8,128)(2,1)}) custom-call(f32[24,2560]{1,0:T(8,128)} %convert_element_type.227.s0, f32[24,3840]{1,0:T(8,128)} %maximum_convert_fusion.s1, bf16[96,768]{1,0:T(8,128)(2,1)} %s2_.1), custom_call_target="tpu_custom_call" | custom-call | tf_op jit(solution)/shard_map/pallas_call | solution.py:235
  93.2 3.7 convert_reduce_fusion.2
  98.8 3.6 add_convert_fusion.1
  102.4 2.3 copy.82
  104.6 4.8 add_convert_fusion.2
  109.5 2.9 copy.81
  112.3 4.8 convolution_convert_fusion.1
  117.2 4.0 copy.83
  121.2 65.2 %while.26 = (s32[]{:T(128)}, bf16[2,640,768]{1,2,0:T(8,128)(2,1)}, f32[2,12,640,1]{2,1,3,0:T(8,128)S(1)}, bf16[2,640,768]{1,2,0:T(8,128)(2,1)S(1)}, pred[2,640]{...) while((s32[]{:T(128)}, bf16[2,640,768]{1,2,0:T(8,128)(2,1)}, ...), condition=%wide.region_4.5_spmd, body=%wide.region_1.4_spmd.sunk | while | flops 1317265920 | bytes 86787368 | solution.py:661
  121.5 1.7 constant_dynamic-slice_fusion.14
  123.2 8.9 %fusion.128 = (f32[12,640]{1,0:T(8,128)S(1)}, f32[12,640,640]{1,2,0:T(8,128)}) fusion(pred[640]{0:T(1024)(128)(4,1)S(1)} %dynamic-slice_reduce_fusion.4, bf16[640,12,64]{0,2,1:T(8,128)(2,1)S(1)} %bitcast.172, bf16[640,12,64]{0,2,1:T(8,128)(2,1)S(1)} %bitcast.171), kind=kOutput, calls=%fused_computation.3.clone.1 | convolution fusion | flops 643883520 | bytes 21658240 | tf_op jit(solution)/shard_map/while/body/eval_jaxpr/qhd,khd->hqk/dot_general | solution.py:474
  132.1 10.6 %fusion.129 = f32[12,640]{1,0:T(8,128)S(1)} fusion(f32[12,640,640]{1,2,0:T(8,128)} %get-tuple-element.350, f32[12,640]{1,0:T(8,128)S(1)} %get-tuple-element.351, pred[640]{0:T(1024)(128)(4,1)S(1)} %dynamic-slice_reduce_fusion.4), kind=kLoop, calls=%fused_computation.4.clone.1 | loop fusion | flops 19653120 | bytes 19722880 | tf_op jit(solution)/shard_map/while/body/eval_jaxpr/reduce_sum | solution.py:488
  142.7 9.5 %fusion.130 = bf16[12,64,640]{2,1,0:T(8,128)(2,1)S(1)} fusion(bf16[640,12,64]{0,2,1:T(8,128)(2,1)S(1)} %bitcast.173, f32[12,640,640]{1,2,0:T(8,128)} %get-tuple-element.350, f32[12,640]{1,0:T(8,128)S(1)} %fusion.129, f32[12,640]{1,0:T(8,128)S(1)} %get-tuple-element.351, pred[640]{0:T(1024)(128)(4,1)S(1)} %dynamic-slice_reduce_fusion.4), kind=kOutput, calls=%fused_computation.5.clone.1 | convolution fusion | flops 653721600 | bytes 21688960 | tf_op jit(solution)/shard_map/while/body/eval_jaxpr/hqk,khd->qhd/dot_general | solution.py:490
  153.8 1.7 constant_dynamic-slice_fusion.14
  155.5 8.9 %fusion.128 = (f32[12,640]{1,0:T(8,128)S(1)}, f32[12,640,640]{1,2,0:T(8,128)}) fusion(pred[640]{0:T(1024)(128)(4,1)S(1)} %dynamic-slice_reduce_fusion.4, bf16[640,12,64]{0,2,1:T(8,128)(2,1)S(1)} %bitcast.172, bf16[640,12,64]{0,2,1:T(8,128)(2,1)S(1)} %bitcast.171), kind=kOutput, calls=%fused_computation.3.clone.1 | convolution fusion | flops 643883520 | bytes 21658240 | tf_op jit(solution)/shard_map/while/body/eval_jaxpr/qhd,khd->hqk/dot_general | solution.py:474
  164.4 10.6 %fusion.129 = f32[12,640]{1,0:T(8,128)S(1)} fusion(f32[12,640,640]{1,2,0:T(8,128)} %get-tuple-element.350, f32[12,640]{1,0:T(8,128)S(1)} %get-tuple-element.351, pred[640]{0:T(1024)(128)(4,1)S(1)} %dynamic-slice_reduce_fusion.4), kind=kLoop, calls=%fused_computation.4.clone.1 | loop fusion | flops 19653120 | bytes 19722880 | tf_op jit(solution)/shard_map/while/body/eval_jaxpr/reduce_sum | solution.py:488
  175.0 9.5 %fusion.130 = bf16[12,64,640]{2,1,0:T(8,128)(2,1)S(1)} fusion(bf16[640,12,64]{0,2,1:T(8,128)(2,1)S(1)} %bitcast.173, f32[12,640,640]{1,2,0:T(8,128)} %get-tuple-element.350, f32[12,640]{1,0:T(8,128)S(1)} %fusion.129, f32[12,640]{1,0:T(8,128)S(1)} %get-tuple-element.351, pred[640]{0:T(1024)(128)(4,1)S(1)} %dynamic-slice_reduce_fusion.4), kind=kOutput, calls=%fused_computation.5.clone.1 | convolution fusion | flops 653721600 | bytes 21688960 | tf_op jit(solution)/shard_map/while/body/eval_jaxpr/hqk,khd->qhd/dot_general | solution.py:490
  186.4 4.8 fusion.73
  191.3 1.8 copy-done.2
  193.7 20.1 %fusion.38 = (u8[640,3072]{1,0:T(8,128)(4,1)}, u8[640,3072]{1,0:T(8,128)(4,1)}, f32[2,640,3072]{2,1,0:T(8,128)}) fusion(f32[3072]{0:T(1024)S(1)} %copy-done.31, bf16[768,3840]{1,0:T(8,128)(2,1)} %bitcast.201, f32[2,640,768]{2,1,0:T(8,128)} %copy-done.2, f32[768]{0:T(1024)S(1)} %copy-done.35, f32[768]{0:T(1024)S(1)} %copy-done.29, ...), kind=kOutput, calls=%fused_computation.91 | convolution fusion | flops 6095831040 | bytes 28340224 | tf_op jit(solution)/shard_map/bsd,de->bse/dot_general | solution.py:454
  213.8 38.6 %fusion.16 = bf16[2,640,3072]{2,1,0:T(8,128)(2,1)S(1)} fusion(f32[2,640,3072]{2,1,0:T(8,128)} %get-tuple-element.238, f32[3072]{0:T(1024)S(1)} %copy-done.31, u8[640,3072]{1,0:T(8,128)(4,1)} %get-tuple-element.161, u8[640,3072]{1,0:T(8,128)(4,1)} %get-tuple-element.160), kind=kLoop, calls=%fused_computation.38 | loop fusion | flops 279183360 | bytes 27537408 | tf_op jit(solution)/shard_map/convert_element_type | solution.py:668
  252.5 12.2 %fusion.74 = (f32[2,640]{1,0:T(2,128)S(1)}, f32[2,640,768]{2,1,0:T(8,128)S(1)}) fusion(f32[768]{0:T(1024)S(1)} %copy-done.36, bf16[2,640,3072]{2,1,0:T(8,128)(2,1)S(1)} %fusion.16, bf16[3072,768,1]{1,0,2:T(8,128)(2,1)} %bitcast.204, f32[768]{0:T(1024)S(1)} %copy-done.35, f32[768]{0:T(1024)S(1)} %copy-done.29, f32[2,640]{1,0:T(2,128)S(1)} %add_rsqrt_fusion.1, ...), kind=kOutput, calls=%fused_computation.162 | convolution fusion | flops 6046678016 | bytes 20471808 | tf_op jit(solution)/shard_map/bsd,de->bse/dot_general | solution.py:454
  265.4 2.3 copy-done.13
  267.7 3.0 fusion.35
  271.8 4.4 fusion.68
  276.2 16.9 %fusion.75 = (bf16[3072]{0:T(1024)(128)(2,1)S(1)}, bf16[2,640,3072]{2,1,0:T(8,128)(2,1)}) fusion(f32[2,640,3072]{2,1,0:T(8,128)} %get-tuple-element.238, f32[3072]{0:T(1024)S(1)} %copy-done.31, bf16[2,640,768]{2,1,0:T(8,128)(2,1)S(1)} %get-tuple-element.220, bf16[3072,768,1]{1,0,2:T(8,128)(2,1)} %bitcast.205), kind=kOutput, calls=%fused_computation.163 | convolution fusion | flops 6086980608 | bytes 30296064 | tf_op jit(solution)/shard_map/bse,de->bsd/dot_general | solution.py:458
  293.2 8.3 %bitcast_convert_fusion.1 = bf16[3072,768]{1,0:T(8,128)(2,1)} fusion(bf16[2,640,3072]{2,1,0:T(8,128)(2,1)S(1)} %bitcast.177, bf16[2,640,768]{2,1,0:T(8,128)(2,1)S(1)} %get-tuple-element.220), kind=kOutput, calls=%fused_computation.64 | convolution fusion | flops 6042157056 | bytes 14548992 | tf_op jit(solution)/shard_map/bsd,bse->de/dot_general | solution.py:462
  301.4 12.9 %multiply_reduce_fusion.1 = (bf16[768]{0:T(1024)(128)(2,1)S(1)}, f32[2,640]{1,0:T(2,128)S(1)}, f32[2,640]{1,0:T(2,128)S(1)}, bf16[768]{0:T(1024)(128)(2,1)S(1)}, f32[2,640,768]{2,1,0:T(8,128)}) fusion(f32[2,640,768]{2,1,0:T(8,128)S(1)} %copy-done.4, f32[2,640]{1,0:T(2,128)S(1)} %add_rsqrt_fusion.1, f32[2,640]{1,0:T(2,128)S(1)} %broadcast_multiply_fusion.5, ...), kind=kOutput, calls=%fused_computation.76 | convolution fusion | flops 6057488384 | bytes 26395648 | tf_op jit(solution)/shard_map/bse,de->bsd/dot_general | solution.py:458
  319.6 4.7 fusion.70
  324.4 10.2 %bitcast_convert_fusion = bf16[768,3072]{1,0:T(8,128)(2,1)S(1)} fusion(bf16[2,640,3072]{2,1,0:T(8,128)(2,1)} %get-tuple-element.243, f32[2,640,768]{2,1,0:T(8,128)S(1)} %copy-done.5, f32[768]{0:T(1024)S(1)} %copy-done.35, f32[768]{0:T(1024)S(1)} %copy-done.29, f32[2,640]{1,0:T(2,128)S(1)} %add_rsqrt_fusion.1, f32[2,640]{1,0:T(2,128)S(1)} %broadcast_multiply_fusion.5), kind=kOutput, calls=%fused_computation.63 | convolution fusion | flops 6047072256 | bytes 16531456 | tf_op jit(solution)/shard_map/bsd,bse->de/dot_general | solution.py:462
  334.6 4.5 convolution_convert_fusion
  339.0 1.7 bitcast_convert_fusion.5
  340.7 2.9 pad_maximum_fusion.refs_1_
  343.7 122.7 %while.27 = (s32[]{:T(128)}, bf16[2,640,768]{1,2,0:T(8,128)(2,1)}, bf16[2,640,768]{1,2,0:T(8,128)(2,1)}, bf16[2,640,768]{1,2,0:T(8,128)(2,1)}, bf16[2,640,768]{1...) while((s32[]{:T(128)}, bf16[2,640,768]{1,2,0:T(8,128)(2,1)}, ...), condition=%wide.region_15.16_spmd, body=%wide.region_13.15_spmd.sunk | while | flops 3221905920 | bytes 236148240 | solution.py:692
  349.6 8.2 %fusion.141 = f32[12,640,640]{1,2,0:T(8,128)} fusion(bf16[640,12,64]{0,2,1:T(8,128)(2,1)S(1)} %bitcast.164, bf16[640,12,64]{0,2,1:T(8,128)(2,1)S(1)} %bitcast.162), kind=kOutput, calls=%fused_computation.164.clone.1 | convolution fusion | flops 629145600 | bytes 21626880 | tf_op jit(solution)/shard_map/while/body/eval_jaxpr/qhd,khd->hqk/dot_general | solution.py:474
  357.8 11.2 %fusion.142 = bf16[12,64,640]{2,1,0:T(8,128)(2,1)S(1)} fusion(bf16[640,12,64]{0,2,1:T(8,128)(2,1)S(1)} %bitcast.168, f32[12,640,640]{1,2,0:T(8,128)} %fusion.141, f32[12,640]{1,0:T(8,128)S(1)} %dynamic-slice_bitcast_fusion.2, pred[640]{0:T(1024)(128)(4,1)S(1)} %dynamic-slice_reduce_fusion.5), kind=kOutput, calls=%fused_computation.22.clone.1 | convolution fusion | flops 649297920 | bytes 21658240 | tf_op jit(solution)/shard_map/while/body/eval_jaxpr/hqk,qhd->khd/dot_general | solution.py:505
  369.1 13.7 %multiply_reduce_fusion.7 = (f32[12,640]{1,0:T(8,128)S(1)}, f32[12,640,640]{1,2,0:T(8,128)}) fusion(f32[12,640,640]{1,2,0:T(8,128)} %fusion.141, f32[12,640]{1,0:T(8,128)S(1)} %dynamic-slice_bitcast_fusion.2, pred[640]{0:T(1024)(128)(4,1)S(1)} %dynamic-slice_reduce_fusion.5, bf16[640,12,64]{0,2,1:T(8,128)(2,1)S(1)} %bitcast.169, ...), kind=kOutput, calls=%fused_computation.15.clone.1 | convolution fusion | flops 653713920 | bytes 41349760 | tf_op jit(solution)/shard_map/while/body/eval_jaxpr/qhd,khd->hqk/dot_general | solution.py:502
  382.8 13.8 %multiply_convert_fusion.6 = bf16[12,640,640]{1,2,0:T(8,128)(2,1)S(1)} fusion(f32[12,640,640]{1,2,0:T(8,128)} %get-tuple-element.362, f32[12,640,640]{1,2,0:T(8,128)} %fusion.141, f32[12,640]{1,0:T(8,128)S(1)} %get-tuple-element.363, f32[12,640]{1,0:T(8,128)S(1)} %dynamic-slice_bitcast_fusion.2, pred[640]{0:T(1024)(128)(4,1)S(1)} %dynamic-slice_reduce_fusion.5), kind=kLoop, calls=%fused_computation.14.clone.1 | loop fusion | flops 29491200 | bytes 49214080 | tf_op jit(solution)/shard_map/while/body/eval_jaxpr/convert_element_type | solution.py:509
  396.5 3.2 multiply_convert_fusion.8
  399.8 1.7 multiply_convert_fusion.7
  410.8 8.2 %fusion.141 = f32[12,640,640]{1,2,0:T(8,128)} fusion(bf16[640,12,64]{0,2,1:T(8,128)(2,1)S(1)} %bitcast.164, bf16[640,12,64]{0,2,1:T(8,128)(2,1)S(1)} %bitcast.162), kind=kOutput, calls=%fused_computation.164.clone.1 | convolution fusion | flops 629145600 | bytes 21626880 | tf_op jit(solution)/shard_map/while/body/eval_jaxpr/qhd,khd->hqk/dot_general | solution.py:474
  419.0 11.2 %fusion.142 = bf16[12,64,640]{2,1,0:T(8,128)(2,1)S(1)} fusion(bf16[640,12,64]{0,2,1:T(8,128)(2,1)S(1)} %bitcast.168, f32[12,640,640]{1,2,0:T(8,128)} %fusion.141, f32[12,640]{1,0:T(8,128)S(1)} %dynamic-slice_bitcast_fusion.2, pred[640]{0:T(1024)(128)(4,1)S(1)} %dynamic-slice_reduce_fusion.5), kind=kOutput, calls=%fused_computation.22.clone.1 | convolution fusion | flops 649297920 | bytes 21658240 | tf_op jit(solution)/shard_map/while/body/eval_jaxpr/hqk,qhd->khd/dot_general | solution.py:505
  430.2 13.7 %multiply_reduce_fusion.7 = (f32[12,640]{1,0:T(8,128)S(1)}, f32[12,640,640]{1,2,0:T(8,128)}) fusion(f32[12,640,640]{1,2,0:T(8,128)} %fusion.141, f32[12,640]{1,0:T(8,128)S(1)} %dynamic-slice_bitcast_fusion.2, pred[640]{0:T(1024)(128)(4,1)S(1)} %dynamic-slice_reduce_fusion.5, bf16[640,12,64]{0,2,1:T(8,128)(2,1)S(1)} %bitcast.169, ...), kind=kOutput, calls=%fused_computation.15.clone.1 | convolution fusion | flops 653713920 | bytes 41349760 | tf_op jit(solution)/shard_map/while/body/eval_jaxpr/qhd,khd->hqk/dot_general | solution.py:502
  444.0 13.8 %multiply_convert_fusion.6 = bf16[12,640,640]{1,2,0:T(8,128)(2,1)S(1)} fusion(f32[12,640,640]{1,2,0:T(8,128)} %get-tuple-element.362, f32[12,640,640]{1,2,0:T(8,128)} %fusion.141, f32[12,640]{1,0:T(8,128)S(1)} %get-tuple-element.363, f32[12,640]{1,0:T(8,128)S(1)} %dynamic-slice_bitcast_fusion.2, pred[640]{0:T(1024)(128)(4,1)S(1)} %dynamic-slice_reduce_fusion.5), kind=kLoop, calls=%fused_computation.14.clone.1 | loop fusion | flops 29491200 | bytes 49214080 | tf_op jit(solution)/shard_map/while/body/eval_jaxpr/convert_element_type | solution.py:509
  457.7 3.2 multiply_convert_fusion.8
  461.0 1.7 multiply_convert_fusion.7
  466.4 1.9 reduce.1
  468.3 1.9 reduce
  473.3 4.3 bitcast_convert_fusion.3
  477.6 2.8 bitcast_convert_fusion.2
  480.3 2.8 bitcast_convert_fusion.4
  483.1 7.7 %concatenate.70.refs_2_ = bf16[16,48,2560]{2,1,0:T(8,128)(2,1)} concatenate(bf16[16,48,768]{2,1,0:T(8,128)(2,1)} %bitcast.190, bf16[16,48,768]{2,1,0:T(8,128)(2,1)S(1)} %bitcast.188, bf16[16,48,768]{2,1,0:T(8,128)(2,1)} %bitcast.189, bf16[16,48,1]{2,1,0:T(8,128)(2,1)} %concatenate.71, bf16[16,48,1]{2,1,0:T(8,128)(2,1)} %concatenate.72, bf16[16,48,1]{2,1,0:T(8,128)(2,1)} %concatenate.73, ...), dimensions={2} | concatenate | bytes 7864320 | tf_op jit(solution)/shard_map/concatenate | solution.py:555
  490.9 76.6 %shard_map.315 = (f32[96,768]{1,0:T(8,128)}, f32[24,3840]{1,0:T(8,128)}, f32[24,2560]{1,0:T(8,128)}) custom-call(bf16[16,2,96,768]{3,2,1,0:T(8,128)(2,1)} %bitcast.178, bf16[16,48,3840]{2,1,0:T(8,128)(2,1)} %pad_maximum_fusion.refs_1_, bf16[16,48,2560]{2,1,0:T(8,128)(2,1)} %concatenate.70.refs_2_), custom_call_target="tpu_custom_call" | custom-call | tf_op jit(solution)/shard_map/pallas_call | solution.py:409
  567.4 1.8 slice_reduce_fusion
  570.0 1.6 fusion.72
  572.3 1.5 slice.136
  573.8 1.7 slice.140
  575.5 3.8 fusion.52
  579.4 1.8 fusion.53
  582.7 3.4 add_add_fusion
  586.2 1.8 fusion.42
  588.0 1.4 pad_maximum_fusion.1
  (197 shorter events, 47.9 us)
Async XLA Ops:
  2.2 94.7 %copy-start.39 = (f32[2,128]{1,0:T(2,128)}, f32[2,128]{1,0:T(2,128)S(1)}, u32[]{:S(2)}) copy-start(f32[2,128]{1,0:T(2,128)S(1)} %broadcast_maximum_fusion) | copy-start | bytes 3076
  14.4 90.2 %copy-start.48 = (f32[2,128,768]{2,1,0:T(8,128)}, f32[2,128,768]{2,1,0:T(8,128)S(1)}, u32[]{:S(2)}) copy-start(f32[2,128,768]{2,1,0:T(8,128)S(1)} %fusion.47) | copy-start | bytes 2359300
  109.5 2.9 copy-start.49
  121.2 65.2 %copy-start.37 = (f32[768]{0:T(1024)S(1)}, f32[768]{0:T(1024)}, u32[]{:S(2)}) copy-start(f32[768]{0:T(1024)} %get-tuple-element.173) | copy-start | bytes 9220
  142.7 9.5 %copy-start.45 = (bf16[2,640,768]{1,2,0:T(8,128)(2,1)S(1)}, bf16[2,640,768]{1,2,0:T(8,128)(2,1)}, u32[]{:S(2)}) copy-start(bf16[2,640,768]{1,2,0:T(8,128)(2,1)} %get-tuple-element.375) | copy-start | bytes 5898244 | tf_op jit(solution)/shard_map/while
  152.4 1.3 copy-start.46
  175.0 9.5 %copy-start.45 = (bf16[2,640,768]{1,2,0:T(8,128)(2,1)S(1)}, bf16[2,640,768]{1,2,0:T(8,128)(2,1)}, u32[]{:S(2)}) copy-start(bf16[2,640,768]{1,2,0:T(8,128)(2,1)} %get-tuple-element.375) | copy-start | bytes 5898244 | tf_op jit(solution)/shard_map/while
  184.7 1.3 copy-start.46
  191.2 1.9 copy-start.2
  191.2 2.5 copy-start.29
  191.2 2.5 copy-start.31
  191.2 2.5 copy-start.35
  193.1 131.3 %copy-start.21 = (f32[2,640]{1,0:T(2,128)}, f32[2,640]{1,0:T(2,128)S(1)}, u32[]{:S(2)}) copy-start(f32[2,640]{1,0:T(2,128)S(1)} %broadcast_multiply_fusion.5) | copy-start | bytes 15364
  193.7 130.6 %copy-start.23 = (f32[2,640]{1,0:T(2,128)}, f32[2,640]{1,0:T(2,128)S(1)}, u32[]{:S(2)}) copy-start(f32[2,640]{1,0:T(2,128)S(1)} %add_rsqrt_fusion.1) | copy-start | bytes 15364
  213.8 38.6 %copy-start.3 = (f32[2,640,768]{2,1,0:T(8,128)S(1)}, f32[2,640,768]{2,1,0:T(8,128)}, u32[]{:S(2)}) copy-start(f32[2,640,768]{2,1,0:T(8,128)} %copy-done.2) | copy-start | bytes 11796484
  213.8 38.7 %copy-start.36 = (f32[768]{0:T(1024)S(1)}, f32[768]{0:T(1024)}, u32[]{:S(2)}) copy-start(f32[768]{0:T(1024)} %get-tuple-element.170) | copy-start | bytes 9220
  252.5 12.2 %copy-start.15 = (bf16[2,640,3072]{2,1,0:T(8,128)(2,1)}, bf16[2,640,3072]{2,1,0:T(8,128)(2,1)S(1)}, u32[]{:S(2)}) copy-start(bf16[2,640,3072]{2,1,0:T(8,128)(2,1)S(1)} %fusion.16) | copy-start | bytes 23592964
  264.7 6.0 %copy-start.7 = (f32[2,640,768]{2,1,0:T(8,128)}, f32[2,640,768]{2,1,0:T(8,128)S(1)}, u32[]{:S(2)}) copy-start(f32[2,640,768]{2,1,0:T(8,128)S(1)} %get-tuple-element.240) | copy-start | bytes 11796484
  264.7 3.0 copy-start.13
  264.7 3.0 copy-start.32
  264.8 2.9 copy-start.33
  271.8 21.3 %slice-start = ((s8[7864320]{0:T(1024)(128)(4,1)}), s8[4194304]{0:T(1024)(128)(4,1)S(1)}, s32[]{:S(2)}) async-start(s8[7864320]{0:T(1024)(128)(4,1)} %bitcast.176), calls=%async_computation | async-start | bytes 8388608
  276.2 16.9 %slice-start.1 = ((s8[7864320]{0:T(1024)(128)(4,1)}), s8[3670016]{0:T(1024)(128)(4,1)S(1)}, s32[]{:S(2)}) async-start(s8[7864320]{0:T(1024)(128)(4,1)} %bitcast.176), calls=%async_computation.1 | async-start | bytes 7340032
  293.1 8.3 %copy-start.4 = (f32[2,640,768]{2,1,0:T(8,128)S(1)}, f32[2,640,768]{2,1,0:T(8,128)}, u32[]{:S(2)}) copy-start(f32[2,640,768]{2,1,0:T(8,128)} %copy-done.2) | copy-start | bytes 11796484
  293.1 8.3 %copy-start.8 = (f32[2,640,768]{2,1,0:T(8,128)S(1)}, f32[2,640,768]{2,1,0:T(8,128)}, u32[]{:S(2)}) copy-start(f32[2,640,768]{2,1,0:T(8,128)} %copy-done.7) | copy-start | bytes 11796484
  293.1 8.3 %copy-start.14 = (bf16[2,640,768]{2,1,0:T(8,128)(2,1)S(1)}, bf16[2,640,768]{2,1,0:T(8,128)(2,1)}, u32[]{:S(2)}) copy-start(bf16[2,640,768]{2,1,0:T(8,128)(2,1)} %param.24) | copy-start | bytes 5898244
  314.4 10.0 %copy-start.25 = (f32[2,640]{1,0:T(2,128)}, f32[2,640]{1,0:T(2,128)S(1)}, u32[]{:S(2)}) copy-start(f32[2,640]{1,0:T(2,128)S(1)} %broadcast_multiply_fusion) | copy-start | bytes 15364
  314.4 10.0 %copy-start.27 = (f32[2,640]{1,0:T(2,128)}, f32[2,640]{1,0:T(2,128)S(1)}, u32[]{:S(2)}) copy-start(f32[2,640]{1,0:T(2,128)S(1)} %broadcast_multiply_fusion.1) | copy-start | bytes 15364
  319.6 4.7 copy-start.5
  334.6 4.5 copy-start.47
  343.8 1.3 copy-start
  399.8 1.7 copy-start.17
  399.8 2.1 copy-start.10
  399.8 2.7 copy-start.42
  401.5 3.5 copy-start.1
  402.5 1.3 copy-start.18
  402.9 1.6 copy-start.11
  402.9 2.1 copy-start.43
  405.0 1.3 copy-start
  461.0 1.7 copy-start.17
  461.0 2.1 copy-start.10
  461.0 2.7 copy-start.42
  462.7 3.5 copy-start.1
  463.7 1.3 copy-start.18
  464.0 1.6 copy-start.11
  464.0 2.1 copy-start.43
  466.4 5.8 copy-start.34
  473.3 4.3 copy-start.12
  473.3 4.3 copy-start.41
  473.3 4.3 copy-start.50
  477.6 2.8 copy-start.19
  575.5 3.8 copy-start.16
  575.5 3.8 copy-start.44
  579.3 2.1 copy-start.6
  579.3 3.3 copy-start.9
  579.3 3.3 copy-start.22
  579.4 3.3 copy-start.24
  579.4 3.3 copy-start.26
  579.4 3.3 copy-start.28
  579.4 3.3 copy-start.30
  582.7 3.5 copy-start.38
  582.7 3.5 copy-start.40
  586.2 3.2 copy-start.20

commit v2 on v1

--- a/solution.py
+++ b/solution.py
@@ -419,326 +419,486 @@
     )(*grads)
 
 
+F = jnp.float32
+BF = jnp.bfloat16
+NN = (((1,), (0,)), ((), ()))
+NT = (((1,), (1,)), ((), ()))
+TN = (((0,), (0,)), ((), ()))
+SMEM = pl.BlockSpec(memory_space=pltpu.SMEM)
 HEADS = 12
 HEAD_DIM = 64
-
-
+QUAD = 4 * HEAD_DIM
+scale = HEAD_DIM**-0.5
 norm_eps = 1e-05
 masked_score = -1000000000.0
-half_root = 0.7071067811865476
-density_scale = 0.3989422804014327
+LIMIT = 60 * 2**20
+
+
+def dot(left, right, dims):
+    return lax.dot_general(left, right, dims, preferred_element_type=F)
+
+
+def once(shape, index):
+    return pl.BlockSpec(shape, index, pipeline_mode=pl.Buffered(1))
+
+
+def key_bias(count):
+    row = lax.broadcasted_iota(jnp.int32, (128, 1), 0)
+    return jnp.where(row < count, 0.0, masked_score).astype(F)
+
+
+def masked(scores, text, bias):
+    return jnp.concatenate([scores[:text], scores[text:] + bias], axis=0)
+
+
+def head_lanes(h):
+    lane = lax.broadcasted_iota(jnp.int32, (1, 128), 1)
+    return (lane < HEAD_DIM) if h == 0 else (lane >= HEAD_DIM)
+
+
+def pair_forward(q2, k2, v2, text, bias):
+    vt = v2.T
+    outs, logs = [], []
+    for h in range(2):
+        qh = jnp.where(head_lanes(h), q2, BF(0))
+        scores = masked(dot(k2, qh, NT), text, bias)
+        top = jnp.max(scores, axis=0, keepdims=True)
+        expo = jnp.exp(scores - top)
+        total = jnp.sum(expo, axis=0, keepdims=True)
+        outs.append(dot(vt[HEAD_DIM * h : HEAD_DIM * (h + 1)], expo.astype(BF), NN) * (1.0 / total))
+        logs.append(top + jnp.log(total))
+    return jnp.concatenate(outs, axis=0).T.astype(BF), logs
+
+
+def pair_backward(q2, k2, v2, o2, do2, logs, text, bias):
+    prod = (do2.astype(F) * o2.astype(F)).T
+    kt = (k2 * BF(scale)).T
+    dq, dk, dv = [], [], []
+    for h in range(2):
+        rows = slice(HEAD_DIM * h, HEAD_DIM * (h + 1))
+        qh = jnp.where(head_lanes(h), q2, BF(0))
+        doh = jnp.where(head_lanes(h), do2, BF(0))
+        delta = jnp.sum(prod[rows], axis=0, keepdims=True)
+        probs = jnp.exp(masked(dot(k2, qh, NT), text, bias) - logs[h])
+        grads = (probs * (dot(v2, doh, NT) - delta)).astype(BF)
+        dv.append(dot(probs.astype(BF), do2, NN))
+        dk.append(dot(grads, q2, NN))
+        dq.append(dot(kt[rows], grads, NN))
+    first = head_lanes(0)
+    return (
+        jnp.concatenate(dq, axis=0).T.astype(BF),
+        jnp.where(first, dk[0], dk[1]).astype(BF),
+        jnp.where(first, dv[0], dv[1]).astype(BF),
+    )
+
+
+def member_of(align, axis, segs):
+    shape = (segs, align.shape[1]) if axis == 0 else (align.shape[0], segs)
+    return (align == lax.broadcasted_iota(jnp.int32, shape, axis)).astype(F)
+
+
+def forward_body(b, j, len_ref, tok_ref, al_ref, w_ref, bias_ref, outs, low_s):
+    base_ref, low_ref, q_ref, k_ref, v_ref, att_ref, lse_ref = outs
+    text, width = al_ref.shape[2], tok_ref.shape[2]
+    segs = tok_ref.shape[1] - text
+
+    @pl.when(j == 0)
+    def _():
+        member = member_of(al_ref[0], 0, segs)
+        counts = jnp.maximum(jnp.sum(member, axis=1, keepdims=True), 1.0)
+        tok = tok_ref[0]
+        pooled = dot(member.astype(BF), tok[:text], NN) / counts
+        seg_base = tok[text:].astype(F) + pooled
+        base_ref[0, :text] = tok[:text].astype(F)
+        base_ref[0, text:] = seg_base
+        low_ref[0, :text] = tok[:text]
+        low_ref[0, text:] = seg_base.astype(BF)
+        low_s[:text] = tok[:text]
+        low_s[text:] = seg_base.astype(BF)
+
+    low = low_s[...]
+    parts = []
+    for i, ref in enumerate((q_ref, k_ref, v_ref)):
+        at = i * width + j * QUAD
+        rows = dot(low, w_ref[:, pl.ds(pl.multiple_of(at, QUAD), QUAD)], NN)
+        if i != 1:
+            rows = rows + bias_ref[i // 2 : i // 2 + 1, pl.ds(pl.multiple_of(j * QUAD, QUAD), QUAD)]
+        rows = rows.astype(BF)
+        if i == 0:
+            rows = rows * BF(scale)
+        ref[0] = rows
+        parts.append(rows)
+    bias = key_bias(len_ref[b])
+    for pr in range(2):
+        cols = slice(128 * pr, 128 * pr + 128)
+        out, logs = pair_forward(parts[0][:, cols], parts[1][:, cols], parts[2][:, cols], text, bias)
+        att_ref[0, :, cols] = out
+        for h in range(2):
+            lse_ref[0, 0, 2 * pr + h : 2 * pr + h + 1, :] = logs[h]
+
+
+def forward_kernel(len_ref, tok_ref, al_ref, w_ref, bias_ref, *rest):
+    forward_body(pl.program_id(0), pl.program_id(1), len_ref, tok_ref, al_ref, w_ref, bias_ref, rest[:7], rest[7])
+
+
+def forward_attention(seg_lengths, tokens, alignment, w0, biases):
+    docs, slots, width = tokens.shape
+    text = alignment.shape[1]
+    quads = width // QUAD
+    doc = pl.BlockSpec((1, slots, width), lambda b, j: (b, 0, 0))
+    quad = pl.BlockSpec((1, slots, QUAD), lambda b, j: (b, 0, j))
+    wide = jax.ShapeDtypeStruct((docs, slots, width), BF)
+    return pl.pallas_call(
+        forward_kernel,
+        grid=(docs, quads),
+        in_specs=[
+            SMEM,
+            doc,
+            pl.BlockSpec((1, 1, text), lambda b, j: (b, 0, 0)),
+            once(w0.shape, lambda b, j: (0, 0)),
+            once(biases.shape, lambda b, j: (0, 0)),
+        ],
+        out_specs=[doc, doc, quad, quad, quad, quad, pl.BlockSpec((1, 1, 8, slots), lambda b, j: (b, j, 0, 0))],
+        out_shape=[
+            jax.ShapeDtypeStruct((docs, slots, width), F),
+            wide,
+            wide,
+            wide,
+            wide,
+            wide,
+            jax.ShapeDtypeStruct((docs, quads, 8, slots), F),
+        ],
+        scratch_shapes=[pltpu.VMEM((slots, width), BF)],
+        compiler_params=pltpu.CompilerParams(vmem_limit_bytes=LIMIT),
+    )(seg_lengths, tokens, alignment[:, None, :], w0, biases)
+
+
+def normal_parts(pre):
+    size = jnp.abs(pre)
+    dens = jnp.exp(pre * pre * -0.5)
+    t = 1.0 / (1.0 + (0.3275911 * 0.7071067811865476) * size)
+    poly = t * (
+        0.5 * 0.254829592
+        + t * (0.5 * -0.284496736 + t * (0.5 * 1.421413741 + t * (0.5 * -1.453152027 + t * (0.5 * 1.061405429))))
+    )
+    tail = poly * dens
+    return jnp.where(pre >= 0, 1.0 - tail, tail), dens * 0.3989422804014327
 
 
 def norm_parts(values_in):
-    centred = values_in - jnp.mean(values_in, axis=-1, keepdims=True)
+    mean = jnp.mean(values_in, axis=-1, keepdims=True)
+    centred = values_in - mean
     inverse = lax.rsqrt(jnp.mean(centred * centred, axis=-1, keepdims=True) + norm_eps)
-    return (centred * inverse, inverse)
-
-
-def norm_back(grad_hat, normed_hat, inverse):
+    return centred * inverse, inverse
+
+
+def norm_back(grad_hat, hat, inverse):
     return inverse * (
         grad_hat
         - jnp.mean(grad_hat, axis=-1, keepdims=True)
-        - normed_hat * jnp.mean(grad_hat * normed_hat, axis=-1, keepdims=True)
+        - hat * jnp.mean(grad_hat * hat, axis=-1, keepdims=True)
     )
 
 
-def gelu_slope(pre_act):
-    return (
-        0.5 * (1.0 + lax.erf(pre_act * half_root))
-        + pre_act * jnp.exp(-0.5 * pre_act * pre_act) * density_scale
-    )
-
-
-def apply_weight(left_rows, weight_mat):
-    return jnp.einsum("bsd,de->bse", left_rows, weight_mat, preferred_element_type=jnp.float32)
-
-
-def apply_transposed(left_rows, weight_mat):
-    return jnp.einsum("bse,de->bsd", left_rows, weight_mat, preferred_element_type=jnp.float32)
-
-
-def weight_grad(left_rows, right_rows):
-    return jnp.einsum("bsd,bse->de", left_rows, right_rows, preferred_element_type=jnp.float32)
-
-
-def column_sum(rows_low):
-    return jnp.sum(rows_low, axis=(0, 1), dtype=jnp.float32)
-
-
-def split_heads(rows_in):
-    return rows_in.reshape(rows_in.shape[0], HEADS, HEAD_DIM)
-
-
-def score_block(query_rows, key_rows, valid_keys):
-    scores = jnp.einsum(
-        "qhd,khd->hqk",
-        split_heads(query_rows),
-        split_heads(key_rows),
-        preferred_element_type=jnp.float32,
-    ) * HEAD_DIM ** (-0.5)
-    return jnp.where(valid_keys[None, None, :], scores, masked_score)
-
-
-def attend_forward(packed):
-    query_rows, key_rows, value_rows, valid_keys = packed
-    scores = score_block(query_rows, key_rows, valid_keys)
-    row_top = jnp.max(scores, axis=-1, keepdims=True)
-    expo = jnp.exp(scores - row_top)
-    total = jnp.sum(expo, axis=-1, keepdims=True)
-    probs_low = (expo / total).astype(jnp.bfloat16)
-    mixed = jnp.einsum(
-        "hqk,khd->qhd", probs_low, split_heads(value_rows), preferred_element_type=jnp.float32
-    )
-    return (mixed.reshape(query_rows.shape[0], HEADS * HEAD_DIM), row_top + jnp.log(total))
-
-
-def attend_backward(packed):
-    query_rows, key_rows, value_rows, valid_keys, log_total, grad_mixed = packed
-    slot_count = query_rows.shape[0]
-    scores = score_block(query_rows, key_rows, valid_keys)
-    probs = jnp.exp(scores - log_total)
-    grad_heads = split_heads(grad_mixed)
-    grad_probs = jnp.einsum(
-        "qhd,khd->hqk", grad_heads, split_heads(value_rows), preferred_element_type=jnp.float32
-    )
-    grad_value = jnp.einsum(
-        "hqk,qhd->khd", probs.astype(jnp.bfloat16), grad_heads, preferred_element_type=jnp.float32
-    )
-    grad_scores = probs * (grad_probs - jnp.sum(probs * grad_probs, axis=-1, keepdims=True))
-    grad_scores_low = grad_scores.astype(jnp.bfloat16)
-    grad_query = jnp.einsum(
-        "hqk,khd->qhd", grad_scores_low, split_heads(key_rows), preferred_element_type=jnp.float32
-    ) * HEAD_DIM ** (-0.5)
-    grad_key = jnp.einsum(
-        "hqk,qhd->khd", grad_scores_low, split_heads(query_rows), preferred_element_type=jnp.float32
-    ) * HEAD_DIM ** (-0.5)
-    width = HEADS * HEAD_DIM
-    return (
-        grad_query.reshape(slot_count, width).astype(jnp.bfloat16),
-        grad_key.reshape(slot_count, width).astype(jnp.bfloat16),
-        grad_value.reshape(slot_count, width).astype(jnp.bfloat16),
-    )
+def col_sum(values):
+    return jnp.sum(values, axis=0, keepdims=True)
+
+
+def mlp_kernel(
+    tiles, ff_cut, att_ref, base_ref, cot_ref, w1_ref, w2_ref, vec_ref, ib_ref,
+    enc_ref, gf_ref, ga_ref, g1_ref, g2_ref, gv_ref, gib_ref,
+    att_s, norm_s, act_s, slope_s, gmlp_s, gpre_s, gbr_s,
+):
+    i = pl.program_id(0)
+    rows, width = att_ref.shape
+    ff = ib_ref.shape[1]
+    chunks = ff // ff_cut
+
+    @pl.when(i == 0)
+    def _():
+        gv_ref[...] = jnp.zeros_like(gv_ref)
+        gib_ref[...] = jnp.zeros_like(gib_ref)
+
+    @pl.when(i < tiles)
+    def _():
+        at = pl.ds(pl.multiple_of(i * rows, rows), rows)
+        vec = lambda k: vec_ref[k : k + 1, :]
+        att = att_ref[...]
+        att_s[at] = att
+        first = base_ref[...] + dot(att, w1_ref[:, :width], NN) + vec(2)
+        first_hat, first_inv = norm_parts(first)
+        normed = first_hat * vec(3) + vec(4)
+        norm_low = normed.astype(BF)
+        norm_s[at] = norm_low
+        second = normed + vec(5)
+        for c in range(chunks):
+            cols = slice(c * ff_cut, (c + 1) * ff_cut)
+            pre = dot(norm_low, w1_ref[:, width + c * ff_cut : width + (c + 1) * ff_cut], NN) + ib_ref[:, cols]
+            phi, dens = normal_parts(pre)
+            act = (pre * phi).astype(BF)
+            act_s[at, cols] = act
+            slope_s[:, cols] = (phi + pre * dens).astype(BF)
+            second = second + dot(act, w2_ref[cols, :], NN)
+        hat, inv = norm_parts(second)
+        enc_ref[...] = (hat * vec(6) + vec(7)).astype(BF)
+        grad_y = cot_ref[...].astype(F)
+        grad_second = norm_back(grad_y * vec(6), hat, inv)
+        gmlp = grad_second.astype(BF)
+        gmlp_s[at] = gmlp
+        grad_normed = grad_second
+        for c in range(chunks):
+            cols = slice(c * ff_cut, (c + 1) * ff_cut)
+            gact = dot(gmlp, w2_ref[cols, :], NT)
+            gpre = (gact * slope_s[:, cols].astype(F)).astype(BF)
+            gpre_s[at, cols] = gpre
+            gib_ref[:, cols] += col_sum(gpre.astype(F))
+            grad_normed = grad_normed + dot(gpre, w1_ref[:, width + c * ff_cut : width + (c + 1) * ff_cut], NT)
+        grad_first = norm_back(grad_normed * vec(3), first_hat, first_inv)
+        gf_ref[...] = grad_first
+        gbr = grad_first.astype(BF)
+        gbr_s[at] = gbr
+        ga_ref[...] = dot(gbr, w1_ref[:, :width], NT).astype(BF)
+        gv_ref[2:3] += col_sum(gbr.astype(F))
+        gv_ref[3:4] += col_sum(grad_normed * first_hat)
+        gv_ref[4:5] += col_sum(grad_normed)
+        gv_ref[5:6] += col_sum(gmlp.astype(F))
+        gv_ref[6:7] += col_sum(grad_y * hat)
+        gv_ref[7:8] += col_sum(grad_y)
+
+    @pl.when((i >= tiles) & (i < tiles + 4))
+    def _():
+        cols = pl.ds(pl.multiple_of((i - tiles) * width, width), width)
+        g2_ref[...] = dot(act_s[:, cols], gmlp_s[...], TN).astype(BF)
+
+    @pl.when((i >= tiles + 4) & (i < tiles + 8))
+    def _():
+        cols = pl.ds(pl.multiple_of((i - tiles - 4) * width, width), width)
+        g1_ref[...] = dot(norm_s[...], gpre_s[:, cols], TN).astype(BF)
+
+    @pl.when(i == tiles + 8)
+    def _():
+        g1_ref[...] = dot(att_s[...], gbr_s[...], TN).astype(BF)
+
+
+def mlp_both(attended, base, cotangent, w1, w2, vec, inner_bias, rows=320, ff_cut=768):
+    total, width = attended.shape
+    ff = inner_bias.shape[1]
+    tiles = total // rows
+    tile = pl.BlockSpec((rows, width), lambda i: (jnp.minimum(i, tiles - 1), 0))
+    whole = lambda shape: once(shape, lambda i: (0, 0))
+    return pl.pallas_call(
+        functools.partial(mlp_kernel, tiles, ff_cut),
+        grid=(tiles + 9,),
+        in_specs=[tile, tile, tile, whole(w1.shape), whole(w2.shape), whole(vec.shape), whole(inner_bias.shape)],
+        out_specs=[
+            tile,
+            tile,
+            tile,
+            pl.BlockSpec((width, width), lambda i: (0, jnp.where(i == tiles + 8, 0, jnp.clip(i - tiles - 4, 0, 3) + 1))),
+            pl.BlockSpec((width, width), lambda i: (jnp.clip(i - tiles, 0, 3), 0)),
+            whole((8, width)),
+            whole((1, ff)),
+        ],
+        out_shape=[
+            jax.ShapeDtypeStruct((total, width), BF),
+            jax.ShapeDtypeStruct((total, width), F),
+            jax.ShapeDtypeStruct((total, width), BF),
+            jax.ShapeDtypeStruct((width, width + ff), BF),
+            jax.ShapeDtypeStruct((ff, width), BF),
+            jax.ShapeDtypeStruct((8, width), F),
+            jax.ShapeDtypeStruct((1, ff), F),
+        ],
+        scratch_shapes=[
+            pltpu.VMEM((total, width), BF),
+            pltpu.VMEM((total, width), BF),
+            pltpu.VMEM((total, ff), BF),
+            pltpu.VMEM((rows, ff), BF),
+            pltpu.VMEM((total, width), BF),
+            pltpu.VMEM((total, ff), BF),
+            pltpu.VMEM((total, width), BF),
+        ],
+        compiler_params=pltpu.CompilerParams(vmem_limit_bytes=LIMIT),
+    )(attended, base, cotangent, w1, w2, vec, inner_bias)
+
+
+def backward_body(j, b, refs, outs, scratch):
+    len_ref, al_ref, q_ref, k_ref, v_ref, o_ref, do_ref, lse_ref, low_ref, gf_ref, w_ref, vec_ref = refs
+    gq_ref, gk_ref, gv_ref, gvec_ref, gt_ref = outs
+    gbase_s, acc_s, vsum_s = scratch
+    text, width = al_ref.shape[1], low_ref.shape[2]
+    segs = low_ref.shape[1] - text
+    quads = width // QUAD
+
+    bias = key_bias(len_ref[b])
+    parts = [[], [], []]
+    for pr in range(2):
+        cols = slice(128 * pr, 128 * pr + 128)
+        logs = [lse_ref[0, 0, 2 * pr + h : 2 * pr + h + 1, :] for h in range(2)]
+        got = pair_backward(
+            q_ref[0, :, cols], k_ref[0, :, cols], v_ref[0, :, cols], o_ref[0, :, cols], do_ref[0, :, cols], logs, text, bias
+        )
+        for i in range(3):
+            parts[i].append(got[i])
+    quad_grads = [jnp.concatenate(p, axis=1) for p in parts]
+    cols = pl.ds(pl.multiple_of(j * QUAD, QUAD), QUAD)
+
+    @pl.when(j == 0)
+    def _():
+        gbase_s[b] = gf_ref[0]
+
+    gbase = gbase_s[b]
+    for i in range(3):
+        at = pl.ds(pl.multiple_of(i * width + j * QUAD, QUAD), QUAD)
+        gbase = gbase + dot(quad_grads[i], w_ref[:, at], NT)
+    gbase_s[b] = gbase
+
+    low = low_ref[0]
+    weight = [dot(low, g, TN) for g in quad_grads]
+    sums = [col_sum(quad_grads[0].astype(F)), col_sum(quad_grads[2].astype(F))]
+
+    @pl.when(b == 0)
+    def _():
+        for i in range(3):
+            acc_s[i] = weight[i]
+        for i in range(2):
+            vsum_s[i : i + 1, cols] = sums[i]
+
+    @pl.when(b == 1)
+    def _():
+        for i, ref in enumerate((gq_ref, gk_ref, gv_ref)):
+            ref[...] = (acc_s[i] + weight[i]).astype(BF)
+        for i in range(2):
+            vsum_s[i : i + 1, cols] += sums[i]
+
+    @pl.when(j == quads - 1)
+    def _():
+        member = member_of(al_ref[0], 1, segs)
+        counts = jnp.maximum(jnp.sum(member, axis=0, keepdims=True), 1.0)
+        share = gbase[text:] / counts.T
+        high = share.astype(BF)
+        rest = (share - high.astype(F)).astype(BF)
+        sel = member.astype(BF)
+        spread = dot(sel, high, NN) + dot(sel, rest, NN)
+        gt_ref[0, :text] = (gbase[:text] + spread).astype(BF)
+        gt_ref[0, text:] = gbase[text:].astype(BF)
+
+    @pl.when((j == quads - 1) & (b == 1))
+    def _():
+        lane = lax.broadcasted_iota(jnp.int32, (1, 128), 1)
+        cols2 = jnp.where(lane < 2, jnp.concatenate([vsum_s[...], jnp.zeros((120, width), F)], axis=0).T, 0.0)
+        gvec_ref[...] = (cols2 + vec_ref[...]).astype(BF)
+
+
+def backward_kernel(*refs):
+    backward_body(pl.program_id(0), pl.program_id(1), refs[:12], refs[12:17], refs[17:])
+
+
+def backward_attention(seg_lengths, alignment, q, k, v, att, gatt, lse, low, gfirst, w0, vec):
+    docs, slots, width = low.shape
+    text = alignment.shape[1]
+    quads = width // QUAD
+    quad = pl.BlockSpec((1, slots, QUAD), lambda j, b: (b, 0, j))
+    doc = pl.BlockSpec((1, slots, width), lambda j, b: (b, 0, 0))
+    wide = jax.ShapeDtypeStruct((width, width), BF)
+    col = pl.BlockSpec((width, QUAD), lambda j, b: (0, j))
+    return pl.pallas_call(
+        backward_kernel,
+        grid=(quads, docs),
+        in_specs=[
+            SMEM,
+            pl.BlockSpec((1, text, 1), lambda j, b: (b, 0, 0)),
+            quad,
+            quad,
+            quad,
+            quad,
+            quad,
+            pl.BlockSpec((1, 1, 8, slots), lambda j, b: (b, j, 0, 0)),
+            doc,
+            pl.BlockSpec((1, slots, width), lambda j, b: (jnp.where(j == 0, b, 1), 0, 0)),
+            once(w0.shape, lambda j, b: (0, 0)),
+            once(vec.shape, lambda j, b: (0, 0)),
+        ],
+        out_specs=[
+            col,
+            col,
+            col,
+            once((width, 128), lambda j, b: (0, 0)),
+            pl.BlockSpec((1, slots, width), lambda j, b: (jnp.where(j == quads - 1, b, 0), 0, 0)),
+        ],
+        out_shape=[wide, wide, wide, jax.ShapeDtypeStruct((width, 128), BF), jax.ShapeDtypeStruct((docs, slots, width), BF)],
+        scratch_shapes=[
+            pltpu.VMEM((docs, slots, width), F),
+            pltpu.VMEM((3, width, QUAD), F),
+            pltpu.VMEM((8, width), F),
+        ],
+        compiler_params=pltpu.CompilerParams(vmem_limit_bytes=LIMIT),
+    )(seg_lengths, alignment[:, :, None], q, k, v, att, gatt, lse, low, gfirst, w0, vec)
 
 
 def own_kernels(shard_rows):
     return lax.axis_size("dp") == PLANES and lax.axis_size("fsdp") == 8 and shard_rows == 24
 
 
-def gather_params(qkv, rest, outer, vectors, inner_bias):
-    rows = outer.shape[0] // 4
-    columns = [v[:, None] for v in vectors] + [inner_bias.reshape(rows, 4)]
-    pad = jnp.zeros((rows, 256 - len(vectors) - 4), jnp.bfloat16)
-    s0 = jnp.concatenate(list(qkv) + columns + [pad], axis=1)
-    s1 = jnp.concatenate(list(rest), axis=1)
-    if own_kernels(rows):
-        w0, w1, w2 = gather_all(s0.astype(jnp.float32), s1.astype(jnp.float32), outer)
+def shards(
+    tokens, cotangent, seg_lengths, alignment, query_weight, query_bias, key_weight, value_weight, value_bias,
+    out_weight, out_bias, first_gain, first_shift, inner_weight, inner_bias, outer_weight, outer_bias, second_gain,
+    second_shift,
+):
+    docs, slots, width = tokens.shape
+    rows = query_weight.shape[0]
+    ff = inner_weight.shape[1]
+    every = ("dp", "fsdp")
+    own = own_kernels(rows)
+    vectors = (query_bias, value_bias, out_bias, first_gain, first_shift, outer_bias, second_gain, second_shift)
+    columns = [t[:, None] for t in vectors] + [inner_bias.reshape(rows, 4)]
+    pad = jnp.zeros((rows, 256 - 12), BF)
+    s0 = jnp.concatenate([query_weight, key_weight, value_weight] + columns + [pad], axis=1)
+    s1 = jnp.concatenate([out_weight, inner_weight], axis=1)
+    if own:
+        w0, w1, w2 = gather_all(s0.astype(F), s1.astype(F), outer_weight)
     else:
-        w0, w1, w2 = (lax.all_gather(s, ("dp", "fsdp"), axis=0, tiled=True) for s in (s0, s1, outer))
-    width = outer.shape[1]
+        w0, w1, w2 = (lax.all_gather(s, every, axis=0, tiled=True) for s in (s0, s1, outer_weight))
     w0, w1, w2 = w0.reshape(width, -1), w1.reshape(width, -1), w2.reshape(-1, width)
-    vec = w0[:, 3 * width :]
-    return (
-        *(w0[:, i * width : (i + 1) * width] for i in range(3)),
-        w1[:, :width],
-        w1[:, width:],
-        w2,
-        *(vec[:, i] for i in range(8)),
-        vec[:, 8:12].reshape(-1),
+    vec = w0[:, 3 * width : 3 * width + 12].astype(F)
+    rows_vec = vec[:, :8].T
+    inner_row = vec[:, 8:12].reshape(1, ff)
+
+    base, low, q, k, v, att, lse = forward_attention(seg_lengths, tokens, alignment, w0, rows_vec)
+    flat = lambda t: t.reshape(docs * slots, width)
+    encoded, gfirst, gatt, g1, g2, gvec, ginner = mlp_both(
+        flat(att), flat(base), flat(cotangent), w1, w2, rows_vec, inner_row
     )
-
-
-def scatter_grads(qkv, rest, outer, vectors, inner_bias):
-    width = outer.shape[1]
-    columns = [v[:, None] for v in vectors] + [inner_bias.reshape(width, 4)]
-    pad = jnp.zeros((width, 256 - len(vectors) - 4), jnp.float32)
-    g0 = jnp.concatenate(list(qkv) + columns + [pad], axis=1)
-    g1 = jnp.concatenate(list(rest), axis=1)
-    devices = lax.axis_size("dp") * lax.axis_size("fsdp")
-    if own_kernels(width // devices):
-        low = jnp.bfloat16
+    whole = lambda t: t.reshape(docs, slots, width)
+    vec_cols = jnp.concatenate([gvec.T, ginner.reshape(width, 4), jnp.zeros((width, 116), F)], axis=1)
+    gq, gk, gv, gcols, grad_tokens = backward_attention(
+        seg_lengths, alignment, q, k, v, att, whole(gatt), lse, low, whole(gfirst), w0, vec_cols
+    )
+    g0 = jnp.concatenate([gq, gk, gv, gcols, jnp.zeros((width, 128), BF)], axis=1)
+    if own:
         o2, o1, o0 = scatter_all(
-            (
-                outer.astype(low).reshape(CHIPS, 2, 96, width),
-                g1.astype(low).reshape(CHIPS, 48, -1),
-                g0.astype(low).reshape(CHIPS, 48, -1),
-            ),
-            1,
+            (g2.reshape(CHIPS, 2, 96, width), g1.reshape(CHIPS, 48, -1), g0.reshape(CHIPS, 48, -1)), 1
         )
     else:
-        o2, o1, o0 = (
-            lax.psum_scatter(g, ("dp", "fsdp"), scatter_dimension=0, tiled=True) for g in (outer, g1, g0)
-        )
-    vec = o0[:, 3 * width :]
+        o2, o1, o0 = (lax.psum_scatter(g.astype(F), every, scatter_dimension=0, tiled=True) for g in (g2, g1, g0))
+    sums = o0[:, 3 * width :]
     return (
+        whole(encoded),
+        grad_tokens,
         o0[:, :width],
-        vec[:, 0],
+        sums[:, 0],
         o0[:, width : 2 * width],
         o0[:, 2 * width : 3 * width],
-        vec[:, 1],
+        sums[:, 1],
         o1[:, :width],
-        vec[:, 2],
-        vec[:, 3],
-        vec[:, 4],
+        sums[:, 2],
+        sums[:, 3],
+        sums[:, 4],
         o1[:, width:],
-        vec[:, 8:12].reshape(-1),
+        sums[:, 8:12].reshape(-1),
         o2,
-        vec[:, 5],
-        vec[:, 6],
-        vec[:, 7],
-    )
-
-
-def shards(
-    tokens,
-    cotangent,
-    seg_lengths,
-    alignment,
-    query_weight,
-    query_bias,
-    key_weight,
-    value_weight,
-    value_bias,
-    out_weight,
-    out_bias,
-    first_gain,
-    first_shift,
-    inner_weight,
-    inner_bias,
-    outer_weight,
-    outer_bias,
-    second_gain,
-    second_shift,
-):
-    w_all = gather_params(
-        (query_weight, key_weight, value_weight), (out_weight, inner_weight), outer_weight,
-        (query_bias, value_bias, out_bias, first_gain, first_shift, outer_bias, second_gain, second_shift),
-        inner_bias,
-    )
-    (
-        w_query,
-        w_key,
-        w_value,
-        w_out,
-        w_inner,
-        w_outer,
-        b_query,
-        b_value,
-        b_out,
-        g_first,
-        s_first,
-        b_outer,
-        g_second,
-        s_second,
-        b_inner,
-    ) = w_all
-    back_query, back_key, back_value, back_out = w_query, w_key, w_value, w_out
-    back_first, back_inner, back_outer, back_second = g_first, w_inner, w_outer, g_second
-    text_count = alignment.shape[1]
-    slot_count = tokens.shape[1]
-    seg_count = slot_count - text_count
-    member = alignment[:, None, :] == jnp.arange(seg_count, dtype=jnp.int32)[None, :, None]
-    member_float = member.astype(jnp.float32)
-    counts = jnp.maximum(jnp.sum(member_float, axis=-1), 1.0)
-    pooled = (
-        jnp.einsum(
-            "bst,btd->bsd",
-            member.astype(jnp.bfloat16),
-            tokens[:, :text_count],
-            preferred_element_type=jnp.float32,
-        )
-        / counts[:, :, None]
-    )
-    text_zeros = jnp.zeros((tokens.shape[0], text_count, tokens.shape[2]), jnp.float32)
-    base = tokens.astype(jnp.float32) + jnp.concatenate([text_zeros, pooled], axis=1)
-    valid_keys = (
-        jnp.arange(slot_count, dtype=jnp.int32)[None, :] < text_count + seg_lengths[:, None]
-    )
-    base_low = base.astype(jnp.bfloat16)
-    query_rows = (apply_weight(base_low, w_query) + b_query).astype(jnp.bfloat16)
-    key_rows = apply_weight(base_low, w_key).astype(jnp.bfloat16)
-    value_rows = (apply_weight(base_low, w_value) + b_value).astype(jnp.bfloat16)
-    attended, log_total = lax.map(attend_forward, (query_rows, key_rows, value_rows, valid_keys))
-    attended_low = attended.astype(jnp.bfloat16)
-    first_sum = base + apply_weight(attended_low, w_out) + b_out
-    first_hat, first_inv = norm_parts(first_sum)
-    normed = first_hat * g_first + s_first
-    normed_low = normed.astype(jnp.bfloat16)
-    pre_act = apply_weight(normed_low, w_inner) + b_inner
-    act_low = jax.nn.gelu(pre_act, approximate=False).astype(jnp.bfloat16)
-    second_sum = normed + apply_weight(act_low, w_outer) + b_outer
-    second_hat, second_inv = norm_parts(second_sum)
-    encoded = (second_hat * g_second + s_second).astype(jnp.bfloat16)
-    grad_y = cotangent.astype(jnp.float32)
-    grad_second_gain = jnp.sum(grad_y * second_hat, axis=(0, 1))
-    grad_second_shift = jnp.sum(grad_y, axis=(0, 1))
-    grad_second = norm_back(grad_y * back_second, second_hat, second_inv)
-    grad_mlp_low = grad_second.astype(jnp.bfloat16)
-    grad_outer_weight = weight_grad(act_low, grad_mlp_low)
-    grad_outer_bias = column_sum(grad_mlp_low)
-    grad_pre_low = (apply_transposed(grad_mlp_low, back_outer) * gelu_slope(pre_act)).astype(
-        jnp.bfloat16
-    )
-    grad_inner_weight = weight_grad(normed_low, grad_pre_low)
-    grad_inner_bias = column_sum(grad_pre_low)
-    grad_normed = grad_second + apply_transposed(grad_pre_low, back_inner)
-    grad_first_gain = jnp.sum(grad_normed * first_hat, axis=(0, 1))
-    grad_first_shift = jnp.sum(grad_normed, axis=(0, 1))
-    grad_first = norm_back(grad_normed * back_first, first_hat, first_inv)
-    grad_branch_low = grad_first.astype(jnp.bfloat16)
-    grad_out_weight = weight_grad(attended_low, grad_branch_low)
-    grad_out_bias = column_sum(grad_branch_low)
-    grad_attended_low = apply_transposed(grad_branch_low, back_out).astype(jnp.bfloat16)
-    grad_query, grad_key, grad_value = lax.map(
-        attend_backward,
-        (query_rows, key_rows, value_rows, valid_keys, log_total, grad_attended_low),
-    )
-    grad_query_weight = weight_grad(base_low, grad_query)
-    grad_query_bias = column_sum(grad_query)
-    grad_key_weight = weight_grad(base_low, grad_key)
-    grad_value_weight = weight_grad(base_low, grad_value)
-    grad_value_bias = column_sum(grad_value)
-    grad_base = (
-        grad_first
-        + apply_transposed(grad_query, back_query)
-        + apply_transposed(grad_key, back_key)
-        + apply_transposed(grad_value, back_value)
-    )
-    spread_back = jnp.einsum(
-        "bst,bsd->btd",
-        member_float,
-        grad_base[:, text_count:] / counts[:, :, None],
-        precision=lax.Precision.HIGHEST,
-    )
-    grad_tokens = jnp.concatenate(
-        [grad_base[:, :text_count] + spread_back, grad_base[:, text_count:]], axis=1
-    ).astype(jnp.bfloat16)
-    owned = scatter_grads(
-        (grad_query_weight, grad_key_weight, grad_value_weight),
-        (grad_out_weight, grad_inner_weight),
-        grad_outer_weight,
-        (grad_query_bias, grad_value_bias, grad_out_bias, grad_first_gain, grad_first_shift, grad_outer_bias,
-         grad_second_gain, grad_second_shift),
-        grad_inner_bias,
-    )
-    return (
-        encoded,
-        grad_tokens,
-        owned[0],
-        owned[1],
-        owned[2],
-        owned[3],
-        owned[4],
-        owned[5],
-        owned[6],
-        owned[7],
-        owned[8],
-        owned[9],
-        owned[10],
-        owned[11],
-        owned[12],
-        owned[13],
-        owned[14],
+        sums[:, 5],
+        sums[:, 6],
+        sums[:, 7],
     )
 
 

time: 599 us -> 332 us (0.55); the launches traced: 590 us -> 331 us
  matrix products: 240 us -> 0 us
  Pallas kernels: 155 us -> 296 us
  other arithmetic: 118 us -> 5.64 us
  local copies, waits for them, and re-layouts: 74.2 us -> 28.3 us
    dot_general x34 -> x0, matrix products: 240 us -> none  [the longest x6 50.4 us: apply_weight(): jnp.einsum('bsd,de->bse', left_rows, weight_mat, preferred_element_type=j...]
    pallas_call x0 -> x3, Pallas kernels: none -> 141 us  [the longest x1 69.1 us: mlp_both(): pl.pallas_call(functools.partial(mlp_kernel, tiles, ff_cut), grid=(tiles...]
    convert_element_type x7 -> x3, other arithmetic: 73.3 us -> 3.34 us  [the longest x2 2.39 us: shards(): w0, w1, w2 = gather_all(s0.astype(F), s1.astype(F), outer_weight)]
    reduce_sum x10 -> x0, other arithmetic: 39.2 us -> none  [the longest x2 21.2 us: attend_forward(): total = jnp.sum(expo, axis=-1, keepdims=True)]
    while x43 -> x0, local copies, waits for them, and re-layouts: 19.8 us -> none
    concatenate x11 -> x3, local copies, waits for them, and re-layouts: 18 us -> 1.02 us  [the longest x1 0.9 us: shards(): jnp.concatenate([query_weight, key_weight, value_weight] + columns + [pad...]
    dynamic_slice x18 -> x0, local copies, waits for them, and re-layouts: 12.8 us -> none  [shards(): lax.map(attend_forward, (query_rows, key_rows, value_rows, valid_keys))]
where the time goes in v2:
time: 332 us; the launch traced here: 331 us
  Pallas kernels  296 us (89%)
  local copies, waits for them, and re-layouts  28.3 us (9%)
  other arithmetic  5.64 us (2%)
    pallas_call x1, Pallas kernels, gather_all(): pl.pallas_call(gather_kernel, out_shape=(jax.ShapeDtypeStruct((CHIPS, 48,...  78.5 us
    pallas_call x1, Pallas kernels, scatter_all(): pl.pallas_call(functools.partial(scatter_kernel, tuple(kinds)), out_shape...  76.5 us
    pallas_call x1, Pallas kernels, mlp_both(): pl.pallas_call(functools.partial(mlp_kernel, tiles, ff_cut), grid=(tiles...  69.1 us
    pallas_call x1, Pallas kernels, backward_attention(): pl.pallas_call(backward_kernel, grid=(quads, docs), in_specs=[SMEM, pl.Bl...  46.6 us
    pallas_call x1, Pallas kernels, forward_attention(): pl.pallas_call(forward_kernel, grid=(docs, quads), in_specs=[SMEM, doc, p...  25.4 us

profile of v2, /device:TPU:0, one launch (start us, length us, event | category | flops | bytes accessed | tf_op | source)
XLA Modules:
  0.0 330.8 jit_solution(8382640247173047982)
XLA Ops:
  0.7 0.7 copy.47
  1.4 0.7 copy.48
  2.1 0.7 copy.49
  2.9 0.7 copy.50
  3.6 0.7 copy.51
  4.4 0.7 copy.52
  5.1 0.7 copy.53
  5.9 0.7 copy.54
  6.6 0.7 reshape.82
  7.4 0.9 concatenate.12
  8.3 0.7 convert_element_type.9.s0
  9.0 1.7 maximum_convert_fusion.s1
  10.7 78.5 %shard_map.314 = (bf16[16,48,2560]{2,1,0:T(8,128)(2,1)}, bf16[16,48,3840]{2,1,0:T(8,128)(2,1)}, bf16[16,2,96,768]{3,2,1,0:T(8,128)(2,1)}) custom-call(f32[24,2560]{1,0:T(8,128)} %convert_element_type.9.s0, f32[24,3840]{1,0:T(8,128)} %maximum_convert_fusion.s1, bf16[96,768]{1,0:T(8,128)(2,1)} %s2_.1), custom_call_target="tpu_custom_call" | custom-call | tf_op jit(solution)/shard_map/pallas_call | solution.py:235
  89.2 1.0 slice_convert_fusion
  90.2 0.7 copy.55.bias_ref.vec_ref
  90.9 1.3 broadcast_in_dim.39.al_ref
  92.2 25.4 %shard_map.315 = (f32[2,640,768]{2,1,0:T(8,128)}, bf16[2,640,768]{2,1,0:T(8,128)(2,1)}, bf16[2,640,768]{2,1,0:T(8,128)(2,1)}, bf16[2,640,768]{2,1,0:T(8,128)(2,1...) custom-call(s32[2]{0:T(128)} %refs_0_.1, bf16[2,640,768]{2,1,0:T(8,128)(2,1)} %tok_ref.1, ...), custom_call_target="tpu_custom_call" | custom-call | tf_op jit(solution)/shard_map/pallas_call | solution.py:551
  117.6 0.2 slice.80
  117.8 0.9 reshape.89.ib_ref
  118.6 0.0 copy-start.3
  118.6 69.1 %shard_map.316 = (bf16[1280,768]{1,0:T(8,128)(2,1)}, f32[1280,768]{1,0:T(8,128)}, bf16[1280,768]{1,0:T(8,128)(2,1)}, bf16[768,3840]{1,0:T(8,128)(2,1)}, bf16[307...) custom-call(bf16[1280,768]{1,0:T(8,128)(2,1)} %bitcast.27, f32[1280,768]{1,0:T(8,128)} %bitcast.34, ...), custom_call_target="tpu_custom_call" | custom-call | tf_op jit(solution)/shard_map/pallas_call | solution.py:689
  187.7 0.5 broadcast.13
  188.2 1.4 reduce.19
  189.6 0.4 reshape.93
  190.0 0.9 copy.57
  190.9 0.1 pad.2.clone
  191.0 0.9 maximum_maximum_fusion.refs_11_
  191.9 0.0 copy-done.3
  191.9 1.0 copy.58.refs_1_
  193.0 46.6 %shard_map.317 = (bf16[768,768]{1,0:T(8,128)(2,1)}, bf16[768,768]{1,0:T(8,128)(2,1)}, bf16[768,768]{1,0:T(8,128)(2,1)}, bf16[768,128]{1,0:T(8,128)(2,1)}, bf16[2,640,768]{2,1,0:T(8,128)(2,1)}) custom-call(s32[2]{0:T(128)} %refs_0_.1, s32[2,512,1]{2,1,0:T(8,128)} %copy.58.refs_1_, bf16[2,640,768]{2,1,0:T(8,128)(2,1)} %get-tuple-element.48.refs_2_, ...), custom_call_target="tpu_custom_call" | custom-call | tf_op jit(solution)/shard_map/pallas_call | solution.py:804
  239.6 0.0 copy-start.1
  239.6 0.0 copy-start.2
  239.6 1.5 constant_dynamic-update-slice_fusion.3
  241.0 1.4 constant_dynamic-update-slice_fusion.2
  242.4 0.0 copy-done.1
  242.4 0.1 constant_dynamic-update-slice_fusion.1
  242.5 0.0 copy-done.2
  242.6 0.0 copy-start
  242.6 1.9 copy-done
  244.6 76.5 %shard_map.318 = (f32[96,768]{1,0:T(8,128)}, f32[24,3840]{1,0:T(8,128)}, f32[24,2560]{1,0:T(8,128)}) custom-call(bf16[16,2,96,768]{3,2,1,0:T(8,128)(2,1)} %bitcast.31, bf16[16,48,3840]{2,1,0:T(8,128)(2,1)} %bitcast.30, bf16[16,48,2560]{2,1,0:T(8,128)(2,1)} %bitcast.28), custom_call_target="tpu_custom_call" | custom-call | tf_op jit(solution)/shard_map/pallas_call | solution.py:409
  321.1 1.7 slice.73
  322.7 1.6 fusion
  324.4 1.5 slice.69
  325.9 0.8 slice.74
  326.7 0.6 reshape.97
  327.3 1.8 slice_reduce_fusion
  329.1 1.7 copy.64
  (5 shorter events, 0.1 us)
Async XLA Ops:
  118.6 73.3 %copy-start.3 = (s32[2,512]{1,0:T(2,128)S(1)}, s32[2,512]{1,0:T(2,128)}, u32[]{:S(2)}) copy-start(s32[2,512]{1,0:T(2,128)} %param.22) | copy-start | bytes 12292
  239.6 2.9 copy-start.1
  239.6 2.9 copy-start.2
  242.6 1.9 copy-start

commit v3 on v2

--- a/solution.py
+++ b/solution.py
@@ -85,42 +85,42 @@
         c = remote(src, dst, self.send.at[index], self.recv.at[index], dev)
         return c
 
-    def start(self, src, dst, index, dev):
-        c = self.copy(src, dst, index, dev)
-        c.start()
-        self.started.append(c)
+    def start(self, make):
+        make().start()
+        self.started.append(make)
 
     def chip(self, back, spot):
         return 4 * self.p.plane(back) + spot
 
     def along_z(self):
         p = self.p
-        mine = self.view(self.chip(0, p.spot))
-        c = pltpu.make_async_copy(self.own, mine, self.local)
-        c.start()
-        self.own_copy = c
+        mine = lambda: self.view(self.chip(0, p.spot))
+        self.own_copy().start()
         for k in range(1, PLANES):
-            self.start(self.own, mine, k - 1, (p.ahead(k), p.f))
+            self.start(lambda k=k: self.copy(self.own, mine(), k - 1, (p.ahead(k), p.f)))
+
+    def own_copy(self):
+        return pltpu.make_async_copy(self.own, self.view(self.chip(0, self.p.spot)), self.local)
 
     def to_neighbours(self, back):
         p = self.p
-        piece = self.view(self.chip(back, p.spot))
+        piece = lambda: self.view(self.chip(back, p.spot))
         if back:
-            self.copy(piece, piece, back - 1, (p.z, p.f)).wait_recv()
-        src = piece if back else self.own
-        self.start(src, piece, 3 + back, (p.z, p.xn))
-        self.start(src, piece, 7 + back, (p.z, p.yn))
+            self.copy(piece(), piece(), back - 1, (p.z, p.f)).wait_recv()
+        src = piece if back else lambda: self.own
+        self.start(lambda: self.copy(src(), piece(), 3 + back, (p.z, p.xn)))
+        self.start(lambda: self.copy(src(), piece(), 7 + back, (p.z, p.yn)))
 
     def to_diagonal(self, back):
         p, cut = self.p, self.cut(back)
-        cx, cy = self.chip(back, p.spot_x), self.chip(back, p.spot_y)
-        full_x, full_y = self.view(cx), self.view(cy)
+        cx, cy = lambda: self.chip(back, p.spot_x), lambda: self.chip(back, p.spot_y)
+        full_x, full_y = self.view(cx()), self.view(cy())
         self.copy(full_x, full_x, 3 + back, (p.z, p.xn)).wait_recv()
-        part = self.view(cx, 0, cut)
-        self.start(part, part, 11 + back, (p.z, p.yn))
+        part_x = lambda: self.view(cx(), 0, cut)
+        self.start(lambda: self.copy(part_x(), part_x(), 11 + back, (p.z, p.yn)))
         self.copy(full_y, full_y, 7 + back, (p.z, p.yn)).wait_recv()
-        part = self.view(cy, cut, self.rows)
-        self.start(part, part, 15 + back, (p.z, p.xn))
+        part_y = lambda: self.view(cy(), cut, self.rows)
+        self.start(lambda: self.copy(part_y(), part_y(), 15 + back, (p.z, p.xn)))
 
     def to_core(self, back):
         p, cut = self.p, self.cut(back)
@@ -129,9 +129,9 @@
         self.copy(a, a, 11 + back, (p.z, p.yn)).wait_recv()
         self.copy(b, b, 15 + back, (p.z, p.xn)).wait_recv()
         if back == 0:
-            self.own_copy.wait()
-        blk = self.block(p.plane(back), p.core)
-        self.start(blk, blk, 19 + back, (p.z, p.sib))
+            self.own_copy().wait()
+        blk = lambda: self.block(p.plane(back), p.core)
+        self.start(lambda: self.copy(blk(), blk(), 19 + back, (p.z, p.sib)))
 
     def finish(self):
         p = self.p
@@ -140,8 +140,8 @@
             self.copy(blk, blk, 19 + back, (p.z, p.sib)).wait_recv()
 
     def drain(self):
-        for c in self.started:
-            c.wait_send()
+        for make in self.started:
+            make().wait_send()
 
 
 def build_own(place, shard, land, own):
@@ -158,103 +158,16 @@
 class Pair:
     def __init__(self, place, shard, land, own, send, recv):
         half = own.shape[1]
-        src = shard.at[:, pl.ds(pl.multiple_of((1 - place.core) * half, 128), half)]
-        self.c = remote(src, land, send, recv, (place.z, place.sib))
+        src = lambda: shard.at[:, pl.ds(pl.multiple_of((1 - place.core) * half, 128), half)]
+        self.c = lambda: remote(src(), land, send, recv, (place.z, place.sib))
         self.args = (place, shard, land, own)
 
     def start(self):
-        self.c.start()
+        self.c().start()
 
     def done(self):
-        self.c.wait()
+        self.c().wait()
         build_own(*self.args)
-
-
-def gather_steps(groups, pairs):
-    g0, g1, g2 = groups
-    steps = []
-
-    def begin():
-        for pr in pairs:
-            pr.start()
-        pairs[0].done()
-        g0.along_z()
-        g0.to_neighbours(0)
-        pairs[1].done()
-        g1.along_z()
-
-    steps.append(begin)
-    for k in (1, 2, 3):
-        steps.append(functools.partial(g0.to_neighbours, k))
-    steps.append(functools.partial(g1.to_neighbours, 0))
-    steps.append(g2.along_z)
-    for k in range(4):
-        steps.append(functools.partial(g0.to_diagonal, k))
-    for k in (1, 2, 3):
-        steps.append(functools.partial(g1.to_neighbours, k))
-    for k in range(4):
-        steps.append(functools.partial(g0.to_core, k))
-    steps.append(functools.partial(g2.to_neighbours, 0))
-    steps.append(g0.finish)
-    for k in range(4):
-        steps.append(functools.partial(g1.to_diagonal, k))
-    for k in (1, 2, 3):
-        steps.append(functools.partial(g2.to_neighbours, k))
-    for k in range(4):
-        steps.append(functools.partial(g1.to_core, k))
-    for k in range(4):
-        steps.append(functools.partial(g2.to_diagonal, k))
-    for k in range(4):
-        steps.append(functools.partial(g2.to_core, k))
-    steps.append(g1.finish)
-    steps.append(g2.finish)
-    for g in groups:
-        steps.append(g.drain)
-    return steps
-
-
-def gather_kernel(s0, s1, s2, w0, w1, w2, land0, land1, own0, own1, pair_sem, local, send, recv):
-    place = Place()
-    place.barrier()
-    pairs = [
-        Pair(place, s0, land0, own0, pair_sem.at[0], pair_sem.at[1]),
-        Pair(place, s1, land1, own1, pair_sem.at[2], pair_sem.at[3]),
-    ]
-    groups = [
-        Gather(place, w0, own0, send.at[0], recv.at[0], local.at[0], w0.shape[2]),
-        Gather(place, w1, own1, send.at[1], recv.at[1], local.at[1], w1.shape[2]),
-        Gather(place, w2, s2, send.at[2], recv.at[2], local.at[2]),
-    ]
-    for step in gather_steps(groups, pairs):
-        step()
-
-
-def gather_all(s0, s1, s2):
-    n0, n1 = s0.shape[1], s1.shape[1]
-    bf = jnp.bfloat16
-    return pl.pallas_call(
-        gather_kernel,
-        out_shape=(
-            jax.ShapeDtypeStruct((CHIPS, 48, n0), bf),
-            jax.ShapeDtypeStruct((CHIPS, 48, n1), bf),
-            jax.ShapeDtypeStruct((CHIPS, 2, 96, s2.shape[1]), bf),
-        ),
-        in_specs=[VMEM] * 3,
-        out_specs=[ANY] * 3,
-        scratch_shapes=[
-            pltpu.VMEM((24, n0 // 2), jnp.float32),
-            pltpu.VMEM((24, n1 // 2), jnp.float32),
-            pltpu.VMEM((48, n0 // 2), bf),
-            pltpu.VMEM((48, n1 // 2), bf),
-            pltpu.SemaphoreType.DMA((4,)),
-            pltpu.SemaphoreType.DMA((3,)),
-            pltpu.SemaphoreType.DMA((3, Gather.SEMS)),
-            pltpu.SemaphoreType.DMA((3, Gather.SEMS)),
-        ],
-        compiler_params=pltpu.CompilerParams(
-            collective_id=0, has_side_effects=True, vmem_limit_bytes=56 * 2**20
-        ),
-    )(s0, s1, s2)
 
 
 class Scatter:
@@ -295,10 +208,14 @@
 
     def from_sibling(self, back):
         p = self.p
-        blk = pl.ds(4 * p.plane(back), 4)
-        c = pltpu.make_async_copy(self.block(p.plane(back), p.core), self.sums.at[blk], self.local.at[back])
+        blk = lambda: pl.ds(4 * p.plane(back), 4)
+        c = pltpu.make_async_copy(self.block(p.plane(back), p.core), self.sums.at[blk()], self.local.at[back])
         c.start()
-        self.start(self.block(p.plane(back), 1 - p.core), self.from_core.at[blk], back, (p.z, p.sib))
+        self.start(
+            lambda: self.copy(
+                self.block(p.plane(back), 1 - p.core), self.from_core.at[blk()], back, (p.z, p.sib)
+            )
+        )
 
     def to_diagonal(self, back):
         p, cut, rows = self.p, self.cut(back), self.rows
@@ -308,9 +225,20 @@
         for j in range(4):
             at = 4 * p.plane(back) + j
             self.sums[at] = self.sums[at] + self.from_core[at]
-        cd = self.chip(back, p.spot_d)
-        self.start(self.sums.at[cd, pl.ds(0, cut)], self.la.at[back, pl.ds(0, cut)], 4 + back, (p.z, p.xn))
-        self.start(self.sums.at[cd, pl.ds(cut, rows - cut)], self.lb.at[back, pl.ds(0, rows - cut)], 8 + back, (p.z, p.yn))
+        cd = lambda: self.chip(back, p.spot_d)
+        self.start(
+            lambda: self.copy(
+                self.sums.at[cd(), pl.ds(0, cut)], self.la.at[back, pl.ds(0, cut)], 4 + back, (p.z, p.xn)
+            )
+        )
+        self.start(
+            lambda: self.copy(
+                self.sums.at[cd(), pl.ds(cut, rows - cut)],
+                self.lb.at[back, pl.ds(0, rows - cut)],
+                8 + back,
+                (p.z, p.yn),
+            )
+        )
 
     def to_neighbours(self, back):
         p, cut, rows = self.p, self.cut(back), self.rows
@@ -318,10 +246,12 @@
         a, b = self.la.at[back, pl.ds(0, cut)], self.lb.at[back, pl.ds(0, rows - cut)]
         self.copy(a, a, 4 + back, (p.z, p.xn)).wait_recv()
         self.sums[cy, 0:cut] = self.sums[cy, 0:cut] + a[...]
-        self.start(self.sums.at[cy], self.ly.at[back], 16 + back, (p.z, p.yn))
+        to_y = lambda: self.sums.at[self.chip(back, p.spot_y)]
+        self.start(lambda: self.copy(to_y(), self.ly.at[back], 16 + back, (p.z, p.yn)))
         self.copy(b, b, 8 + back, (p.z, p.yn)).wait_recv()
         self.sums[cx, cut:rows] = self.sums[cx, cut:rows] + b[...]
-        self.start(self.sums.at[cx], self.lx.at[back], 12 + back, (p.z, p.xn))
+        to_x = lambda: self.sums.at[self.chip(back, p.spot_x)]
+        self.start(lambda: self.copy(to_x(), self.lx.at[back], 12 + back, (p.z, p.xn)))
 
     def along_z(self, back):
         p = self.p
@@ -333,7 +263,8 @@
         got = self.sums[c0].astype(f) + lx[...].astype(f) + ly[...].astype(f)
         self.sums[c0] = got.astype(jnp.bfloat16)
         if back:
-            self.start(self.sums.at[c0], self.lz.at[back - 1], 20 + back - 1, (p.plane(back), p.f))
+            mine = lambda: self.sums.at[self.chip(back, p.spot)]
+            self.start(lambda: self.copy(mine(), self.lz.at[back - 1], 20 + back - 1, (p.plane(back), p.f)))
 
     def owner(self):
         p = self.p
@@ -349,8 +280,8 @@
             return
         self.total[...] = total
         rows = self.rows // 2
-        theirs = pl.ds(pl.multiple_of((1 - p.core) * rows, 8), rows)
-        self.start(self.total.at[theirs], self.last, 23, (p.z, p.sib))
+        theirs = lambda: self.total.at[pl.ds(pl.multiple_of((1 - p.core) * rows, 8), rows)]
+        self.start(lambda: self.copy(theirs(), self.last, 23, (p.z, p.sib)))
 
     def finish(self):
         if self.half is None:
@@ -361,62 +292,6 @@
         mine = pl.ds(pl.multiple_of(p.core * rows, 8), rows)
         self.out[:, pl.ds(pl.multiple_of(p.core * half, 128), half)] = self.total[mine]
         self.out[:, pl.ds(pl.multiple_of((1 - p.core) * half, 128), half)] = self.last[...]
-
-
-def scatter_steps(groups):
-    stages = [[], [], [], [], []]
-    seq = []
-    for i, g in enumerate(groups):
-        for s, fn in enumerate((g.from_sibling, g.to_diagonal, g.to_neighbours, g.along_z)):
-            for k in (3, 2, 1, 0):
-                seq.append((i + s, i, s, functools.partial(fn, k)))
-        seq.append((i + 4, i, 4, g.owner))
-        seq.append((i + 5, i, 5, g.finish))
-    seq.sort(key=lambda t: (t[0], -t[2] if t[2] < 1 else 0, t[1]))
-    steps = [t[3] for t in seq]
-    for g in groups:
-        steps.append(g.drain)
-    return steps
-
-
-def scatter_kernel(kinds, *refs):
-    n = len(kinds)
-    fulls, outs, rest = refs[:n], refs[n : 2 * n], list(refs[2 * n :])
-    local, send, recv = rest[-3:]
-    place = Place()
-    place.barrier()
-    groups, at = [], 0
-    for i, width in enumerate(kinds):
-        count = 7 if width is None else 9
-        groups.append(Scatter(place, fulls[i], rest[at : at + count], outs[i], send.at[i], recv.at[i], local.at[i], width))
-        at += count
-    for step in scatter_steps(groups):
-        step()
-
-
-def scatter_all(grads, cid):
-    kinds, outs, scratch = [], [], []
-    for g in grads:
-        if g.ndim == 3:
-            kinds.append(g.shape[2])
-            outs.append(jax.ShapeDtypeStruct((24, g.shape[2]), jnp.float32))
-            scratch += Scatter.scratch(48, g.shape[2] // 2, True)
-        else:
-            kinds.append(None)
-            outs.append(jax.ShapeDtypeStruct((96, g.shape[3]), jnp.float32))
-            scratch += Scatter.scratch(96, g.shape[3], False)
-    n = len(kinds)
-    return pl.pallas_call(
-        functools.partial(scatter_kernel, tuple(kinds)),
-        out_shape=tuple(outs),
-        in_specs=[ANY] * n,
-        out_specs=tuple([VMEM] * n),
-        scratch_shapes=scratch
-        + [pltpu.SemaphoreType.DMA((n, 4)), pltpu.SemaphoreType.DMA((n, Scatter.SEMS)), pltpu.SemaphoreType.DMA((n, Scatter.SEMS))],
-        compiler_params=pltpu.CompilerParams(
-            collective_id=cid, has_side_effects=True, vmem_limit_bytes=56 * 2**20
-        ),
-    )(*grads)
 
 
 F = jnp.float32
@@ -497,7 +372,7 @@
     return (align == lax.broadcasted_iota(jnp.int32, shape, axis)).astype(F)
 
 
-def forward_body(b, j, len_ref, tok_ref, al_ref, w_ref, bias_ref, outs, low_s):
+def forward_body(b, j, len_ref, tok_ref, al_ref, w_cols, bias_ref, outs, low_s, hook=lambda at: None):
     base_ref, low_ref, q_ref, k_ref, v_ref, att_ref, lse_ref = outs
     text, width = al_ref.shape[2], tok_ref.shape[2]
     segs = tok_ref.shape[1] - text
@@ -516,11 +391,12 @@
         low_s[:text] = tok[:text]
         low_s[text:] = seg_base.astype(BF)
 
+    hook(0)
     low = low_s[...]
     parts = []
     for i, ref in enumerate((q_ref, k_ref, v_ref)):
         at = i * width + j * QUAD
-        rows = dot(low, w_ref[:, pl.ds(pl.multiple_of(at, QUAD), QUAD)], NN)
+        rows = dot(low, w_cols(pl.ds(pl.multiple_of(at, QUAD), QUAD)), NN)
         if i != 1:
             rows = rows + bias_ref[i // 2 : i // 2 + 1, pl.ds(pl.multiple_of(j * QUAD, QUAD), QUAD)]
         rows = rows.astype(BF)
@@ -535,10 +411,12 @@
         att_ref[0, :, cols] = out
         for h in range(2):
             lse_ref[0, 0, 2 * pr + h : 2 * pr + h + 1, :] = logs[h]
+        hook(1 + pr)
 
 
 def forward_kernel(len_ref, tok_ref, al_ref, w_ref, bias_ref, *rest):
-    forward_body(pl.program_id(0), pl.program_id(1), len_ref, tok_ref, al_ref, w_ref, bias_ref, rest[:7], rest[7])
+    w_cols = lambda cols: w_ref[:, cols]
+    forward_body(pl.program_id(0), pl.program_id(1), len_ref, tok_ref, al_ref, w_cols, bias_ref, rest[:7], rest[7])
 
 
 def forward_attention(seg_lengths, tokens, alignment, w0, biases):
@@ -721,14 +599,14 @@
     )(attended, base, cotangent, w1, w2, vec, inner_bias)
 
 
-def backward_body(j, b, refs, outs, scratch):
+def backward_body(j, b, refs, keep, gt_ref, scratch, hook=lambda at: None):
     len_ref, al_ref, q_ref, k_ref, v_ref, o_ref, do_ref, lse_ref, low_ref, gf_ref, w_ref, vec_ref = refs
-    gq_ref, gk_ref, gv_ref, gvec_ref, gt_ref = outs
     gbase_s, acc_s, vsum_s = scratch
     text, width = al_ref.shape[1], low_ref.shape[2]
     segs = low_ref.shape[1] - text
     quads = width // QUAD
 
+    hook(0)
     bias = key_bias(len_ref[b])
     parts = [[], [], []]
     for pr in range(2):
@@ -739,6 +617,8 @@
         )
         for i in range(3):
             parts[i].append(got[i])
+        if pr == 0:
+            hook(1)
     quad_grads = [jnp.concatenate(p, axis=1) for p in parts]
     cols = pl.ds(pl.multiple_of(j * QUAD, QUAD), QUAD)
 
@@ -765,10 +645,9 @@
 
     @pl.when(b == 1)
     def _():
-        for i, ref in enumerate((gq_ref, gk_ref, gv_ref)):
-            ref[...] = (acc_s[i] + weight[i]).astype(BF)
         for i in range(2):
             vsum_s[i : i + 1, cols] += sums[i]
+        keep(lambda i: (acc_s[i] + weight[i]).astype(BF))
 
     @pl.when(j == quads - 1)
     def _():
@@ -782,15 +661,27 @@
         gt_ref[0, :text] = (gbase[:text] + spread).astype(BF)
         gt_ref[0, text:] = gbase[text:].astype(BF)
 
-    @pl.when((j == quads - 1) & (b == 1))
-    def _():
-        lane = lax.broadcasted_iota(jnp.int32, (1, 128), 1)
-        cols2 = jnp.where(lane < 2, jnp.concatenate([vsum_s[...], jnp.zeros((120, width), F)], axis=0).T, 0.0)
-        gvec_ref[...] = (cols2 + vec_ref[...]).astype(BF)
+    hook(2)
+
+
+def vector_cols(vsum_s, vec_ref):
+    lane = lax.broadcasted_iota(jnp.int32, (1, 128), 1)
+    pad = jnp.zeros((120, vsum_s.shape[1]), F)
+    return (jnp.where(lane < 2, jnp.concatenate([vsum_s[...], pad], axis=0).T, 0.0) + vec_ref[...]).astype(BF)
 
 
 def backward_kernel(*refs):
-    backward_body(pl.program_id(0), pl.program_id(1), refs[:12], refs[12:17], refs[17:])
+    gvec_ref, gt_ref = refs[15:17]
+
+    def keep(grad):
+        for i in range(3):
+            refs[12 + i][...] = grad(i)
+
+        @pl.when(pl.program_id(0) == pl.num_programs(0) - 1)
+        def _():
+            gvec_ref[...] = vector_cols(refs[19], refs[11])
+
+    backward_body(pl.program_id(0), pl.program_id(1), refs[:12], keep, gt_ref, refs[17:])
 
 
 def backward_attention(seg_lengths, alignment, q, k, v, att, gatt, lse, low, gfirst, w0, vec):
@@ -835,8 +726,254 @@
     )(seg_lengths, alignment[:, :, None], q, k, v, att, gatt, lse, low, gfirst, w0, vec)
 
 
-def own_kernels(shard_rows):
-    return lax.axis_size("dp") == PLANES and lax.axis_size("fsdp") == 8 and shard_rows == 24
+def at_slots(plan, step, slot):
+    for (when, where), calls in plan.items():
+        if where == slot:
+
+            @pl.when(step == when)
+            def _():
+                for call in calls:
+                    call()
+
+
+def each(fn, *backs):
+    return [functools.partial(fn, k) for k in backs]
+
+
+def forward_fused_kernel(
+    len_ref, tok_ref, al_ref, s0, s1, s2, *rest
+):
+    outs, (w0, w1, w2) = rest[:7], rest[7:10]
+    low_s, w0_s, bias_s, land0, land1, own0, own1, pair_sem, local, send, recv = rest[10:]
+    b, j = pl.program_id(0), pl.program_id(1)
+    quads = pl.num_programs(1)
+    step = b * quads + j
+    place = Place()
+    pairs = [
+        Pair(place, s0, land0, own0, pair_sem.at[0], pair_sem.at[1]),
+        Pair(place, s1, land1, own1, pair_sem.at[2], pair_sem.at[3]),
+    ]
+    g0 = Gather(place, w0_s, own0, send.at[0], recv.at[0], local.at[0], w0.shape[2])
+    g1 = Gather(place, w1, own1, send.at[1], recv.at[1], local.at[1], w1.shape[2])
+    g2 = Gather(place, w2, s2, send.at[2], recv.at[2], local.at[2])
+    width = tok_ref.shape[2]
+    save = lambda: pltpu.make_async_copy(w0_s, w0, local.at[3])
+
+    def bias_rows():
+        vec = w0_s[:, :, 3 * width : 3 * width + 128].reshape(width, 128).astype(F)
+        bias_s[...] = vec.T[:8]
+
+    plan = {
+        (0, -1): [
+            place.barrier, pairs[0].start, pairs[1].start, pairs[0].done, g0.along_z,
+            functools.partial(g0.to_neighbours, 0), pairs[1].done, g1.along_z, g2.along_z,
+        ],
+        (0, 0): [
+            *each(g0.to_neighbours, 1, 2, 3), *each(g0.to_diagonal, 0), *each(g1.to_neighbours, 0),
+            *each(g0.to_diagonal, 1, 2, 3), *each(g1.to_neighbours, 1, 2, 3), *each(g0.to_core, 0, 1, 2, 3),
+            *each(g2.to_neighbours, 0, 1), g0.finish, save().start, bias_rows,
+        ],
+        (0, 1): each(g1.to_diagonal, 0, 1),
+        (0, 2): [*each(g1.to_diagonal, 2), *each(g2.to_neighbours, 2, 3)],
+        (1, 1): [*each(g1.to_diagonal, 3), *each(g1.to_core, 0)],
+        (1, 2): each(g1.to_core, 1),
+        (2, 1): [*each(g2.to_diagonal, 0), *each(g1.to_core, 2)],
+        (2, 2): [*each(g2.to_diagonal, 1), *each(g1.to_core, 3)],
+        (3, 1): each(g2.to_diagonal, 2),
+        (3, 2): each(g2.to_diagonal, 3),
+        (4, 1): each(g2.to_core, 0),
+        (4, 2): each(g2.to_core, 1),
+        (5, 2): [
+            *each(g2.to_core, 2, 3), g1.finish, g2.finish, lambda: save().wait(), g0.drain, g1.drain, g2.drain,
+        ],
+    }
+    at_slots(plan, step, -1)
+    w_cols = lambda cols: w0_s[:, :, cols].reshape(width, QUAD)
+    forward_body(
+        b, j, len_ref, tok_ref, al_ref, w_cols, bias_s, outs, low_s, functools.partial(at_slots, plan, step)
+    )
+
+
+def forward_fused(seg_lengths, tokens, alignment, s0, s1, s2):
+    docs, slots, width = tokens.shape
+    text = alignment.shape[1]
+    quads = width // QUAD
+    n0, n1 = s0.shape[1], s1.shape[1]
+    doc = pl.BlockSpec((1, slots, width), lambda b, j: (b, 0, 0))
+    quad = pl.BlockSpec((1, slots, QUAD), lambda b, j: (b, 0, j))
+    wide = jax.ShapeDtypeStruct((docs, slots, width), BF)
+    full = lambda a: once(a.shape, lambda b, j: (0, 0))
+    return pl.pallas_call(
+        forward_fused_kernel,
+        grid=(docs, quads),
+        in_specs=[SMEM, doc, pl.BlockSpec((1, 1, text), lambda b, j: (b, 0, 0)), full(s0), full(s1), full(s2)],
+        out_specs=[doc, doc, quad, quad, quad, quad, pl.BlockSpec((1, 1, 8, slots), lambda b, j: (b, j, 0, 0))]
+        + [ANY] * 3,
+        out_shape=[
+            jax.ShapeDtypeStruct((docs, slots, width), F),
+            wide,
+            wide,
+            wide,
+            wide,
+            wide,
+            jax.ShapeDtypeStruct((docs, quads, 8, slots), F),
+            jax.ShapeDtypeStruct((CHIPS, 48, n0), BF),
+            jax.ShapeDtypeStruct((CHIPS, 48, n1), BF),
+            jax.ShapeDtypeStruct((CHIPS, 2, 96, width), BF),
+        ],
+        scratch_shapes=[
+            pltpu.VMEM((slots, width), BF),
+            pltpu.VMEM((CHIPS, 48, n0), BF),
+            pltpu.VMEM((8, width), F),
+            pltpu.VMEM((24, n0 // 2), F),
+            pltpu.VMEM((24, n1 // 2), F),
+            pltpu.VMEM((48, n0 // 2), BF),
+            pltpu.VMEM((48, n1 // 2), BF),
+            pltpu.SemaphoreType.DMA((4,)),
+            pltpu.SemaphoreType.DMA((4,)),
+            pltpu.SemaphoreType.DMA((3, Gather.SEMS)),
+            pltpu.SemaphoreType.DMA((3, Gather.SEMS)),
+        ],
+        compiler_params=pltpu.CompilerParams(collective_id=0, has_side_effects=True, vmem_limit_bytes=LIMIT),
+    )(seg_lengths, tokens, alignment[:, None, :], s0, s1, s2)
+
+
+def backward_fused_kernel(widths, *refs):
+    ins, (g2_ref, g1_ref) = refs[:12], refs[12:14]
+    gt_ref, o_wide, o_inner, o_outer, o_vec = refs[14], refs[15:19], refs[19], refs[20], refs[21]
+    scratch = refs[22:25]
+    rest = list(refs[25:])
+    local, send, recv = rest[-3:]
+    j, b = pl.program_id(0), pl.program_id(1)
+    step = 2 * j + b
+    width = ins[8].shape[2]
+    place = Place()
+    take = lambda n: [rest.pop(0) for _ in range(n)]
+    quad_s, stage = take(3), take(1)[0]
+    sources = [g2_ref, g1_ref, *quad_s]
+    groups = []
+    for i, (src, wide) in enumerate(zip(sources, widths)):
+        bufs = take(7 if wide is None else 9)
+        out = o_outer if wide is None else stage.at[:, pl.ds(0, wide)]
+        groups.append(Scatter(place, src, bufs, out, send.at[i], recv.at[i], local.at[i], wide))
+    g2, g1, q0, q1, q2 = groups
+
+    def give_rest():
+        g1.finish()
+        o_wide[3][...] = stage[:, :width]
+        o_inner[...] = stage[:, width : widths[1]]
+
+    def give_quad(k):
+        groups[2 + k].finish()
+        for i in range(3):
+            o_wide[i][:, k * QUAD : (k + 1) * QUAD] = stage[:, i * QUAD : (i + 1) * QUAD]
+        if k == 2:
+            o_vec[...] = stage[:, 3 * QUAD : 3 * QUAD + 128]
+
+    def keep(grad):
+        for k in range(3):
+
+            @pl.when(j == k)
+            def _():
+                for i in range(3):
+                    quad_s[k][:, :, i * QUAD : (i + 1) * QUAD] = grad(i).reshape(CHIPS, 48, QUAD)
+                if k == 2:
+                    vec = vector_cols(scratch[2], ins[11])
+                    both = jnp.concatenate([vec, jnp.zeros_like(vec)], axis=1)
+                    quad_s[k][:, :, 3 * QUAD :] = both.reshape(CHIPS, 48, QUAD)
+
+    late, soon = (3, 2), (1, 0)
+    all4 = late + soon
+    plan = {
+        (0, 0): [place.barrier, *each(g2.from_sibling, *all4), *each(g1.from_sibling, *all4)],
+        (0, 1): each(g2.to_diagonal, *late),
+        (0, 2): [*each(g2.to_diagonal, *soon), *each(g1.to_diagonal, *late)],
+        (1, 1): [*each(g2.to_neighbours, *late), *each(g1.to_diagonal, *soon)],
+        (1, 2): [*each(g2.to_neighbours, *soon), *each(q0.from_sibling, *all4)],
+        (2, 1): [*each(g1.to_neighbours, *late), *each(g2.along_z, *late)],
+        (2, 2): [*each(g1.to_neighbours, *soon), *each(q0.to_diagonal, *all4), *each(g2.along_z, *soon)],
+        (3, 1): [*each(g1.along_z, *late)],
+        (3, 2): [*each(q0.to_neighbours, *all4), *each(q1.from_sibling, *all4), *each(g1.along_z, *soon), g2.owner],
+        (4, 1): [g2.finish, *each(q1.to_diagonal, *all4)],
+        (4, 2): [*each(q0.along_z, *all4), g1.owner],
+        (5, 1): [*each(q1.to_neighbours, *all4), give_rest],
+        (5, 2): [
+            *each(q2.from_sibling, *all4), *each(q1.along_z, *all4), q0.owner, *each(q2.to_diagonal, *all4),
+            functools.partial(give_quad, 0), *each(q2.to_neighbours, *all4), q1.owner, *each(q2.along_z, *all4),
+            functools.partial(give_quad, 1), q2.owner, functools.partial(give_quad, 2),
+            *[g.drain for g in groups],
+        ],
+    }
+    backward_body(j, b, ins, keep, gt_ref, scratch, functools.partial(at_slots, plan, step))
+
+
+def backward_fused(seg_lengths, alignment, q, k, v, att, gatt, lse, low, gfirst, w0, vec, g2, g1):
+    docs, slots, width = low.shape
+    text = alignment.shape[1]
+    quads = width // QUAD
+    quad = pl.BlockSpec((1, slots, QUAD), lambda j, b: (b, 0, j))
+    doc = pl.BlockSpec((1, slots, width), lambda j, b: (b, 0, 0))
+    whole = lambda *shape: once(shape, lambda j, b: (0,) * len(shape))
+    n1 = g1.shape[2]
+    widths = (None, n1, 3 * QUAD, 3 * QUAD, 4 * QUAD)
+    bufs = []
+    for wide in widths:
+        bufs += Scatter.scratch(96, width, False) if wide is None else Scatter.scratch(48, wide // 2, True)
+    n = len(widths)
+    shard = jax.ShapeDtypeStruct((24, width), F)
+    return pl.pallas_call(
+        functools.partial(backward_fused_kernel, widths),
+        grid=(quads, docs),
+        in_specs=[
+            SMEM,
+            pl.BlockSpec((1, text, 1), lambda j, b: (b, 0, 0)),
+            quad,
+            quad,
+            quad,
+            quad,
+            quad,
+            pl.BlockSpec((1, 1, 8, slots), lambda j, b: (b, j, 0, 0)),
+            doc,
+            pl.BlockSpec((1, slots, width), lambda j, b: (jnp.where(j == 0, b, 1), 0, 0)),
+            whole(*w0.shape),
+            whole(*vec.shape),
+            ANY,
+            ANY,
+        ],
+        out_specs=[
+            pl.BlockSpec((1, slots, width), lambda j, b: (jnp.where(j == quads - 1, b, 0), 0, 0)),
+            *[whole(24, width)] * 4,
+            whole(24, n1 - width),
+            whole(96, width),
+            whole(24, 128),
+        ],
+        out_shape=[
+            jax.ShapeDtypeStruct((docs, slots, width), BF),
+            shard,
+            shard,
+            shard,
+            shard,
+            jax.ShapeDtypeStruct((24, n1 - width), F),
+            jax.ShapeDtypeStruct((96, width), F),
+            jax.ShapeDtypeStruct((24, 128), F),
+        ],
+        scratch_shapes=[
+            pltpu.VMEM((docs, slots, width), F),
+            pltpu.VMEM((3, width, QUAD), F),
+            pltpu.VMEM((8, width), F),
+            *[pltpu.VMEM((CHIPS, 48, wide), BF) for wide in widths[2:]],
+            pltpu.VMEM((24, n1), F),
+            *bufs,
+            pltpu.SemaphoreType.DMA((n, 4)),
+            pltpu.SemaphoreType.DMA((n, Scatter.SEMS)),
+            pltpu.SemaphoreType.DMA((n, Scatter.SEMS)),
+        ],
+        compiler_params=pltpu.CompilerParams(collective_id=1, has_side_effects=True, vmem_limit_bytes=LIMIT),
+    )(seg_lengths, alignment[:, :, None], q, k, v, att, gatt, lse, low, gfirst, w0, vec, g2, g1)
+
+
+def own_kernels(shard_rows, docs):
+    return lax.axis_size("dp") == PLANES and lax.axis_size("fsdp") == 8 and shard_rows == 24 and docs == 2
 
 
 def shards(
@@ -848,57 +985,44 @@
     rows = query_weight.shape[0]
     ff = inner_weight.shape[1]
     every = ("dp", "fsdp")
-    own = own_kernels(rows)
+    own = own_kernels(rows, docs)
     vectors = (query_bias, value_bias, out_bias, first_gain, first_shift, outer_bias, second_gain, second_shift)
     columns = [t[:, None] for t in vectors] + [inner_bias.reshape(rows, 4)]
     pad = jnp.zeros((rows, 256 - 12), BF)
     s0 = jnp.concatenate([query_weight, key_weight, value_weight] + columns + [pad], axis=1)
     s1 = jnp.concatenate([out_weight, inner_weight], axis=1)
     if own:
-        w0, w1, w2 = gather_all(s0.astype(F), s1.astype(F), outer_weight)
+        *saved, w0, w1, w2 = forward_fused(seg_lengths, tokens, alignment, s0.astype(F), s1.astype(F), outer_weight)
     else:
         w0, w1, w2 = (lax.all_gather(s, every, axis=0, tiled=True) for s in (s0, s1, outer_weight))
     w0, w1, w2 = w0.reshape(width, -1), w1.reshape(width, -1), w2.reshape(-1, width)
     vec = w0[:, 3 * width : 3 * width + 12].astype(F)
     rows_vec = vec[:, :8].T
     inner_row = vec[:, 8:12].reshape(1, ff)
-
-    base, low, q, k, v, att, lse = forward_attention(seg_lengths, tokens, alignment, w0, rows_vec)
+    if not own:
+        saved = forward_attention(seg_lengths, tokens, alignment, w0, rows_vec)
+    base, low, q, k, v, att, lse = saved
+
     flat = lambda t: t.reshape(docs * slots, width)
     encoded, gfirst, gatt, g1, g2, gvec, ginner = mlp_both(
         flat(att), flat(base), flat(cotangent), w1, w2, rows_vec, inner_row
     )
     whole = lambda t: t.reshape(docs, slots, width)
     vec_cols = jnp.concatenate([gvec.T, ginner.reshape(width, 4), jnp.zeros((width, 116), F)], axis=1)
-    gq, gk, gv, gcols, grad_tokens = backward_attention(
-        seg_lengths, alignment, q, k, v, att, whole(gatt), lse, low, whole(gfirst), w0, vec_cols
-    )
-    g0 = jnp.concatenate([gq, gk, gv, gcols, jnp.zeros((width, 128), BF)], axis=1)
+    back = (seg_lengths, alignment, q, k, v, att, whole(gatt), lse, low, whole(gfirst), w0, vec_cols)
     if own:
-        o2, o1, o0 = scatter_all(
-            (g2.reshape(CHIPS, 2, 96, width), g1.reshape(CHIPS, 48, -1), g0.reshape(CHIPS, 48, -1)), 1
+        grad_tokens, gq, gk, gv, gout, ginn, gouter, sums = backward_fused(
+            *back, g2.reshape(CHIPS, 2, 96, width), g1.reshape(CHIPS, 48, -1)
         )
     else:
-        o2, o1, o0 = (lax.psum_scatter(g.astype(F), every, scatter_dimension=0, tiled=True) for g in (g2, g1, g0))
-    sums = o0[:, 3 * width :]
+        gq, gk, gv, gcols, grad_tokens = backward_attention(*back)
+        owned = lambda g: lax.psum_scatter(g.astype(F), every, scatter_dimension=0, tiled=True)
+        gq, gk, gv, sums, gouter = (owned(g) for g in (gq, gk, gv, gcols, g2))
+        g1 = owned(g1)
+        gout, ginn = g1[:, :width], g1[:, width:]
     return (
-        whole(encoded),
-        grad_tokens,
-        o0[:, :width],
-        sums[:, 0],
-        o0[:, width : 2 * width],
-        o0[:, 2 * width : 3 * width],
-        sums[:, 1],
-        o1[:, :width],
-        sums[:, 2],
-        sums[:, 3],
-        sums[:, 4],
-        o1[:, width:],
-        sums[:, 8:12].reshape(-1),
-        o2,
-        sums[:, 5],
-        sums[:, 6],
-        sums[:, 7],
+        whole(encoded), grad_tokens, gq, sums[:, 0], gk, gv, sums[:, 1], gout, sums[:, 2], sums[:, 3], sums[:, 4],
+        ginn, sums[:, 8:12].reshape(-1), gouter, sums[:, 5], sums[:, 6], sums[:, 7],
     )
 
 

time: 332 us -> 285 us (0.86)
  Pallas kernels: 296 us -> 254 us
  local copies, waits for them, and re-layouts: 28.3 us -> 23.8 us
    pallas_call x4 -> x2, Pallas kernels: 227 us -> 185 us  [the longest x1 95.3 us: backward_fused(): pl.pallas_call(functools.partial(backward_fused_kernel, widths), grid=(qu...]
    slice x3 -> x0, local copies, waits for them, and re-layouts: 4.86 us -> none  [the longest x1 1.7 us: shards(): o1[:, width:]]
    unnamed x13 -> x21, local copies, waits for them, and re-layouts: 6.59 us -> 7 us
where the time goes in v3:
time: 285 us; the launch traced here: 284 us
  Pallas kernels  254 us (89%)
  local copies, waits for them, and re-layouts  23.8 us (8%)
  other arithmetic  5.66 us (2%)
    pallas_call x1, Pallas kernels, backward_fused(): pl.pallas_call(functools.partial(backward_fused_kernel, widths), grid=(qu...  95.3 us
    pallas_call x1, Pallas kernels, forward_fused(): pl.pallas_call(forward_fused_kernel, grid=(docs, quads), in_specs=[SMEM,...  89.5 us
    pallas_call x1, Pallas kernels, mlp_both(): pl.pallas_call(functools.partial(mlp_kernel, tiles, ff_cut), grid=(tiles...  69.1 us
    unnamed x21, local copies, waits for them, and re-layouts  7 us
    broadcast_in_dim x8, local copies, waits for them, and re-layouts, shards(): columns = [t[:, None] for t in vectors] + [inner_bias.reshape(rows, 4)]  5.97 us

profile of v3, /device:TPU:0, one launch (start us, length us, event | category | flops | bytes accessed | tf_op | source)
XLA Modules:
  0.0 284.1 jit_solution(7376415015309646388)
XLA Ops:
  0.7 0.7 copy.46
  1.4 0.7 copy.47
  2.1 0.7 copy.48
  2.9 0.7 copy.49
  3.6 0.7 copy.50
  4.4 0.7 copy.51
  5.1 0.7 copy.52
  5.9 0.7 copy.53
  6.6 0.7 reshape.79
  7.4 0.9 concatenate.9
  8.3 0.7 convert_element_type.9.s0
  9.0 1.7 maximum_convert_fusion.s1
  10.7 1.3 broadcast_in_dim.36.al_ref
  12.0 89.5 %shard_map.314 = (f32[2,640,768]{2,1,0:T(8,128)}, bf16[2,640,768]{2,1,0:T(8,128)(2,1)}, bf16[2,640,768]{2,1,0:T(8,128)(2,1)}, bf16[2,640,768]{2,1,0:T(8,128)(2,1...) custom-call(s32[2]{0:T(128)} %refs_0_.1, ...), custom_call_target="tpu_custom_call" | custom-call | tf_op jit(solution)/shard_map/pallas_call | solution.py:806
  101.5 1.0 slice_convert_fusion
  102.4 0.7 copy.54.vec_ref
  103.2 0.2 slice.50
  103.4 0.9 reshape.86.ib_ref
  104.2 69.1 %shard_map.315 = (bf16[1280,768]{1,0:T(8,128)(2,1)}, f32[1280,768]{1,0:T(8,128)}, bf16[1280,768]{1,0:T(8,128)(2,1)}, bf16[768,3840]{1,0:T(8,128)(2,1)}, bf16[307...) custom-call(bf16[1280,768]{1,0:T(8,128)(2,1)} %bitcast.23, f32[1280,768]{1,0:T(8,128)} %bitcast.30, ...), custom_call_target="tpu_custom_call" | custom-call | tf_op jit(solution)/shard_map/pallas_call | solution.py:567
  173.3 0.0 copy-start.6
  173.3 0.5 broadcast.13
  173.8 1.4 reduce.19
  175.2 0.4 reshape.90
  175.6 0.9 copy.55
  176.5 0.1 pad.2.clone
  176.6 0.9 maximum_maximum_fusion.refs_11_
  177.5 0.0 copy-done.6
  177.5 1.0 copy.56.refs_1_
  178.5 95.3 %shard_map.316 = (bf16[2,640,768]{2,1,0:T(8,128)(2,1)}, f32[24,768]{1,0:T(8,128)}, f32[24,768]{1,0:T(8,128)}, f32[24,768]{1,0:T(8,128)}, f32[24,768]{1,0:T(8,128...) custom-call(s32[2]{0:T(128)} %refs_0_.1, s32[2,512,1]{2,1,0:T(8,128)} %copy.56.refs_1_, ...), custom_call_target="tpu_custom_call" | custom-call | tf_op jit(solution)/shard_map/pallas_call | solution.py:924
  273.9 0.8 slice.44
  274.7 0.6 reshape.93
  275.3 1.8 slice_reduce_fusion
  277.1 0.0 copy-start.5
  277.1 0.0 copy-start.4
  277.1 0.0 copy-start.3
  277.1 0.0 copy-start.2
  277.1 0.0 copy-start.1
  277.1 0.0 copy-start
  277.1 3.0 %copy.64 = bf16[2,640,768]{2,1,0:T(8,128)(2,1)} copy(bf16[2,640,768]{2,1,0:T(8,128)(2,1)} %get-tuple-element.93) | data formatting | bytes 3932160
  280.2 0.0 copy-done.5
  280.2 0.6 copy.65
  280.8 0.0 copy-done.4
  280.8 0.6 copy.66
  281.4 0.0 copy-done.3
  281.4 0.6 copy.67
  282.1 0.0 copy-done.2
  282.1 0.6 copy.68
  282.7 0.0 copy-done.1
  282.7 0.7 copy.69
  283.4 0.0 copy-done
  283.4 0.7 copy.70
  (3 shorter events, 0.0 us)
Async XLA Ops:
  173.3 4.2 %copy-start.6 = (s32[2,512]{1,0:T(2,128)S(1)}, s32[2,512]{1,0:T(2,128)}, u32[]{:S(2)}) copy-start(s32[2,512]{1,0:T(2,128)} %param.22) | copy-start | bytes 12292
  277.1 3.0 %copy-start.5 = (f32[24,768]{1,0:T(8,128)S(1)}, f32[24,768]{1,0:T(8,128)}, u32[]{:S(2)}) copy-start(f32[24,768]{1,0:T(8,128)} %get-tuple-element.94) | copy-start | bytes 221188
  277.1 3.7 %copy-start.4 = (f32[24,768]{1,0:T(8,128)S(1)}, f32[24,768]{1,0:T(8,128)}, u32[]{:S(2)}) copy-start(f32[24,768]{1,0:T(8,128)} %get-tuple-element.96) | copy-start | bytes 221188
  277.1 4.3 %copy-start.3 = (f32[24,768]{1,0:T(8,128)S(1)}, f32[24,768]{1,0:T(8,128)}, u32[]{:S(2)}) copy-start(f32[24,768]{1,0:T(8,128)} %get-tuple-element.97) | copy-start | bytes 221188
  277.1 4.9 %copy-start.2 = (f32[24,768]{1,0:T(8,128)S(1)}, f32[24,768]{1,0:T(8,128)}, u32[]{:S(2)}) copy-start(f32[24,768]{1,0:T(8,128)} %get-tuple-element.99) | copy-start | bytes 221188
  277.1 5.6 %copy-start.1 = (f32[24,3072]{1,0:T(8,128)S(1)}, f32[24,3072]{1,0:T(8,128)}, u32[]{:S(2)}) copy-start(f32[24,3072]{1,0:T(8,128)} %get-tuple-element.103) | copy-start | bytes 884740
  277.1 6.3 %copy-start = (f32[96,768]{1,0:T(8,128)S(1)}, f32[96,768]{1,0:T(8,128)}, u32[]{:S(2)}) copy-start(f32[96,768]{1,0:T(8,128)} %get-tuple-element.105) | copy-start | bytes 884740

commit v4 on v3

--- a/solution.py
+++ b/solution.py
@@ -31,6 +31,9 @@
     def plane(self, back):
         return (self.z + PLANES - back) % PLANES
 
+    def coming(self, k):
+        return (self.z, 1 + self.z % 2, (self.z + 2) % PLANES, 3 * ((self.z + 1) % 2))[k]
+
     def ahead(self, step):
         return (self.z + step) % PLANES
 
@@ -53,7 +56,7 @@
 
 
 class Gather:
-    SEMS = 3 + 4 + 4 + 4 + 4 + 4
+    SEMS = 29
 
     def __init__(self, place, full, own, send, recv, local, width=None):
         self.p, self.full, self.own = place, full, own
@@ -76,72 +79,96 @@
         cols = pl.ds(pl.multiple_of(core * self.half, 128), self.half)
         return self.full.at[pl.ds(4 * plane, 4), :, cols]
 
-    def cut(self, back):
+    def cut(self, k):
         if self.rows == 96:
             return 48
-        return 32 if back % 2 == 0 else 16
-
-    def copy(self, src, dst, index, dev):
-        c = remote(src, dst, self.send.at[index], self.recv.at[index], dev)
-        return c
-
-    def start(self, make):
-        make().start()
-        self.started.append(make)
-
-    def chip(self, back, spot):
-        return 4 * self.p.plane(back) + spot
+        return 32 if k % 2 == 0 else 16
+
+    def copy(self, src, dst, index, dev, send=None):
+        return remote(src, dst, self.send.at[index if send is None else send], self.recv.at[index], dev)
+
+    def start(self, make, when=None):
+        if when is None:
+            make().start()
+        else:
+            pl.when(when())(lambda: make().start())
+        self.started.append((make, when))
+
+    def drain(self):
+        for make, when in self.started:
+            if when is None:
+                make().wait_send()
+            else:
+                pl.when(when())(lambda: make().wait_send())
+
+    def chip(self, k, spot):
+        return 4 * self.p.coming(k) + spot
+
+    def own_copy(self):
+        return pltpu.make_async_copy(self.own, self.view(self.chip(0, self.p.spot)), self.local)
 
     def along_z(self):
         p = self.p
         mine = lambda: self.view(self.chip(0, p.spot))
         self.own_copy().start()
-        for k in range(1, PLANES):
-            self.start(lambda k=k: self.copy(self.own, mine(), k - 1, (p.ahead(k), p.f)))
-
-    def own_copy(self):
-        return pltpu.make_async_copy(self.own, self.view(self.chip(0, self.p.spot)), self.local)
-
-    def to_neighbours(self, back):
+        self.start(lambda: self.copy(self.own, mine(), p.z, (p.z - 1, p.f), 24), lambda: p.z > 0)
+        self.start(lambda: self.copy(self.own, mine(), p.z, (p.z + 1, p.f), 25), lambda: p.z < PLANES - 1)
+
+    def onward(self, k, when=None):
         p = self.p
-        piece = lambda: self.view(self.chip(back, p.spot))
-        if back:
-            self.copy(piece(), piece(), back - 1, (p.z, p.f)).wait_recv()
-        src = piece if back else lambda: self.own
-        self.start(lambda: self.copy(src(), piece(), 3 + back, (p.z, p.xn)))
-        self.start(lambda: self.copy(src(), piece(), 7 + back, (p.z, p.yn)))
-
-    def to_diagonal(self, back):
-        p, cut = self.p, self.cut(back)
-        cx, cy = lambda: self.chip(back, p.spot_x), lambda: self.chip(back, p.spot_y)
+        piece = lambda: self.view(self.chip(k, p.spot))
+        goal = lambda: p.z + jnp.where(p.coming(k) < p.z, 1, -1)
+        goes = lambda: (goal() >= 0) & (goal() < PLANES)
+        wait = lambda: self.copy(piece(), piece(), p.coming(k), (p.z, p.f)).wait_recv()
+        both = goes if when is None else lambda: when() & goes()
+        if when is None:
+            wait()
+        else:
+            pl.when(when())(wait)
+        self.start(lambda: self.copy(piece(), piece(), p.coming(k), (goal(), p.f), 25 + k), both)
+
+    def to_neighbours(self, k):
+        p = self.p
+        piece = lambda: self.view(self.chip(k, p.spot))
+        middle = lambda: p.z % 3 != 0
+        if k == 1:
+            self.onward(1)
+            self.onward(3, middle)
+        elif k == 2:
+            self.onward(2)
+        elif k == 3:
+            self.onward(3, lambda: p.z % 3 == 0)
+        src = piece if k else lambda: self.own
+        self.start(lambda: self.copy(src(), piece(), 4 + k, (p.z, p.xn)))
+        self.start(lambda: self.copy(src(), piece(), 8 + k, (p.z, p.yn)))
+
+    def to_diagonal(self, k):
+        p, cut = self.p, self.cut(k)
+        cx, cy = lambda: self.chip(k, p.spot_x), lambda: self.chip(k, p.spot_y)
         full_x, full_y = self.view(cx()), self.view(cy())
-        self.copy(full_x, full_x, 3 + back, (p.z, p.xn)).wait_recv()
+        self.copy(full_x, full_x, 4 + k, (p.z, p.xn)).wait_recv()
         part_x = lambda: self.view(cx(), 0, cut)
-        self.start(lambda: self.copy(part_x(), part_x(), 11 + back, (p.z, p.yn)))
-        self.copy(full_y, full_y, 7 + back, (p.z, p.yn)).wait_recv()
+        self.start(lambda: self.copy(part_x(), part_x(), 12 + k, (p.z, p.yn)))
+        self.copy(full_y, full_y, 8 + k, (p.z, p.yn)).wait_recv()
         part_y = lambda: self.view(cy(), cut, self.rows)
-        self.start(lambda: self.copy(part_y(), part_y(), 15 + back, (p.z, p.xn)))
-
-    def to_core(self, back):
-        p, cut = self.p, self.cut(back)
-        cd = self.chip(back, p.spot_d)
+        self.start(lambda: self.copy(part_y(), part_y(), 16 + k, (p.z, p.xn)))
+
+    def to_core(self, k):
+        p, cut = self.p, self.cut(k)
+        cd = self.chip(k, p.spot_d)
         a, b = self.view(cd, 0, cut), self.view(cd, cut, self.rows)
-        self.copy(a, a, 11 + back, (p.z, p.yn)).wait_recv()
-        self.copy(b, b, 15 + back, (p.z, p.xn)).wait_recv()
-        if back == 0:
+        self.copy(a, a, 12 + k, (p.z, p.yn)).wait_recv()
+        self.copy(b, b, 16 + k, (p.z, p.xn)).wait_recv()
+        if k == 0:
             self.own_copy().wait()
-        blk = lambda: self.block(p.plane(back), p.core)
-        self.start(lambda: self.copy(blk(), blk(), 19 + back, (p.z, p.sib)))
+        blk = lambda: self.block(p.coming(k), p.core)
+        self.start(lambda: self.copy(blk(), blk(), 20 + k, (p.z, p.sib)))
 
     def finish(self):
         p = self.p
-        for back in range(PLANES):
-            blk = self.block(p.plane(back), 1 - p.core)
-            self.copy(blk, blk, 19 + back, (p.z, p.sib)).wait_recv()
-
-    def drain(self):
-        for make in self.started:
-            make().wait_send()
+        for k in range(PLANES):
+            blk = self.block(p.coming(k), 1 - p.core)
+            self.copy(blk, blk, 20 + k, (p.z, p.sib)).wait_recv()
 
 
 def build_own(place, shard, land, own):
@@ -199,8 +226,10 @@
             shapes += [pltpu.VMEM((rows, cols), jnp.float32), pltpu.VMEM((rows // 2, cols), jnp.float32)]
         return shapes
 
+    def chip(self, back, spot):
+        return 4 * self.p.plane(back) + spot
+
     cut = Gather.cut
-    chip = Gather.chip
     copy = Gather.copy
     start = Gather.start
     drain = Gather.drain
@@ -331,7 +360,7 @@
     return (lane < HEAD_DIM) if h == 0 else (lane >= HEAD_DIM)
 
 
-def pair_forward(q2, k2, v2, text, bias):
+def pair_forward(q2, k2, v2, text, bias, between):
     vt = v2.T
     outs, logs = [], []
     for h in range(2):
@@ -342,10 +371,12 @@
         total = jnp.sum(expo, axis=0, keepdims=True)
         outs.append(dot(vt[HEAD_DIM * h : HEAD_DIM * (h + 1)], expo.astype(BF), NN) * (1.0 / total))
         logs.append(top + jnp.log(total))
+        if h == 0:
+            between()
     return jnp.concatenate(outs, axis=0).T.astype(BF), logs
 
 
-def pair_backward(q2, k2, v2, o2, do2, logs, text, bias):
+def pair_backward(q2, k2, v2, o2, do2, logs, text, bias, between):
     prod = (do2.astype(F) * o2.astype(F)).T
     kt = (k2 * BF(scale)).T
     dq, dk, dv = [], [], []
@@ -359,6 +390,8 @@
         dv.append(dot(probs.astype(BF), do2, NN))
         dk.append(dot(grads, q2, NN))
         dq.append(dot(kt[rows], grads, NN))
+        if h == 0:
+            between()
     first = head_lanes(0)
     return (
         jnp.concatenate(dq, axis=0).T.astype(BF),
@@ -367,19 +400,18 @@
     )
 
 
-def member_of(align, axis, segs):
-    shape = (segs, align.shape[1]) if axis == 0 else (align.shape[0], segs)
-    return (align == lax.broadcasted_iota(jnp.int32, shape, axis)).astype(F)
+def member_of(align, segs):
+    return (align == lax.broadcasted_iota(jnp.int32, (segs, align.shape[1]), 0)).astype(F)
 
 
 def forward_body(b, j, len_ref, tok_ref, al_ref, w_cols, bias_ref, outs, low_s, hook=lambda at: None):
     base_ref, low_ref, q_ref, k_ref, v_ref, att_ref, lse_ref = outs
-    text, width = al_ref.shape[2], tok_ref.shape[2]
+    text, width = al_ref.shape[1], tok_ref.shape[2]
     segs = tok_ref.shape[1] - text
 
     @pl.when(j == 0)
     def _():
-        member = member_of(al_ref[0], 0, segs)
+        member = member_of(al_ref[pl.ds(b, 1), :], segs)
         counts = jnp.maximum(jnp.sum(member, axis=1, keepdims=True), 1.0)
         tok = tok_ref[0]
         pooled = dot(member.astype(BF), tok[:text], NN) / counts
@@ -407,11 +439,11 @@
     bias = key_bias(len_ref[b])
     for pr in range(2):
         cols = slice(128 * pr, 128 * pr + 128)
-        out, logs = pair_forward(parts[0][:, cols], parts[1][:, cols], parts[2][:, cols], text, bias)
+        out, logs = pair_forward(parts[0][:, cols], parts[1][:, cols], parts[2][:, cols], text, bias, lambda: hook(1 + 2 * pr))
         att_ref[0, :, cols] = out
         for h in range(2):
             lse_ref[0, 0, 2 * pr + h : 2 * pr + h + 1, :] = logs[h]
-        hook(1 + pr)
+        hook(2 + 2 * pr)
 
 
 def forward_kernel(len_ref, tok_ref, al_ref, w_ref, bias_ref, *rest):
@@ -421,7 +453,6 @@
 
 def forward_attention(seg_lengths, tokens, alignment, w0, biases):
     docs, slots, width = tokens.shape
-    text = alignment.shape[1]
     quads = width // QUAD
     doc = pl.BlockSpec((1, slots, width), lambda b, j: (b, 0, 0))
     quad = pl.BlockSpec((1, slots, QUAD), lambda b, j: (b, 0, j))
@@ -432,7 +463,7 @@
         in_specs=[
             SMEM,
             doc,
-            pl.BlockSpec((1, 1, text), lambda b, j: (b, 0, 0)),
+            once(alignment.shape, lambda b, j: (0, 0)),
             once(w0.shape, lambda b, j: (0, 0)),
             once(biases.shape, lambda b, j: (0, 0)),
         ],
@@ -448,7 +479,7 @@
         ],
         scratch_shapes=[pltpu.VMEM((slots, width), BF)],
         compiler_params=pltpu.CompilerParams(vmem_limit_bytes=LIMIT),
-    )(seg_lengths, tokens, alignment[:, None, :], w0, biases)
+    )(seg_lengths, tokens, alignment, w0, biases)
 
 
 def normal_parts(pre):
@@ -482,15 +513,59 @@
     return jnp.sum(values, axis=0, keepdims=True)
 
 
+def mlp_first(att, base, w_out, w_in, vec, inner_bias, put, ff_cut=768, hook=lambda at: None):
+    first = base + dot(att, w_out(), NN) + vec(2)
+    hat, inv = norm_parts(first)
+    low = (hat * vec(3) + vec(4)).astype(BF)
+    put("norm", hat, inv, low)
+    chunks = inner_bias.shape[1] // ff_cut
+    pre_of = lambda c: dot(low, w_in(c * ff_cut, ff_cut), NN) + inner_bias[:, c * ff_cut : (c + 1) * ff_cut]
+    pre = pre_of(0)
+    for c in range(chunks):
+        later = pre_of(c + 1) if c + 1 < chunks else None
+        phi, dens = normal_parts(pre)
+        put("act", slice(c * ff_cut, (c + 1) * ff_cut), (pre * phi).astype(BF), (phi + pre * dens).astype(BF))
+        pre = later
+        hook(1 + c)
+
+
+def mlp_second(hat1, act, w_outer, cot, vec, ff_cut=768):
+    second = hat1 * vec(3) + vec(4) + vec(5)
+    for c in range(act.shape[1] // ff_cut):
+        second = second + dot(act[:, c * ff_cut : (c + 1) * ff_cut], w_outer(c * ff_cut, ff_cut), NN)
+    hat, inv = norm_parts(second)
+    grad_y = cot.astype(F)
+    sums = (col_sum(grad_y * hat), col_sum(grad_y))
+    return (hat * vec(6) + vec(7)).astype(BF), norm_back(grad_y * vec(6), hat, inv), sums
+
+
+def mlp_back(grad_second, gmlp, hat1, inv1, slope, w_outer, w_out, w_in, vec, put, ff_cut=768, hook=lambda at: None):
+    grad_normed = grad_second
+    chunks = slope.shape[1] // ff_cut
+    act_of = lambda c: dot(gmlp, w_outer(c * ff_cut, ff_cut), NT)
+    gact = act_of(0)
+    for c in range(chunks):
+        later = act_of(c + 1) if c + 1 < chunks else None
+        cols = slice(c * ff_cut, (c + 1) * ff_cut)
+        gpre = (gact * slope[:, cols].astype(F)).astype(BF)
+        put("pre", cols, gpre)
+        grad_normed = grad_normed + dot(gpre, w_in(c * ff_cut, ff_cut), NT)
+        gact = later
+        if c == 1:
+            hook(1)
+    grad_first = norm_back(grad_normed * vec(3), hat1, inv1)
+    low = grad_first.astype(BF)
+    put("first", grad_first, low, col_sum(grad_normed * hat1), col_sum(grad_normed))
+    return dot(low, w_out(), NT).astype(BF)
+
+
 def mlp_kernel(
-    tiles, ff_cut, att_ref, base_ref, cot_ref, w1_ref, w2_ref, vec_ref, ib_ref,
+    tiles, att_ref, base_ref, cot_ref, w1_ref, w2_ref, vec_ref, ib_ref,
     enc_ref, gf_ref, ga_ref, g1_ref, g2_ref, gv_ref, gib_ref,
     att_s, norm_s, act_s, slope_s, gmlp_s, gpre_s, gbr_s,
 ):
     i = pl.program_id(0)
     rows, width = att_ref.shape
-    ff = ib_ref.shape[1]
-    chunks = ff // ff_cut
 
     @pl.when(i == 0)
     def _():
@@ -501,47 +576,36 @@
     def _():
         at = pl.ds(pl.multiple_of(i * rows, rows), rows)
         vec = lambda k: vec_ref[k : k + 1, :]
-        att = att_ref[...]
-        att_s[at] = att
-        first = base_ref[...] + dot(att, w1_ref[:, :width], NN) + vec(2)
-        first_hat, first_inv = norm_parts(first)
-        normed = first_hat * vec(3) + vec(4)
-        norm_low = normed.astype(BF)
-        norm_s[at] = norm_low
-        second = normed + vec(5)
-        for c in range(chunks):
-            cols = slice(c * ff_cut, (c + 1) * ff_cut)
-            pre = dot(norm_low, w1_ref[:, width + c * ff_cut : width + (c + 1) * ff_cut], NN) + ib_ref[:, cols]
-            phi, dens = normal_parts(pre)
-            act = (pre * phi).astype(BF)
-            act_s[at, cols] = act
-            slope_s[:, cols] = (phi + pre * dens).astype(BF)
-            second = second + dot(act, w2_ref[cols, :], NN)
-        hat, inv = norm_parts(second)
-        enc_ref[...] = (hat * vec(6) + vec(7)).astype(BF)
-        grad_y = cot_ref[...].astype(F)
-        grad_second = norm_back(grad_y * vec(6), hat, inv)
+        w_out = lambda: w1_ref[:, :width]
+        w_in = lambda c, n: w1_ref[:, width + c : width + c + n]
+        w_outer = lambda c, n: w2_ref[c : c + n, :]
+        kept = {}
+
+        def put(kind, *got):
+            if kind == "norm":
+                kept["hat"], kept["inv"], norm_s[at] = got
+            elif kind == "act":
+                act_s[at, got[0]], slope_s[:, got[0]] = got[1:]
+            elif kind == "pre":
+                gpre_s[at, got[0]] = got[1]
+                gib_ref[:, got[0]] += col_sum(got[1].astype(F))
+            else:
+                gf_ref[...], gbr_s[at] = got[:2]
+                gv_ref[2:3] += col_sum(got[1].astype(F))
+                gv_ref[3:4] += got[2]
+                gv_ref[4:5] += got[3]
+
+        att_s[at] = att_ref[...]
+        mlp_first(att_ref[...], base_ref[...], w_out, w_in, vec, ib_ref[...], put)
+        enc_ref[...], grad_second, sums = mlp_second(kept["hat"], act_s[at], w_outer, cot_ref[...], vec)
         gmlp = grad_second.astype(BF)
         gmlp_s[at] = gmlp
-        grad_normed = grad_second
-        for c in range(chunks):
-            cols = slice(c * ff_cut, (c + 1) * ff_cut)
-            gact = dot(gmlp, w2_ref[cols, :], NT)
-            gpre = (gact * slope_s[:, cols].astype(F)).astype(BF)
-            gpre_s[at, cols] = gpre
-            gib_ref[:, cols] += col_sum(gpre.astype(F))
-            grad_normed = grad_normed + dot(gpre, w1_ref[:, width + c * ff_cut : width + (c + 1) * ff_cut], NT)
-        grad_first = norm_back(grad_normed * vec(3), first_hat, first_inv)
-        gf_ref[...] = grad_first
-        gbr = grad_first.astype(BF)
-        gbr_s[at] = gbr
-        ga_ref[...] = dot(gbr, w1_ref[:, :width], NT).astype(BF)
-        gv_ref[2:3] += col_sum(gbr.astype(F))
-        gv_ref[3:4] += col_sum(grad_normed * first_hat)
-        gv_ref[4:5] += col_sum(grad_normed)
         gv_ref[5:6] += col_sum(gmlp.astype(F))
-        gv_ref[6:7] += col_sum(grad_y * hat)
-        gv_ref[7:8] += col_sum(grad_y)
+        gv_ref[6:7] += sums[0]
+        gv_ref[7:8] += sums[1]
+        ga_ref[...] = mlp_back(
+            grad_second, gmlp, kept["hat"], kept["inv"], slope_s[...], w_outer, w_out, w_in, vec, put
+        )
 
     @pl.when((i >= tiles) & (i < tiles + 4))
     def _():
@@ -558,14 +622,14 @@
         g1_ref[...] = dot(att_s[...], gbr_s[...], TN).astype(BF)
 
 
-def mlp_both(attended, base, cotangent, w1, w2, vec, inner_bias, rows=320, ff_cut=768):
+def mlp_both(attended, base, cotangent, w1, w2, vec, inner_bias, rows=320):
     total, width = attended.shape
     ff = inner_bias.shape[1]
     tiles = total // rows
     tile = pl.BlockSpec((rows, width), lambda i: (jnp.minimum(i, tiles - 1), 0))
     whole = lambda shape: once(shape, lambda i: (0, 0))
     return pl.pallas_call(
-        functools.partial(mlp_kernel, tiles, ff_cut),
+        functools.partial(mlp_kernel, tiles),
         grid=(tiles + 9,),
         in_specs=[tile, tile, tile, whole(w1.shape), whole(w2.shape), whole(vec.shape), whole(inner_bias.shape)],
         out_specs=[
@@ -600,11 +664,12 @@
 
 
 def backward_body(j, b, refs, keep, gt_ref, scratch, hook=lambda at: None):
-    len_ref, al_ref, q_ref, k_ref, v_ref, o_ref, do_ref, lse_ref, low_ref, gf_ref, w_ref, vec_ref = refs
+    len_ref, al_ref, q_ref, k_ref, v_ref, o_ref, do_ref, lse_ref, low_ref, gf_ref, w_ref = refs
     gbase_s, acc_s, vsum_s = scratch
     text, width = al_ref.shape[1], low_ref.shape[2]
     segs = low_ref.shape[1] - text
     quads = width // QUAD
+    align = al_ref[pl.ds(b, 1), :]
 
     hook(0)
     bias = key_bias(len_ref[b])
@@ -613,12 +678,13 @@
         cols = slice(128 * pr, 128 * pr + 128)
         logs = [lse_ref[0, 0, 2 * pr + h : 2 * pr + h + 1, :] for h in range(2)]
         got = pair_backward(
-            q_ref[0, :, cols], k_ref[0, :, cols], v_ref[0, :, cols], o_ref[0, :, cols], do_ref[0, :, cols], logs, text, bias
+            q_ref[0, :, cols], k_ref[0, :, cols], v_ref[0, :, cols], o_ref[0, :, cols], do_ref[0, :, cols], logs, text, bias,
+            lambda: hook(1 + 2 * pr),
         )
         for i in range(3):
             parts[i].append(got[i])
         if pr == 0:
-            hook(1)
+            hook(2)
     quad_grads = [jnp.concatenate(p, axis=1) for p in parts]
     cols = pl.ds(pl.multiple_of(j * QUAD, QUAD), QUAD)
 
@@ -651,42 +717,41 @@
 
     @pl.when(j == quads - 1)
     def _():
-        member = member_of(al_ref[0], 1, segs)
-        counts = jnp.maximum(jnp.sum(member, axis=0, keepdims=True), 1.0)
-        share = gbase[text:] / counts.T
+        member = member_of(align, segs)
+        counts = jnp.maximum(jnp.sum(member, axis=1, keepdims=True), 1.0)
+        share = gbase[text:] / counts
         high = share.astype(BF)
         rest = (share - high.astype(F)).astype(BF)
         sel = member.astype(BF)
-        spread = dot(sel, high, NN) + dot(sel, rest, NN)
+        spread = dot(sel, high, TN) + dot(sel, rest, TN)
         gt_ref[0, :text] = (gbase[:text] + spread).astype(BF)
         gt_ref[0, text:] = gbase[text:].astype(BF)
 
-    hook(2)
-
-
-def vector_cols(vsum_s, vec_ref):
-    lane = lax.broadcasted_iota(jnp.int32, (1, 128), 1)
-    pad = jnp.zeros((120, vsum_s.shape[1]), F)
-    return (jnp.where(lane < 2, jnp.concatenate([vsum_s[...], pad], axis=0).T, 0.0) + vec_ref[...]).astype(BF)
+    hook(4)
+
+
+def vector_cols(vsum_s, gv_ref, gib_ref, cols_s):
+    width = gv_ref.shape[1]
+    rows = jnp.concatenate([vsum_s[:2], gv_ref[2:], jnp.zeros((120, width), F)], axis=0)
+    cols_s[...] = jnp.zeros_like(cols_s)
+    share = gib_ref.shape[1] * 24 // width
+    for d in range(width // 24):
+        cols_s[24 * d : 24 * d + 1, :share] = gib_ref[:, d * share : (d + 1) * share]
+    return jnp.concatenate([rows.T, cols_s[...]], axis=1).astype(BF)
 
 
 def backward_kernel(*refs):
-    gvec_ref, gt_ref = refs[15:17]
+    vsum_ref, gt_ref = refs[14:16]
 
     def keep(grad):
         for i in range(3):
-            refs[12 + i][...] = grad(i)
-
-        @pl.when(pl.program_id(0) == pl.num_programs(0) - 1)
-        def _():
-            gvec_ref[...] = vector_cols(refs[19], refs[11])
-
-    backward_body(pl.program_id(0), pl.program_id(1), refs[:12], keep, gt_ref, refs[17:])
-
-
-def backward_attention(seg_lengths, alignment, q, k, v, att, gatt, lse, low, gfirst, w0, vec):
+            refs[11 + i][...] = grad(i)
+
+    backward_body(pl.program_id(0), pl.program_id(1), refs[:11], keep, gt_ref, [refs[16], refs[17], vsum_ref])
+
+
+def backward_attention(seg_lengths, alignment, q, k, v, att, gatt, lse, low, gfirst, w0):
     docs, slots, width = low.shape
-    text = alignment.shape[1]
     quads = width // QUAD
     quad = pl.BlockSpec((1, slots, QUAD), lambda j, b: (b, 0, j))
     doc = pl.BlockSpec((1, slots, width), lambda j, b: (b, 0, 0))
@@ -697,7 +762,7 @@
         grid=(quads, docs),
         in_specs=[
             SMEM,
-            pl.BlockSpec((1, text, 1), lambda j, b: (b, 0, 0)),
+            once(alignment.shape, lambda j, b: (0, 0)),
             quad,
             quad,
             quad,
@@ -707,23 +772,21 @@
             doc,
             pl.BlockSpec((1, slots, width), lambda j, b: (jnp.where(j == 0, b, 1), 0, 0)),
             once(w0.shape, lambda j, b: (0, 0)),
-            once(vec.shape, lambda j, b: (0, 0)),
         ],
         out_specs=[
             col,
             col,
             col,
-            once((width, 128), lambda j, b: (0, 0)),
+            once((8, width), lambda j, b: (0, 0)),
             pl.BlockSpec((1, slots, width), lambda j, b: (jnp.where(j == quads - 1, b, 0), 0, 0)),
         ],
-        out_shape=[wide, wide, wide, jax.ShapeDtypeStruct((width, 128), BF), jax.ShapeDtypeStruct((docs, slots, width), BF)],
+        out_shape=[wide, wide, wide, jax.ShapeDtypeStruct((8, width), F), jax.ShapeDtypeStruct((docs, slots, width), BF)],
         scratch_shapes=[
             pltpu.VMEM((docs, slots, width), F),
             pltpu.VMEM((3, width, QUAD), F),
-            pltpu.VMEM((8, width), F),
         ],
         compiler_params=pltpu.CompilerParams(vmem_limit_bytes=LIMIT),
-    )(seg_lengths, alignment[:, :, None], q, k, v, att, gatt, lse, low, gfirst, w0, vec)
+    )(seg_lengths, alignment, q, k, v, att, gatt, lse, low, gfirst, w0)
 
 
 def at_slots(plan, step, slot):
@@ -740,109 +803,363 @@
     return [functools.partial(fn, k) for k in backs]
 
 
+TILE = 320
+ATTEND = 6
+
+
 def forward_fused_kernel(
-    len_ref, tok_ref, al_ref, s0, s1, s2, *rest
+    len_ref, tok_ref, al_ref, wq, wk, wv, wo, wi, s2, vp, *rest
 ):
-    outs, (w0, w1, w2) = rest[:7], rest[7:10]
-    low_s, w0_s, bias_s, land0, land1, own0, own1, pair_sem, local, send, recv = rest[10:]
-    b, j = pl.program_id(0), pl.program_id(1)
-    quads = pl.num_programs(1)
-    step = b * quads + j
+    low_ref, q_ref, k_ref, v_ref, att_ref, lse_ref = rest[:6]
+    hat_ref, inv_ref, norm_ref, act_ref, slope_ref, vec_ref, w0, w1, w2 = rest[6:15]
+    (
+        low_s, base_s, att_s, w0_s, w1_s, ib_s, cols_s, s0, s1, land0, land1, own0, own1, pair_sem, local, send, recv,
+    ) = rest[15:]
+    step = pl.program_id(0)
+    width, ff = tok_ref.shape[2], wi.shape[1]
     place = Place()
     pairs = [
         Pair(place, s0, land0, own0, pair_sem.at[0], pair_sem.at[1]),
         Pair(place, s1, land1, own1, pair_sem.at[2], pair_sem.at[3]),
     ]
     g0 = Gather(place, w0_s, own0, send.at[0], recv.at[0], local.at[0], w0.shape[2])
-    g1 = Gather(place, w1, own1, send.at[1], recv.at[1], local.at[1], w1.shape[2])
+    g1 = Gather(place, w1_s, own1, send.at[1], recv.at[1], local.at[1], w1.shape[2])
     g2 = Gather(place, w2, s2, send.at[2], recv.at[2], local.at[2])
-    width = tok_ref.shape[2]
-    save = lambda: pltpu.make_async_copy(w0_s, w0, local.at[3])
-
-    def bias_rows():
-        vec = w0_s[:, :, 3 * width : 3 * width + 128].reshape(width, 128).astype(F)
-        bias_s[...] = vec.T[:8]
-
-    plan = {
+    saves = [
+        lambda: pltpu.make_async_copy(w0_s, w0, local.at[3]),
+        lambda: pltpu.make_async_copy(w1_s, w1, local.at[4]),
+    ]
+    start_of = lambda k: lambda: saves[k]().start()
+    wait_of = lambda k: lambda: saves[k]().wait()
+
+    def pack():
+        for i, ref in enumerate((wq, wk, wv)):
+            s0[:, i * width : (i + 1) * width] = ref[...].astype(F)
+        rows = jnp.concatenate([vp[:8], jnp.zeros((120, 128), F)], axis=0)
+        s0[:, 3 * width : 3 * width + 128] = rows.T[:24]
+        top = lax.broadcasted_iota(jnp.int32, (24, 1), 0) == 0
+        s0[:, 3 * width + 128 :] = jnp.where(top, vp[8:9], 0.0)
+
+    def pack_rest():
+        s1[:, :width] = wo[...].astype(F)
+        s1[:, width:] = wi[...].astype(F)
+
+    def vectors():
+        cols = w0_s[:, :, 3 * width : 3 * width + 128].reshape(width, 128).astype(F)
+        vec_ref[...] = cols.T[:8]
+        cols_s[...] = w0_s[:, :, 3 * width + 128 :].reshape(width, 128).astype(F)
+        share = ff * 24 // width
+        for d in range(width // 24):
+            ib_s[:, d * share : (d + 1) * share] = cols_s[24 * d : 24 * d + 1, :share]
+
+    attend_plan = {
         (0, -1): [
-            place.barrier, pairs[0].start, pairs[1].start, pairs[0].done, g0.along_z,
-            functools.partial(g0.to_neighbours, 0), pairs[1].done, g1.along_z, g2.along_z,
+            pack, place.barrier, pairs[0].start, pack_rest, pairs[1].start, pairs[0].done, g0.along_z,
+            functools.partial(g0.to_neighbours, 0), pairs[1].done,
         ],
         (0, 0): [
-            *each(g0.to_neighbours, 1, 2, 3), *each(g0.to_diagonal, 0), *each(g1.to_neighbours, 0),
-            *each(g0.to_diagonal, 1, 2, 3), *each(g1.to_neighbours, 1, 2, 3), *each(g0.to_core, 0, 1, 2, 3),
-            *each(g2.to_neighbours, 0, 1), g0.finish, save().start, bias_rows,
-        ],
-        (0, 1): each(g1.to_diagonal, 0, 1),
-        (0, 2): [*each(g1.to_diagonal, 2), *each(g2.to_neighbours, 2, 3)],
-        (1, 1): [*each(g1.to_diagonal, 3), *each(g1.to_core, 0)],
-        (1, 2): each(g1.to_core, 1),
-        (2, 1): [*each(g2.to_diagonal, 0), *each(g1.to_core, 2)],
-        (2, 2): [*each(g2.to_diagonal, 1), *each(g1.to_core, 3)],
-        (3, 1): each(g2.to_diagonal, 2),
-        (3, 2): each(g2.to_diagonal, 3),
-        (4, 1): each(g2.to_core, 0),
-        (4, 2): each(g2.to_core, 1),
-        (5, 2): [
-            *each(g2.to_core, 2, 3), g1.finish, g2.finish, lambda: save().wait(), g0.drain, g1.drain, g2.drain,
-        ],
+            *each(g0.to_neighbours, 1), *each(g0.to_diagonal, 0), *each(g0.to_neighbours, 2), *each(g0.to_diagonal, 1),
+            *each(g0.to_neighbours, 3), g1.along_z, *each(g0.to_core, 0), *each(g0.to_diagonal, 2),
+            *each(g1.to_neighbours, 0), *each(g0.to_core, 1), *each(g0.to_diagonal, 3), *each(g0.to_core, 2, 3),
+            *each(g1.to_neighbours, 1), g0.finish, start_of(0), vectors,
+        ],
+        (0, 1): [*each(g1.to_diagonal, 0), *each(g1.to_neighbours, 2)],
+        (0, 2): each(g1.to_diagonal, 1),
+        (0, 4): each(g1.to_neighbours, 3),
+        (1, 1): each(g1.to_diagonal, 2),
+        (1, 2): each(g1.to_core, 0),
+        (1, 4): [*each(g1.to_diagonal, 3), *each(g1.to_core, 1)],
+        (2, 2): each(g1.to_core, 2),
+        (2, 4): [g2.along_z, *each(g1.to_core, 3)],
+        (3, 1): each(g2.to_neighbours, 0),
+        (3, 3): each(g2.to_neighbours, 1),
+        (4, 1): [*each(g2.to_neighbours, 2), *each(g2.to_diagonal, 0)],
+        (4, 3): each(g2.to_diagonal, 1),
+        (5, 1): each(g2.to_neighbours, 3),
+        (5, 3): each(g2.to_diagonal, 2),
     }
-    at_slots(plan, step, -1)
-    w_cols = lambda cols: w0_s[:, :, cols].reshape(width, QUAD)
-    forward_body(
-        b, j, len_ref, tok_ref, al_ref, w_cols, bias_s, outs, low_s, functools.partial(at_slots, plan, step)
-    )
-
-
-def forward_fused(seg_lengths, tokens, alignment, s0, s1, s2):
+    mlp_plan = {
+        (6, 0): [g1.finish, start_of(1)],
+        (6, 1): each(g2.to_core, 0),
+        (6, 3): each(g2.to_core, 1),
+        (7, 1): each(g2.to_diagonal, 3),
+        (7, 3): each(g2.to_core, 2),
+        (8, 1): each(g2.to_core, 3),
+        (9, 5): [g2.finish, wait_of(0), wait_of(1), g0.drain, g1.drain, g2.drain],
+    }
+
+    @pl.when(step < ATTEND)
+    def _():
+        at_slots(attend_plan, step, -1)
+        b, j = step // 3, step % 3
+        outs = (base_s.at[pl.ds(b, 1)], low_ref, q_ref, k_ref, v_ref, att_ref, lse_ref)
+        w_cols = lambda cols: w0_s[:, :, cols].reshape(width, QUAD)
+        hook = functools.partial(at_slots, attend_plan, step)
+        forward_body(b, j, len_ref, tok_ref, al_ref, w_cols, vec_ref, outs, low_s, hook)
+        att_s[b, :, pl.ds(pl.multiple_of(j * QUAD, QUAD), QUAD)] = att_ref[0]
+
+    @pl.when(step >= ATTEND)
+    def _():
+        hook = functools.partial(at_slots, mlp_plan, step)
+        hook(0)
+        t = step - ATTEND
+        rows = pl.ds(pl.multiple_of((t % 2) * TILE, TILE), TILE)
+
+        def put(kind, *got):
+            if kind == "norm":
+                hat_ref[...] = got[0]
+                inv_ref[...] = jnp.broadcast_to(got[1], inv_ref.shape)
+                norm_ref[...] = got[2]
+            else:
+                act_ref[:, got[0]], slope_ref[:, got[0]] = got[1:]
+
+        w_out = lambda: w1_s[:, :, :width].reshape(width, width)
+        w_in = lambda c, n: w1_s[:, :, width + c : width + c + n].reshape(width, n)
+        vec = lambda k: vec_ref[k : k + 1, :]
+        mlp_first(att_s[t // 2, rows], base_s[t // 2, rows], w_out, w_in, vec, ib_s[...], put, hook=hook)
+        hook(5)
+
+
+def forward_fused(seg_lengths, tokens, alignment, wq, wk, wv, wo, wi, s2, vp):
     docs, slots, width = tokens.shape
-    text = alignment.shape[1]
+    ff = wi.shape[1]
     quads = width // QUAD
-    n0, n1 = s0.shape[1], s1.shape[1]
-    doc = pl.BlockSpec((1, slots, width), lambda b, j: (b, 0, 0))
-    quad = pl.BlockSpec((1, slots, QUAD), lambda b, j: (b, 0, j))
+    n0, n1 = 3 * width + 256, width + ff
+    total = docs * slots
+    last = ATTEND - 1
+    doc_of = lambda s: jnp.minimum(s, last) // quads
+    doc = pl.BlockSpec((1, slots, width), lambda s: (doc_of(s), 0, 0))
+    quad = pl.BlockSpec((1, slots, QUAD), lambda s: (doc_of(s), 0, jnp.minimum(s, last) % quads))
     wide = jax.ShapeDtypeStruct((docs, slots, width), BF)
-    full = lambda a: once(a.shape, lambda b, j: (0, 0))
+    full = lambda *shape: once(shape, lambda s: (0,) * len(shape))
+    tile = lambda n: pl.BlockSpec((TILE, n), lambda s: (jnp.maximum(s - ATTEND, 0), 0))
+    ins = (alignment, wq, wk, wv, wo, wi, s2, vp)
     return pl.pallas_call(
         forward_fused_kernel,
-        grid=(docs, quads),
-        in_specs=[SMEM, doc, pl.BlockSpec((1, 1, text), lambda b, j: (b, 0, 0)), full(s0), full(s1), full(s2)],
-        out_specs=[doc, doc, quad, quad, quad, quad, pl.BlockSpec((1, 1, 8, slots), lambda b, j: (b, j, 0, 0))]
+        grid=(ATTEND + total // TILE,),
+        in_specs=[SMEM, doc] + [full(*a.shape) for a in ins],
+        out_specs=[
+            doc, quad, quad, quad, quad,
+            pl.BlockSpec((1, 1, 8, slots), lambda s: (doc_of(s), jnp.minimum(s, last) % quads, 0, 0)),
+            tile(width), tile(128), tile(width), tile(ff), tile(ff), full(8, width),
+        ]
         + [ANY] * 3,
         out_shape=[
-            jax.ShapeDtypeStruct((docs, slots, width), F),
             wide,
             wide,
             wide,
             wide,
             wide,
             jax.ShapeDtypeStruct((docs, quads, 8, slots), F),
+            jax.ShapeDtypeStruct((total, width), F),
+            jax.ShapeDtypeStruct((total, 128), F),
+            jax.ShapeDtypeStruct((total, width), BF),
+            jax.ShapeDtypeStruct((total, ff), BF),
+            jax.ShapeDtypeStruct((total, ff), BF),
+            jax.ShapeDtypeStruct((8, width), F),
             jax.ShapeDtypeStruct((CHIPS, 48, n0), BF),
             jax.ShapeDtypeStruct((CHIPS, 48, n1), BF),
             jax.ShapeDtypeStruct((CHIPS, 2, 96, width), BF),
         ],
         scratch_shapes=[
             pltpu.VMEM((slots, width), BF),
+            pltpu.VMEM((docs, slots, width), F),
+            pltpu.VMEM((docs, slots, width), BF),
             pltpu.VMEM((CHIPS, 48, n0), BF),
-            pltpu.VMEM((8, width), F),
+            pltpu.VMEM((CHIPS, 48, n1), BF),
+            pltpu.VMEM((1, ff), F),
+            pltpu.VMEM((width, 128), F),
+            pltpu.VMEM((24, n0), F),
+            pltpu.VMEM((24, n1), F),
             pltpu.VMEM((24, n0 // 2), F),
             pltpu.VMEM((24, n1 // 2), F),
             pltpu.VMEM((48, n0 // 2), BF),
             pltpu.VMEM((48, n1 // 2), BF),
             pltpu.SemaphoreType.DMA((4,)),
-            pltpu.SemaphoreType.DMA((4,)),
+            pltpu.SemaphoreType.DMA((5,)),
             pltpu.SemaphoreType.DMA((3, Gather.SEMS)),
             pltpu.SemaphoreType.DMA((3, Gather.SEMS)),
         ],
         compiler_params=pltpu.CompilerParams(collective_id=0, has_side_effects=True, vmem_limit_bytes=LIMIT),
-    )(seg_lengths, tokens, alignment[:, None, :], s0, s1, s2)
+    )(seg_lengths, tokens, *ins)
+
+
+def middle_kernel(hat_ref, inv_ref, cot_ref, vec_ref, *rest):
+    act_h, slope_h, norm_h, att_h, w1_h, w2_h = rest[:6]
+    enc_ref, gf_ref, ga_ref, g1_ref, gv_ref, gib_ref, o_outer = rest[6:13]
+    act_s, slope_s, w1_s, w2_s, gsec_s, gmlp_s, g2_s = rest[13:20]
+    bufs = rest[20:27]
+    load_sem, local, send, recv = rest[27:]
+    i = pl.program_id(0)
+    rows, width = hat_ref.shape
+    norm_s, att_s, gbr_s = (act_s.at[:, pl.ds(k * width, width)] for k in range(3))
+    tiles = act_s.shape[0] // rows
+    place = Place()
+    g2 = Scatter(place, g2_s, bufs, o_outer, send.at[0], recv.at[0], local.at[0])
+
+    cut = lambda t: pl.ds(t * rows, rows)
+    loads = [lambda: pltpu.make_async_copy(w2_h, w2_s, load_sem.at[0])]
+    for t in range(tiles):
+        loads.append(lambda t=t: pltpu.make_async_copy(act_h.at[cut(t)], act_s.at[cut(t)], load_sem.at[1 + t]))
+    for t in range(tiles):
+        loads.append(lambda t=t: pltpu.make_async_copy(slope_h.at[cut(t)], slope_s.at[cut(t)], load_sem.at[5 + t]))
+    loads += [
+        lambda: pltpu.make_async_copy(w1_h, w1_s, load_sem.at[9]),
+        lambda: pltpu.make_async_copy(norm_h, norm_s, load_sem.at[10]),
+        lambda: pltpu.make_async_copy(att_h, att_s, load_sem.at[11]),
+    ]
+    wait = lambda k: lambda: loads[k]().wait()
+    loads_start = lambda k: lambda: loads[k]().start()
+
+    def begin():
+        for load in loads[:2]:
+            load().start()
+        gv_ref[...] = jnp.zeros_like(gv_ref)
+        gib_ref[...] = jnp.zeros_like(gib_ref)
+        place.barrier()
+
+    plan = {
+        (0, 0): [begin, wait(0), wait(1), *map(loads_start, (2, 3, 4))],
+        (1, 0): [wait(2), *map(loads_start, (9, 5))],
+        (2, 0): [wait(3), *map(loads_start, (6, 7, 8))],
+        (3, 0): [wait(4)],
+        (4, 2): each(g2.from_sibling, 3),
+        (5, 2): each(g2.from_sibling, 2),
+        (6, 2): each(g2.from_sibling, 1),
+        (7, 2): each(g2.from_sibling, 0),
+        (6, 0): each(g2.to_diagonal, 3),
+        (7, 0): each(g2.to_diagonal, 2),
+        (8, 0): [loads_start(10), loads_start(11), wait(9), wait(5), *each(g2.to_diagonal, 1)],
+        (8, 1): [*each(g2.to_diagonal, 0), *each(g2.to_neighbours, 3)],
+        (8, 2): each(g2.to_neighbours, 2),
+        (9, 0): [wait(6)],
+        (9, 1): each(g2.to_neighbours, 1),
+        (9, 2): each(g2.to_neighbours, 0),
+        (10, 0): [wait(7)],
+        (10, 1): each(g2.along_z, 3),
+        (10, 2): each(g2.along_z, 2),
+        (11, 0): [wait(8)],
+        (11, 2): each(g2.along_z, 1),
+        (12, 0): [wait(10)],
+        (12, 2): each(g2.along_z, 0),
+        (16, 0): [wait(11)],
+        (16, 2): [g2.owner, g2.drain],
+    }
+    hook = functools.partial(at_slots, plan, i)
+    hook(0)
+    vec = lambda k: vec_ref[k : k + 1, :]
+    w_outer = lambda c, n: w2_s[c * CHIPS // act_s.shape[1] : (c + n) * CHIPS // act_s.shape[1]].reshape(n, width)
+
+    @pl.when(i < tiles)
+    def _():
+        at = pl.ds(pl.multiple_of(i * rows, rows), rows)
+        enc_ref[...], grad_second, sums = mlp_second(hat_ref[...], act_s[at], w_outer, cot_ref[...], vec)
+        gsec_s[at] = grad_second
+        gmlp = grad_second.astype(BF)
+        gmlp_s[at] = gmlp
+        gv_ref[5:6] += col_sum(gmlp.astype(F))
+        gv_ref[6:7] += sums[0]
+        gv_ref[7:8] += sums[1]
+
+    @pl.when((i >= tiles) & (i < 2 * tiles))
+    def _():
+        plane = place.plane(2 * tiles - 1 - i)
+        cols = pl.ds(pl.multiple_of(plane * width, width), width)
+        g2_s[pl.ds(4 * plane, 4)] = dot(act_s[:, cols], gmlp_s[...], TN).astype(BF).reshape(4, 2, 96, width)
+
+    @pl.when((i >= 2 * tiles) & (i < 3 * tiles))
+    def _():
+        at = pl.ds(pl.multiple_of((i - 2 * tiles) * rows, rows), rows)
+
+        def put(kind, *got):
+            if kind == "pre":
+                slope_s[at, got[0]] = got[1]
+                gib_ref[:, got[0]] += col_sum(got[1].astype(F))
+            else:
+                gf_ref[...], gbr_s[at] = got[:2]
+                gv_ref[2:3] += col_sum(got[1].astype(F))
+                gv_ref[3:4] += got[2]
+                gv_ref[4:5] += got[3]
+
+        w_out = lambda: w1_s[:, :, :width].reshape(width, width)
+        w_in = lambda c, n: w1_s[:, :, width + c : width + c + n].reshape(width, n)
+        ga_ref[...] = mlp_back(
+            gsec_s[at], gmlp_s[at], hat_ref[...], inv_ref[:, 0:1], slope_s[at], w_outer, w_out, w_in, vec, put, hook=hook
+        )
+
+    @pl.when((i >= 3 * tiles) & (i < 4 * tiles))
+    def _():
+        cols = pl.ds(pl.multiple_of((i - 3 * tiles) * width, width), width)
+        g1_ref[...] = dot(norm_s[...], slope_s[:, cols], TN).astype(BF)
+
+    @pl.when(i == 4 * tiles)
+    def _():
+        g1_ref[...] = dot(att_s[...], gbr_s[...], TN).astype(BF)
+
+    hook(2)
+
+
+def middle(hat, inv, cotangent, vec, act, slope, norm, att, w1, w2):
+    total, width = hat.shape
+    ff = act.shape[1]
+    tiles = total // TILE
+    early = lambda n: pl.BlockSpec((TILE, n), lambda i: (jnp.minimum(i, tiles - 1), 0))
+    late = lambda n: pl.BlockSpec((TILE, n), lambda i: (jnp.clip(i - 2 * tiles, 0, tiles - 1), 0))
+    full = lambda *shape: once(shape, lambda i: (0,) * len(shape))
+    return pl.pallas_call(
+        middle_kernel,
+        grid=(4 * tiles + 1,),
+        in_specs=[
+            pl.BlockSpec(
+                (TILE, width),
+                lambda i: (jnp.where(i < 2 * tiles, jnp.minimum(i, tiles - 1), jnp.minimum(i - 2 * tiles, tiles - 1)), 0),
+            ),
+            late(128),
+            early(width),
+            full(8, width),
+        ]
+        + [ANY] * 6,
+        out_specs=[
+            early(width),
+            late(width),
+            late(width),
+            pl.BlockSpec((width, width), lambda i: (0, jnp.where(i == 4 * tiles, 0, jnp.clip(i - 3 * tiles, 0, 3) + 1))),
+            full(8, width),
+            full(1, ff),
+            full(96, width),
+        ],
+        out_shape=[
+            jax.ShapeDtypeStruct((total, width), BF),
+            jax.ShapeDtypeStruct((total, width), F),
+            jax.ShapeDtypeStruct((total, width), BF),
+            jax.ShapeDtypeStruct((width, width + ff), BF),
+            jax.ShapeDtypeStruct((8, width), F),
+            jax.ShapeDtypeStruct((1, ff), F),
+            jax.ShapeDtypeStruct((96, width), F),
+        ],
+        scratch_shapes=[
+            pltpu.VMEM((total, ff), BF),
+            pltpu.VMEM((total, ff), BF),
+            pltpu.VMEM(w1.shape, BF),
+            pltpu.VMEM(w2.shape, BF),
+            pltpu.VMEM((total, width), F),
+            pltpu.VMEM((total, width), BF),
+            pltpu.VMEM(w2.shape, BF),
+            *Scatter.scratch(96, width, False),
+            pltpu.SemaphoreType.DMA((12,)),
+            pltpu.SemaphoreType.DMA((1, 4)),
+            pltpu.SemaphoreType.DMA((1, Scatter.SEMS)),
+            pltpu.SemaphoreType.DMA((1, Scatter.SEMS)),
+        ],
+        compiler_params=pltpu.CompilerParams(collective_id=2, has_side_effects=True, vmem_limit_bytes=LIMIT),
+    )(hat, inv, cotangent, vec, act, slope, norm, att, w1, w2)
 
 
 def backward_fused_kernel(widths, *refs):
-    ins, (g2_ref, g1_ref) = refs[:12], refs[12:14]
-    gt_ref, o_wide, o_inner, o_outer, o_vec = refs[14], refs[15:19], refs[19], refs[20], refs[21]
-    scratch = refs[22:25]
-    rest = list(refs[25:])
+    ins, (gv_ref, gib_ref, g1_ref) = refs[:11], refs[11:14]
+    gt_ref, o_wide, o_inner, o_vec, o_ib = refs[14], refs[15:19], refs[19], refs[20], refs[21]
+    scratch, cols_s = refs[22:25], refs[25]
+    rest = list(refs[26:])
     local, send, recv = rest[-3:]
     j, b = pl.program_id(0), pl.program_id(1)
     step = 2 * j + b
@@ -850,25 +1167,25 @@
     place = Place()
     take = lambda n: [rest.pop(0) for _ in range(n)]
     quad_s, stage = take(3), take(1)[0]
-    sources = [g2_ref, g1_ref, *quad_s]
+    sources = [g1_ref, *quad_s]
     groups = []
     for i, (src, wide) in enumerate(zip(sources, widths)):
-        bufs = take(7 if wide is None else 9)
-        out = o_outer if wide is None else stage.at[:, pl.ds(0, wide)]
-        groups.append(Scatter(place, src, bufs, out, send.at[i], recv.at[i], local.at[i], wide))
-    g2, g1, q0, q1, q2 = groups
+        out = stage.at[:, pl.ds(0, wide)]
+        groups.append(Scatter(place, src, take(9), out, send.at[i], recv.at[i], local.at[i], wide))
+    g1, q0, q1, q2 = groups
 
     def give_rest():
         g1.finish()
         o_wide[3][...] = stage[:, :width]
-        o_inner[...] = stage[:, width : widths[1]]
+        o_inner[...] = stage[:, width : widths[0]]
 
     def give_quad(k):
-        groups[2 + k].finish()
+        groups[1 + k].finish()
         for i in range(3):
             o_wide[i][:, k * QUAD : (k + 1) * QUAD] = stage[:, i * QUAD : (i + 1) * QUAD]
         if k == 2:
-            o_vec[...] = stage[:, 3 * QUAD : 3 * QUAD + 128]
+            o_vec[...] = stage[:, 3 * QUAD : 3 * QUAD + 128].T[:8]
+            o_ib[...] = stage[0:1, 3 * QUAD + 128 : 4 * QUAD]
 
     def keep(grad):
         for k in range(3):
@@ -878,47 +1195,45 @@
                 for i in range(3):
                     quad_s[k][:, :, i * QUAD : (i + 1) * QUAD] = grad(i).reshape(CHIPS, 48, QUAD)
                 if k == 2:
-                    vec = vector_cols(scratch[2], ins[11])
-                    both = jnp.concatenate([vec, jnp.zeros_like(vec)], axis=1)
+                    both = vector_cols(scratch[2], gv_ref, gib_ref, cols_s)
                     quad_s[k][:, :, 3 * QUAD :] = both.reshape(CHIPS, 48, QUAD)
 
     late, soon = (3, 2), (1, 0)
     all4 = late + soon
     plan = {
-        (0, 0): [place.barrier, *each(g2.from_sibling, *all4), *each(g1.from_sibling, *all4)],
-        (0, 1): each(g2.to_diagonal, *late),
-        (0, 2): [*each(g2.to_diagonal, *soon), *each(g1.to_diagonal, *late)],
-        (1, 1): [*each(g2.to_neighbours, *late), *each(g1.to_diagonal, *soon)],
-        (1, 2): [*each(g2.to_neighbours, *soon), *each(q0.from_sibling, *all4)],
-        (2, 1): [*each(g1.to_neighbours, *late), *each(g2.along_z, *late)],
-        (2, 2): [*each(g1.to_neighbours, *soon), *each(q0.to_diagonal, *all4), *each(g2.along_z, *soon)],
-        (3, 1): [*each(g1.along_z, *late)],
-        (3, 2): [*each(q0.to_neighbours, *all4), *each(q1.from_sibling, *all4), *each(g1.along_z, *soon), g2.owner],
-        (4, 1): [g2.finish, *each(q1.to_diagonal, *all4)],
-        (4, 2): [*each(q0.along_z, *all4), g1.owner],
-        (5, 1): [*each(q1.to_neighbours, *all4), give_rest],
-        (5, 2): [
+        (0, 0): [place.barrier, *each(g1.from_sibling, *all4)],
+        (0, 2): each(g1.to_diagonal, 3),
+        (0, 4): each(g1.to_diagonal, 2, 1, 0),
+        (1, 2): each(g1.to_neighbours, 3),
+        (1, 4): [*each(g1.to_neighbours, 2, 1, 0), *each(q0.from_sibling, *all4)],
+        (2, 2): each(g1.along_z, 3),
+        (2, 4): [*each(g1.along_z, 2), *each(q0.to_diagonal, *all4)],
+        (3, 2): each(g1.along_z, 1),
+        (3, 4): [*each(g1.along_z, 0), *each(q0.to_neighbours, *all4), *each(q1.from_sibling, *all4)],
+        (4, 2): each(q1.to_diagonal, *all4),
+        (4, 4): [*each(q0.along_z, *all4), *each(q1.to_neighbours, *all4)],
+        (5, 2): [g1.owner],
+        (5, 4): [
             *each(q2.from_sibling, *all4), *each(q1.along_z, *all4), q0.owner, *each(q2.to_diagonal, *all4),
-            functools.partial(give_quad, 0), *each(q2.to_neighbours, *all4), q1.owner, *each(q2.along_z, *all4),
-            functools.partial(give_quad, 1), q2.owner, functools.partial(give_quad, 2),
+            give_rest, functools.partial(give_quad, 0), *each(q2.to_neighbours, *all4), q1.owner,
+            *each(q2.along_z, *all4), functools.partial(give_quad, 1), q2.owner, functools.partial(give_quad, 2),
             *[g.drain for g in groups],
         ],
     }
     backward_body(j, b, ins, keep, gt_ref, scratch, functools.partial(at_slots, plan, step))
 
 
-def backward_fused(seg_lengths, alignment, q, k, v, att, gatt, lse, low, gfirst, w0, vec, g2, g1):
+def backward_fused(seg_lengths, alignment, q, k, v, att, gatt, lse, low, gfirst, w0, gv, gib, g1):
     docs, slots, width = low.shape
-    text = alignment.shape[1]
     quads = width // QUAD
     quad = pl.BlockSpec((1, slots, QUAD), lambda j, b: (b, 0, j))
     doc = pl.BlockSpec((1, slots, width), lambda j, b: (b, 0, 0))
     whole = lambda *shape: once(shape, lambda j, b: (0,) * len(shape))
     n1 = g1.shape[2]
-    widths = (None, n1, 3 * QUAD, 3 * QUAD, 4 * QUAD)
+    widths = (n1, 3 * QUAD, 3 * QUAD, 4 * QUAD)
     bufs = []
     for wide in widths:
-        bufs += Scatter.scratch(96, width, False) if wide is None else Scatter.scratch(48, wide // 2, True)
+        bufs += Scatter.scratch(48, wide // 2, True)
     n = len(widths)
     shard = jax.ShapeDtypeStruct((24, width), F)
     return pl.pallas_call(
@@ -926,7 +1241,7 @@
         grid=(quads, docs),
         in_specs=[
             SMEM,
-            pl.BlockSpec((1, text, 1), lambda j, b: (b, 0, 0)),
+            whole(*alignment.shape),
             quad,
             quad,
             quad,
@@ -936,16 +1251,16 @@
             doc,
             pl.BlockSpec((1, slots, width), lambda j, b: (jnp.where(j == 0, b, 1), 0, 0)),
             whole(*w0.shape),
-            whole(*vec.shape),
-            ANY,
+            whole(*gv.shape),
+            whole(*gib.shape),
             ANY,
         ],
         out_specs=[
             pl.BlockSpec((1, slots, width), lambda j, b: (jnp.where(j == quads - 1, b, 0), 0, 0)),
             *[whole(24, width)] * 4,
             whole(24, n1 - width),
-            whole(96, width),
-            whole(24, 128),
+            whole(8, 24),
+            whole(1, 128),
         ],
         out_shape=[
             jax.ShapeDtypeStruct((docs, slots, width), BF),
@@ -954,14 +1269,15 @@
             shard,
             shard,
             jax.ShapeDtypeStruct((24, n1 - width), F),
-            jax.ShapeDtypeStruct((96, width), F),
-            jax.ShapeDtypeStruct((24, 128), F),
+            jax.ShapeDtypeStruct((8, 24), F),
+            jax.ShapeDtypeStruct((1, 128), F),
         ],
         scratch_shapes=[
             pltpu.VMEM((docs, slots, width), F),
             pltpu.VMEM((3, width, QUAD), F),
             pltpu.VMEM((8, width), F),
-            *[pltpu.VMEM((CHIPS, 48, wide), BF) for wide in widths[2:]],
+            pltpu.VMEM((width, 128), F),
+            *[pltpu.VMEM((CHIPS, 48, wide), BF) for wide in widths[1:]],
             pltpu.VMEM((24, n1), F),
             *bufs,
             pltpu.SemaphoreType.DMA((n, 4)),
@@ -969,7 +1285,7 @@
             pltpu.SemaphoreType.DMA((n, Scatter.SEMS)),
         ],
         compiler_params=pltpu.CompilerParams(collective_id=1, has_side_effects=True, vmem_limit_bytes=LIMIT),
-    )(seg_lengths, alignment[:, :, None], q, k, v, att, gatt, lse, low, gfirst, w0, vec, g2, g1)
+    )(seg_lengths, alignment, q, k, v, att, gatt, lse, low, gfirst, w0, gv, gib, g1)
 
 
 def own_kernels(shard_rows, docs):
@@ -983,46 +1299,46 @@
 ):
     docs, slots, width = tokens.shape
     rows = query_weight.shape[0]
-    ff = inner_weight.shape[1]
     every = ("dp", "fsdp")
-    own = own_kernels(rows, docs)
     vectors = (query_bias, value_bias, out_bias, first_gain, first_shift, outer_bias, second_gain, second_shift)
-    columns = [t[:, None] for t in vectors] + [inner_bias.reshape(rows, 4)]
-    pad = jnp.zeros((rows, 256 - 12), BF)
-    s0 = jnp.concatenate([query_weight, key_weight, value_weight] + columns + [pad], axis=1)
-    s1 = jnp.concatenate([out_weight, inner_weight], axis=1)
-    if own:
-        *saved, w0, w1, w2 = forward_fused(seg_lengths, tokens, alignment, s0.astype(F), s1.astype(F), outer_weight)
+    weights = (query_weight, key_weight, value_weight, out_weight, inner_weight, outer_weight)
+    flat = lambda t: t.reshape(docs * slots, width)
+    whole = lambda t: t.reshape(docs, slots, width)
+    if own_kernels(rows, docs):
+        wide = lambda t: jnp.pad(t.astype(F), ((0, 128 - t.shape[0]),))
+        packed = jnp.stack([wide(t) for t in (*vectors, inner_bias)] + [jnp.zeros((128,), F)] * 7)
+        low, q, k, v, att, lse, hat, inv, norm, act, slope, vec, w0, w1, w2 = forward_fused(
+            seg_lengths, tokens, alignment, *weights, packed
+        )
+        encoded, gfirst, gatt, g1, gvec, ginner, gouter = middle(
+            hat, inv, flat(cotangent), vec, act, slope, norm, flat(att), w1, w2
+        )
+        grad_tokens, gq, gk, gv, gout, ginn, sums, gib = backward_fused(
+            seg_lengths, alignment, q, k, v, att, whole(gatt), lse, low, whole(gfirst), w0.reshape(width, -1), gvec,
+            ginner, g1.reshape(CHIPS, 48, -1),
+        )
+        sums, gib = tuple(sums[i] for i in range(8)), gib[0, : inner_bias.shape[0]]
     else:
-        w0, w1, w2 = (lax.all_gather(s, every, axis=0, tiled=True) for s in (s0, s1, outer_weight))
-    w0, w1, w2 = w0.reshape(width, -1), w1.reshape(width, -1), w2.reshape(-1, width)
-    vec = w0[:, 3 * width : 3 * width + 12].astype(F)
-    rows_vec = vec[:, :8].T
-    inner_row = vec[:, 8:12].reshape(1, ff)
-    if not own:
-        saved = forward_attention(seg_lengths, tokens, alignment, w0, rows_vec)
-    base, low, q, k, v, att, lse = saved
-
-    flat = lambda t: t.reshape(docs * slots, width)
-    encoded, gfirst, gatt, g1, g2, gvec, ginner = mlp_both(
-        flat(att), flat(base), flat(cotangent), w1, w2, rows_vec, inner_row
-    )
-    whole = lambda t: t.reshape(docs, slots, width)
-    vec_cols = jnp.concatenate([gvec.T, ginner.reshape(width, 4), jnp.zeros((width, 116), F)], axis=1)
-    back = (seg_lengths, alignment, q, k, v, att, whole(gatt), lse, low, whole(gfirst), w0, vec_cols)
-    if own:
-        grad_tokens, gq, gk, gv, gout, ginn, gouter, sums = backward_fused(
-            *back, g2.reshape(CHIPS, 2, 96, width), g1.reshape(CHIPS, 48, -1)
+        gather = lambda s: lax.all_gather(s, every, axis=0, tiled=True)
+        owned = lambda g: lax.psum_scatter(g.astype(F), every, scatter_dimension=0, tiled=True)
+        wq, wk, wv, wo, wi, w2 = (gather(w) for w in weights)
+        w0, w1 = jnp.concatenate([wq, wk, wv], axis=1), jnp.concatenate([wo, wi], axis=1)
+        vec = jnp.stack([gather(t).astype(F) for t in vectors])
+        inner_row = gather(inner_bias).astype(F)[None]
+        base, low, q, k, v, att, lse = forward_attention(seg_lengths, tokens, alignment, w0, vec)
+        encoded, gfirst, gatt, g1, g2, gvec, ginner = mlp_both(
+            flat(att), flat(base), flat(cotangent), w1, w2, vec, inner_row
         )
-    else:
-        gq, gk, gv, gcols, grad_tokens = backward_attention(*back)
-        owned = lambda g: lax.psum_scatter(g.astype(F), every, scatter_dimension=0, tiled=True)
-        gq, gk, gv, sums, gouter = (owned(g) for g in (gq, gk, gv, gcols, g2))
-        g1 = owned(g1)
+        gq, gk, gv, two, grad_tokens = backward_attention(
+            seg_lengths, alignment, q, k, v, att, whole(gatt), lse, low, whole(gfirst), w0
+        )
+        gq, gk, gv, g1, gouter = (owned(g) for g in (gq, gk, gv, g1, g2))
         gout, ginn = g1[:, :width], g1[:, width:]
+        sums = tuple(owned(two[i] if i < 2 else gvec[i]) for i in range(8))
+        gib = owned(ginner[0])
     return (
-        whole(encoded), grad_tokens, gq, sums[:, 0], gk, gv, sums[:, 1], gout, sums[:, 2], sums[:, 3], sums[:, 4],
-        ginn, sums[:, 8:12].reshape(-1), gouter, sums[:, 5], sums[:, 6], sums[:, 7],
+        whole(encoded), grad_tokens, gq, sums[0], gk, gv, sums[1], gout, sums[2], sums[3], sums[4], ginn, gib, gouter,
+        sums[5], sums[6], sums[7],
     )
 
 

time: 285 us -> 247 us (0.87)
  Pallas kernels: 254 us -> 232 us
  local copies, waits for them, and re-layouts: 23.8 us -> 11.4 us
    pallas_call x1, Pallas kernels: 95.3 us -> 72.2 us  [backward_fused(): pl.pallas_call(functools.partial(backward_fused_kernel, widths), grid=(qu...]
    broadcast_in_dim x12 -> x0, local copies, waits for them, and re-layouts: 8.27 us -> none  [the longest x8 5.97 us: shards(): columns = [t[:, None] for t in vectors] + [inner_bias.reshape(rows, 4)]]
    another operation x0 -> x5, other arithmetic: none -> 3.36 us  [shards(): jnp.stack([wide(t) for t in (*vectors, inner_bias)] + [jnp.zeros((128,),...]
    convert_element_type x3 -> x0, other arithmetic: 3.34 us -> none  [the longest x1 1.67 us: shards(): s1.astype(F)]
    unnamed x21 -> x24, local copies, waits for them, and re-layouts: 7 us -> 7.51 us
where the time goes in v4:
time: 247 us
  Pallas kernels  232 us (94%)
  local copies, waits for them, and re-layouts  11.4 us (5%)
  other arithmetic  3.36 us (1%)
    pallas_call x1, Pallas kernels, forward_fused(): pl.pallas_call(forward_fused_kernel, grid=(ATTEND + total // TILE,), in_s...  104 us
    pallas_call x1, Pallas kernels, backward_fused(): pl.pallas_call(functools.partial(backward_fused_kernel, widths), grid=(qu...  72.2 us
    pallas_call x1, Pallas kernels, middle(): pl.pallas_call(middle_kernel, grid=(4 * tiles + 1,), in_specs=[pl.BlockSp...  55.8 us
    unnamed x24, local copies, waits for them, and re-layouts  7.51 us

profile of v4, /device:TPU:0, one launch (start us, length us, event | category | flops | bytes accessed | tf_op | source)
XLA Modules:
  0.0 247.0 jit_solution(7497779820469493863)
XLA Ops:
  0.7 0.7 bitcast_convert_fusion.8
  1.3 0.7 bitcast_convert_fusion.6
  2.0 0.7 bitcast_convert_fusion.4
  2.7 0.7 bitcast_convert_fusion
  3.3 0.7 bitcast_convert_fusion.2
  4.0 1.2 stack.83.vp
  5.2 103.7 %shard_map.314 = (bf16[2,640,768]{2,1,0:T(8,128)(2,1)}, bf16[2,640,768]{2,1,0:T(8,128)(2,1)}, bf16[2,640,768]{2,1,0:T(8,128)(2,1)}, bf16[2,640,768]{2,1,0:T(8,12...) custom-call(s32[2]{0:T(128)} %refs_0_.1, ...), custom_call_target="tpu_custom_call" | custom-call | tf_op jit(solution)/shard_map/pallas_call | solution.py:937
  108.9 55.8 %shard_map.315 = (bf16[1280,768]{1,0:T(8,128)(2,1)}, f32[1280,768]{1,0:T(8,128)}, bf16[1280,768]{1,0:T(8,128)(2,1)}, bf16[768,3840]{1,0:T(8,128)(2,1)}, f32[8,76...) custom-call(f32[1280,768]{1,0:T(8,128)} %get-tuple-element.47.hat_ref, f32[1280,128]{1,0:T(8,128)} %get-tuple-element.48.inv_ref, ...), custom_call_target="tpu_custom_call" | custom-call | tf_op jit(solution)/shard_map/pallas_call | solution.py:1109
  164.7 0.0 copy-start
  164.7 72.2 %shard_map.316 = (bf16[2,640,768]{2,1,0:T(8,128)(2,1)}, f32[24,768]{1,0:T(8,128)}, f32[24,768]{1,0:T(8,128)}, f32[24,768]{1,0:T(8,128)}, f32[24,768]{1,0:T(8,128...) custom-call(s32[2]{0:T(128)} %refs_0_.1, s32[2,512]{1,0:T(2,128)} %refs_1_.1, ...), custom_call_target="tpu_custom_call" | custom-call | tf_op jit(solution)/shard_map/pallas_call | solution.py:1239
  236.9 1.1 slice_bitcast_fusion.3
  238.0 1.5 slice_bitcast_fusion
  239.5 0.0 copy-done
  239.5 0.0 copy-start.1
  239.5 1.3 copy.44
  240.8 1.0 copy-done.1
  241.8 0.0 copy-start.7
  241.8 0.0 copy-start.6
  241.8 0.0 copy-start.5
  241.8 0.0 copy-start.4
  241.8 0.0 copy-start.3
  241.8 0.0 copy-start.2
  241.8 1.3 copy.45
  243.1 0.0 copy-done.7
  243.1 0.6 copy.46
  243.7 0.0 copy-done.6
  243.7 0.6 copy.47
  244.3 0.0 copy-done.5
  244.3 0.6 copy.48
  245.0 0.0 copy-done.4
  245.0 0.6 copy.49
  245.6 0.0 copy-done.3
  245.6 0.7 copy.50
  246.3 0.0 copy-done.2
  246.3 0.7 copy.51
  (3 shorter events, 0.0 us)
Async XLA Ops:
  164.7 74.8 %copy-start = (bf16[1280,768]{1,0:T(8,128)(2,1)S(1)}, bf16[1280,768]{1,0:T(8,128)(2,1)}, u32[]{:S(2)}) copy-start(bf16[1280,768]{1,0:T(8,128)(2,1)} %get-tuple-element.56) | copy-start | bytes 5898244
  239.5 2.3 copy-start.1
  241.8 1.3 copy-start.7
  241.8 1.9 copy-start.6
  241.8 2.6 %copy-start.5 = (f32[24,768]{1,0:T(8,128)S(1)}, f32[24,768]{1,0:T(8,128)}, u32[]{:S(2)}) copy-start(f32[24,768]{1,0:T(8,128)} %get-tuple-element.115) | copy-start | bytes 221188
  241.8 3.2 %copy-start.4 = (f32[24,768]{1,0:T(8,128)S(1)}, f32[24,768]{1,0:T(8,128)}, u32[]{:S(2)}) copy-start(f32[24,768]{1,0:T(8,128)} %get-tuple-element.117) | copy-start | bytes 221188
  241.8 3.8 %copy-start.3 = (f32[24,3072]{1,0:T(8,128)S(1)}, f32[24,3072]{1,0:T(8,128)}, u32[]{:S(2)}) copy-start(f32[24,3072]{1,0:T(8,128)} %get-tuple-element.121) | copy-start | bytes 884740
  241.8 4.5 %copy-start.2 = (f32[96,768]{1,0:T(8,128)S(1)}, f32[96,768]{1,0:T(8,128)}, u32[]{:S(2)}) copy-start(f32[96,768]{1,0:T(8,128)} %get-tuple-element.123) | copy-start | bytes 884740

commit v5 on v4

--- a/solution.py
+++ b/solution.py
@@ -513,18 +513,20 @@
     return jnp.sum(values, axis=0, keepdims=True)
 
 
-def mlp_first(att, base, w_out, w_in, vec, inner_bias, put, ff_cut=768, hook=lambda at: None):
+def mlp_norm(att, base, w_out, vec):
     first = base + dot(att, w_out(), NN) + vec(2)
     hat, inv = norm_parts(first)
-    low = (hat * vec(3) + vec(4)).astype(BF)
-    put("norm", hat, inv, low)
+    return hat, inv, (hat * vec(3) + vec(4)).astype(BF)
+
+
+def mlp_units(low, w_in, inner_bias, put, first, ff_cut=768, hook=lambda at: None):
     chunks = inner_bias.shape[1] // ff_cut
-    pre_of = lambda c: dot(low, w_in(c * ff_cut, ff_cut), NN) + inner_bias[:, c * ff_cut : (c + 1) * ff_cut]
+    pre_of = lambda c: dot(low, w_in(first + c * ff_cut, ff_cut), NN) + inner_bias[:, c * ff_cut : (c + 1) * ff_cut]
     pre = pre_of(0)
     for c in range(chunks):
         later = pre_of(c + 1) if c + 1 < chunks else None
         phi, dens = normal_parts(pre)
-        put("act", slice(c * ff_cut, (c + 1) * ff_cut), (pre * phi).astype(BF), (phi + pre * dens).astype(BF))
+        put(slice(c * ff_cut, (c + 1) * ff_cut), (pre * phi).astype(BF), (phi + pre * dens).astype(BF))
         pre = later
         hook(1 + c)
 
@@ -579,14 +581,12 @@
         w_out = lambda: w1_ref[:, :width]
         w_in = lambda c, n: w1_ref[:, width + c : width + c + n]
         w_outer = lambda c, n: w2_ref[c : c + n, :]
-        kept = {}
+
+        def put_units(cols, act, slope):
+            act_s[at, cols], slope_s[:, cols] = act, slope
 
         def put(kind, *got):
-            if kind == "norm":
-                kept["hat"], kept["inv"], norm_s[at] = got
-            elif kind == "act":
-                act_s[at, got[0]], slope_s[:, got[0]] = got[1:]
-            elif kind == "pre":
+            if kind == "pre":
                 gpre_s[at, got[0]] = got[1]
                 gib_ref[:, got[0]] += col_sum(got[1].astype(F))
             else:
@@ -596,15 +596,17 @@
                 gv_ref[4:5] += got[3]
 
         att_s[at] = att_ref[...]
-        mlp_first(att_ref[...], base_ref[...], w_out, w_in, vec, ib_ref[...], put)
-        enc_ref[...], grad_second, sums = mlp_second(kept["hat"], act_s[at], w_outer, cot_ref[...], vec)
+        hat1, inv1, low = mlp_norm(att_ref[...], base_ref[...], w_out, vec)
+        norm_s[at] = low
+        mlp_units(low, w_in, ib_ref[...], put_units, 0)
+        enc_ref[...], grad_second, sums = mlp_second(hat1, act_s[at], w_outer, cot_ref[...], vec)
         gmlp = grad_second.astype(BF)
         gmlp_s[at] = gmlp
         gv_ref[5:6] += col_sum(gmlp.astype(F))
         gv_ref[6:7] += sums[0]
         gv_ref[7:8] += sums[1]
         ga_ref[...] = mlp_back(
-            grad_second, gmlp, kept["hat"], kept["inv"], slope_s[...], w_outer, w_out, w_in, vec, put
+            grad_second, gmlp, hat1, inv1, slope_s[...], w_outer, w_out, w_in, vec, put
         )
 
     @pl.when((i >= tiles) & (i < tiles + 4))
@@ -804,6 +806,7 @@
 
 
 TILE = 320
+TILES = 4
 ATTEND = 6
 
 
@@ -811,38 +814,47 @@
     len_ref, tok_ref, al_ref, wq, wk, wv, wo, wi, s2, vp, *rest
 ):
     low_ref, q_ref, k_ref, v_ref, att_ref, lse_ref = rest[:6]
-    hat_ref, inv_ref, norm_ref, act_ref, slope_ref, vec_ref, w0, w1, w2 = rest[6:15]
+    hat_ref, inv_ref, norm_ref, act_ref, slope_ref, vec_ref, w0, wa, wb, w2 = rest[6:16]
     (
-        low_s, base_s, att_s, w0_s, w1_s, ib_s, cols_s, s0, s1, land0, land1, own0, own1, pair_sem, local, send, recv,
-    ) = rest[15:]
+        low_s, base_s, att_s, norm_s, w0_s, wa_s, wb_s, ib_s, cols_s, s0, sa, sb, land0, landa, landb, own0, owna, ownb,
+        pair_sem, local, send, recv,
+    ) = rest[16:]
     step = pl.program_id(0)
     width, ff = tok_ref.shape[2], wi.shape[1]
     place = Place()
     pairs = [
         Pair(place, s0, land0, own0, pair_sem.at[0], pair_sem.at[1]),
-        Pair(place, s1, land1, own1, pair_sem.at[2], pair_sem.at[3]),
+        Pair(place, sa, landa, owna, pair_sem.at[2], pair_sem.at[3]),
+        Pair(place, sb, landb, ownb, pair_sem.at[4], pair_sem.at[5]),
     ]
     g0 = Gather(place, w0_s, own0, send.at[0], recv.at[0], local.at[0], w0.shape[2])
-    g1 = Gather(place, w1_s, own1, send.at[1], recv.at[1], local.at[1], w1.shape[2])
-    g2 = Gather(place, w2, s2, send.at[2], recv.at[2], local.at[2])
+    ga = Gather(place, wa_s, owna, send.at[1], recv.at[1], local.at[1], wa.shape[2])
+    gb = Gather(place, wb_s, ownb, send.at[2], recv.at[2], local.at[2], wb.shape[2])
+    g2 = Gather(place, w2, s2, send.at[3], recv.at[3], local.at[3])
     saves = [
-        lambda: pltpu.make_async_copy(w0_s, w0, local.at[3]),
-        lambda: pltpu.make_async_copy(w1_s, w1, local.at[4]),
+        lambda: pltpu.make_async_copy(w0_s, w0, local.at[4]),
+        lambda: pltpu.make_async_copy(wa_s, wa, local.at[5]),
+        lambda: pltpu.make_async_copy(wb_s, wb, local.at[6]),
     ]
+    half = ff // 2
     start_of = lambda k: lambda: saves[k]().start()
     wait_of = lambda k: lambda: saves[k]().wait()
 
     def pack():
         for i, ref in enumerate((wq, wk, wv)):
             s0[:, i * width : (i + 1) * width] = ref[...].astype(F)
-        rows = jnp.concatenate([vp[:8], jnp.zeros((120, 128), F)], axis=0)
-        s0[:, 3 * width : 3 * width + 128] = rows.T[:24]
-        top = lax.broadcasted_iota(jnp.int32, (24, 1), 0) == 0
-        s0[:, 3 * width + 128 :] = jnp.where(top, vp[8:9], 0.0)
+        cols_s[:128] = jnp.zeros((128, 128), F)
+        for k in range(8):
+            cols_s[k : k + 1, :24] = vp[:, 24 * k : 24 * k + 24]
+        s0[:, 3 * width : 3 * width + 128] = cols_s[:128].T[:24]
+        s0[:, 3 * width + 128 :] = jnp.zeros((24, 128), F)
+        share = ff * 24 // width
+        s0[0:1, 3 * width + 128 : 3 * width + 128 + share] = vp[:, 192 : 192 + share]
 
     def pack_rest():
-        s1[:, :width] = wo[...].astype(F)
-        s1[:, width:] = wi[...].astype(F)
+        sa[:, :width] = wo[...].astype(F)
+        sa[:, width:] = wi[:, :half].astype(F)
+        sb[...] = wi[:, half:].astype(F)
 
     def vectors():
         cols = w0_s[:, :, 3 * width : 3 * width + 128].reshape(width, 128).astype(F)
@@ -854,38 +866,47 @@
 
     attend_plan = {
         (0, -1): [
-            pack, place.barrier, pairs[0].start, pack_rest, pairs[1].start, pairs[0].done, g0.along_z,
-            functools.partial(g0.to_neighbours, 0), pairs[1].done,
+            pack, place.barrier, pairs[0].start, pack_rest, pairs[1].start, pairs[2].start, pairs[0].done, g0.along_z,
+            functools.partial(g0.to_neighbours, 0), pairs[1].done, pairs[2].done,
         ],
         (0, 0): [
             *each(g0.to_neighbours, 1), *each(g0.to_diagonal, 0), *each(g0.to_neighbours, 2), *each(g0.to_diagonal, 1),
-            *each(g0.to_neighbours, 3), g1.along_z, *each(g0.to_core, 0), *each(g0.to_diagonal, 2),
-            *each(g1.to_neighbours, 0), *each(g0.to_core, 1), *each(g0.to_diagonal, 3), *each(g0.to_core, 2, 3),
-            *each(g1.to_neighbours, 1), g0.finish, start_of(0), vectors,
-        ],
-        (0, 1): [*each(g1.to_diagonal, 0), *each(g1.to_neighbours, 2)],
-        (0, 2): each(g1.to_diagonal, 1),
-        (0, 4): each(g1.to_neighbours, 3),
-        (1, 1): each(g1.to_diagonal, 2),
-        (1, 2): each(g1.to_core, 0),
-        (1, 4): [*each(g1.to_diagonal, 3), *each(g1.to_core, 1)],
-        (2, 2): each(g1.to_core, 2),
-        (2, 4): [g2.along_z, *each(g1.to_core, 3)],
-        (3, 1): each(g2.to_neighbours, 0),
-        (3, 3): each(g2.to_neighbours, 1),
-        (4, 1): [*each(g2.to_neighbours, 2), *each(g2.to_diagonal, 0)],
-        (4, 3): each(g2.to_diagonal, 1),
-        (5, 1): each(g2.to_neighbours, 3),
-        (5, 3): each(g2.to_diagonal, 2),
+            *each(g0.to_neighbours, 3), ga.along_z, *each(g0.to_core, 0), *each(g0.to_diagonal, 2),
+            *each(ga.to_neighbours, 0), *each(g0.to_core, 1), *each(g0.to_diagonal, 3), *each(g0.to_core, 2, 3),
+            *each(ga.to_neighbours, 1), g0.finish, start_of(0), vectors,
+        ],
+        (0, 1): [*each(ga.to_diagonal, 0), *each(ga.to_neighbours, 2)],
+        (0, 2): [gb.along_z],
+        (0, 3): each(ga.to_diagonal, 1),
+        (0, 4): [*each(ga.to_neighbours, 3), *each(gb.to_neighbours, 0)],
+        (1, 1): each(ga.to_core, 0),
+        (1, 2): [*each(ga.to_diagonal, 2), *each(gb.to_neighbours, 1)],
+        (1, 4): each(ga.to_core, 1),
+        (2, 1): [*each(ga.to_diagonal, 3), *each(gb.to_neighbours, 2)],
+        (2, 2): each(gb.to_diagonal, 0),
+        (2, 3): [g2.along_z, *each(ga.to_core, 2)],
+        (2, 4): [*each(gb.to_neighbours, 3), *each(gb.to_diagonal, 1)],
+        (3, 1): [*each(ga.to_core, 3), *each(g2.to_neighbours, 0)],
+        (3, 3): [*each(gb.to_diagonal, 2), *each(gb.to_core, 0)],
+        (3, 4): each(g2.to_neighbours, 1),
+        (4, 1): [*each(gb.to_diagonal, 3), *each(gb.to_core, 1)],
+        (4, 3): [*each(g2.to_diagonal, 0), *each(gb.to_core, 2)],
+        (4, 4): each(g2.to_neighbours, 2),
+        (5, 1): [*each(gb.to_core, 3), *each(g2.to_diagonal, 1)],
+        (5, 3): each(g2.to_neighbours, 3),
     }
     mlp_plan = {
-        (6, 0): [g1.finish, start_of(1)],
+        (6, 0): [ga.finish, start_of(1)],
         (6, 1): each(g2.to_core, 0),
-        (6, 3): each(g2.to_core, 1),
-        (7, 1): each(g2.to_diagonal, 3),
-        (7, 3): each(g2.to_core, 2),
-        (8, 1): each(g2.to_core, 3),
-        (9, 5): [g2.finish, wait_of(0), wait_of(1), g0.drain, g1.drain, g2.drain],
+        (6, 5): each(g2.to_diagonal, 2),
+        (7, 2): each(g2.to_core, 1),
+        (8, 1): each(g2.to_diagonal, 3),
+        (9, 1): each(g2.to_core, 2),
+        (10, 0): [gb.finish, start_of(2)],
+        (10, 2): each(g2.to_core, 3),
+        (13, 5): [
+            g2.finish, wait_of(0), wait_of(1), wait_of(2), g0.drain, ga.drain, gb.drain, g2.drain,
+        ],
     }
 
     @pl.when(step < ATTEND)
@@ -902,21 +923,32 @@
     def _():
         hook = functools.partial(at_slots, mlp_plan, step)
         hook(0)
-        t = step - ATTEND
-        rows = pl.ds(pl.multiple_of((t % 2) * TILE, TILE), TILE)
-
-        def put(kind, *got):
-            if kind == "norm":
-                hat_ref[...] = got[0]
-                inv_ref[...] = jnp.broadcast_to(got[1], inv_ref.shape)
-                norm_ref[...] = got[2]
-            else:
-                act_ref[:, got[0]], slope_ref[:, got[0]] = got[1:]
-
-        w_out = lambda: w1_s[:, :, :width].reshape(width, width)
-        w_in = lambda c, n: w1_s[:, :, width + c : width + c + n].reshape(width, n)
+        first_plan = {at: calls for at, calls in mlp_plan.items() if at[0] < ATTEND + TILES}
+        second_plan = {at: calls for at, calls in mlp_plan.items() if at[0] >= ATTEND + TILES}
+        t = (step - ATTEND) % TILES
+        here = pl.ds(pl.multiple_of(t * TILE, TILE), TILE)
         vec = lambda k: vec_ref[k : k + 1, :]
-        mlp_first(att_s[t // 2, rows], base_s[t // 2, rows], w_out, w_in, vec, ib_s[...], put, hook=hook)
+
+        def put(cols, act, slope):
+            act_ref[:, cols], slope_ref[:, cols] = act, slope
+
+        @pl.when(step < ATTEND + TILES)
+        def _():
+            rows = pl.ds(pl.multiple_of((t % 2) * TILE, TILE), TILE)
+            w_out = lambda: wa_s[:, :, :width].reshape(width, width)
+            w_in = lambda c, n: wa_s[:, :, width + c : width + c + n].reshape(width, n)
+            hat, inv, low = mlp_norm(att_s[t // 2, rows], base_s[t // 2, rows], w_out, vec)
+            hat_ref[...] = hat
+            inv_ref[...] = jnp.broadcast_to(inv, inv_ref.shape)
+            norm_ref[...] = low
+            norm_s[here] = low
+            mlp_units(low, w_in, ib_s[:, :half], put, 0, hook=functools.partial(at_slots, first_plan, step))
+
+        @pl.when(step >= ATTEND + TILES)
+        def _():
+            w_in = lambda c, n: wb_s[:, :, c : c + n].reshape(width, n)
+            mlp_units(norm_s[here], w_in, ib_s[:, half:], put, 0, hook=functools.partial(at_slots, second_plan, step))
+
         hook(5)
 
 
@@ -924,7 +956,7 @@
     docs, slots, width = tokens.shape
     ff = wi.shape[1]
     quads = width // QUAD
-    n0, n1 = 3 * width + 256, width + ff
+    n0, na, nb = 3 * width + 256, width + ff // 2, ff // 2
     total = docs * slots
     last = ATTEND - 1
     doc_of = lambda s: jnp.minimum(s, last) // quads
@@ -932,18 +964,20 @@
     quad = pl.BlockSpec((1, slots, QUAD), lambda s: (doc_of(s), 0, jnp.minimum(s, last) % quads))
     wide = jax.ShapeDtypeStruct((docs, slots, width), BF)
     full = lambda *shape: once(shape, lambda s: (0,) * len(shape))
-    tile = lambda n: pl.BlockSpec((TILE, n), lambda s: (jnp.maximum(s - ATTEND, 0), 0))
+    tile = lambda n: pl.BlockSpec((TILE, n), lambda s: (jnp.clip(s - ATTEND, 0, TILES - 1), 0))
+    past = lambda s: jnp.maximum(s - ATTEND, 0)
+    units = pl.BlockSpec((TILE, ff // 2), lambda s: (past(s) % TILES, past(s) // TILES))
     ins = (alignment, wq, wk, wv, wo, wi, s2, vp)
     return pl.pallas_call(
         forward_fused_kernel,
-        grid=(ATTEND + total // TILE,),
+        grid=(ATTEND + 2 * TILES,),
         in_specs=[SMEM, doc] + [full(*a.shape) for a in ins],
         out_specs=[
             doc, quad, quad, quad, quad,
             pl.BlockSpec((1, 1, 8, slots), lambda s: (doc_of(s), jnp.minimum(s, last) % quads, 0, 0)),
-            tile(width), tile(128), tile(width), tile(ff), tile(ff), full(8, width),
+            tile(width), tile(128), tile(width), units, units, full(8, width),
         ]
-        + [ANY] * 3,
+        + [ANY] * 4,
         out_shape=[
             wide,
             wide,
@@ -957,39 +991,35 @@
             jax.ShapeDtypeStruct((total, ff), BF),
             jax.ShapeDtypeStruct((total, ff), BF),
             jax.ShapeDtypeStruct((8, width), F),
-            jax.ShapeDtypeStruct((CHIPS, 48, n0), BF),
-            jax.ShapeDtypeStruct((CHIPS, 48, n1), BF),
+            *[jax.ShapeDtypeStruct((CHIPS, 48, n), BF) for n in (n0, na, nb)],
             jax.ShapeDtypeStruct((CHIPS, 2, 96, width), BF),
         ],
         scratch_shapes=[
             pltpu.VMEM((slots, width), BF),
             pltpu.VMEM((docs, slots, width), F),
             pltpu.VMEM((docs, slots, width), BF),
-            pltpu.VMEM((CHIPS, 48, n0), BF),
-            pltpu.VMEM((CHIPS, 48, n1), BF),
+            pltpu.VMEM((total, width), BF),
+            *[pltpu.VMEM((CHIPS, 48, n), BF) for n in (n0, na, nb)],
             pltpu.VMEM((1, ff), F),
             pltpu.VMEM((width, 128), F),
-            pltpu.VMEM((24, n0), F),
-            pltpu.VMEM((24, n1), F),
-            pltpu.VMEM((24, n0 // 2), F),
-            pltpu.VMEM((24, n1 // 2), F),
-            pltpu.VMEM((48, n0 // 2), BF),
-            pltpu.VMEM((48, n1 // 2), BF),
-            pltpu.SemaphoreType.DMA((4,)),
-            pltpu.SemaphoreType.DMA((5,)),
-            pltpu.SemaphoreType.DMA((3, Gather.SEMS)),
-            pltpu.SemaphoreType.DMA((3, Gather.SEMS)),
+            *[pltpu.VMEM((24, n), F) for n in (n0, na, nb)],
+            *[pltpu.VMEM((24, n // 2), F) for n in (n0, na, nb)],
+            *[pltpu.VMEM((48, n // 2), BF) for n in (n0, na, nb)],
+            pltpu.SemaphoreType.DMA((6,)),
+            pltpu.SemaphoreType.DMA((7,)),
+            pltpu.SemaphoreType.DMA((4, Gather.SEMS)),
+            pltpu.SemaphoreType.DMA((4, Gather.SEMS)),
         ],
         compiler_params=pltpu.CompilerParams(collective_id=0, has_side_effects=True, vmem_limit_bytes=LIMIT),
     )(seg_lengths, tokens, *ins)
 
 
 def middle_kernel(hat_ref, inv_ref, cot_ref, vec_ref, *rest):
-    act_h, slope_h, norm_h, att_h, w1_h, w2_h = rest[:6]
-    enc_ref, gf_ref, ga_ref, g1_ref, gv_ref, gib_ref, o_outer = rest[6:13]
-    act_s, slope_s, w1_s, w2_s, gsec_s, gmlp_s, g2_s = rest[13:20]
-    bufs = rest[20:27]
-    load_sem, local, send, recv = rest[27:]
+    act_h, slope_h, norm_h, att_h, wa_h, wb_h, w2_h = rest[:7]
+    enc_ref, gf_ref, ga_ref, g1_ref, gv_ref, gib_ref, o_outer = rest[7:14]
+    act_s, slope_s, wa_s, wb_s, w2_s, gsec_s, gmlp_s, g2_s = rest[14:22]
+    bufs = rest[22:29]
+    load_sem, local, send, recv = rest[29:]
     i = pl.program_id(0)
     rows, width = hat_ref.shape
     norm_s, att_s, gbr_s = (act_s.at[:, pl.ds(k * width, width)] for k in range(3))
@@ -1004,9 +1034,10 @@
     for t in range(tiles):
         loads.append(lambda t=t: pltpu.make_async_copy(slope_h.at[cut(t)], slope_s.at[cut(t)], load_sem.at[5 + t]))
     loads += [
-        lambda: pltpu.make_async_copy(w1_h, w1_s, load_sem.at[9]),
+        lambda: pltpu.make_async_copy(wa_h, wa_s, load_sem.at[9]),
         lambda: pltpu.make_async_copy(norm_h, norm_s, load_sem.at[10]),
         lambda: pltpu.make_async_copy(att_h, att_s, load_sem.at[11]),
+        lambda: pltpu.make_async_copy(wb_h, wb_s, load_sem.at[12]),
     ]
     wait = lambda k: lambda: loads[k]().wait()
     loads_start = lambda k: lambda: loads[k]().start()
@@ -1020,7 +1051,7 @@
 
     plan = {
         (0, 0): [begin, wait(0), wait(1), *map(loads_start, (2, 3, 4))],
-        (1, 0): [wait(2), *map(loads_start, (9, 5))],
+        (1, 0): [wait(2), *map(loads_start, (9, 12, 5))],
         (2, 0): [wait(3), *map(loads_start, (6, 7, 8))],
         (3, 0): [wait(4)],
         (4, 2): each(g2.from_sibling, 3),
@@ -1029,7 +1060,7 @@
         (7, 2): each(g2.from_sibling, 0),
         (6, 0): each(g2.to_diagonal, 3),
         (7, 0): each(g2.to_diagonal, 2),
-        (8, 0): [loads_start(10), loads_start(11), wait(9), wait(5), *each(g2.to_diagonal, 1)],
+        (8, 0): [loads_start(10), loads_start(11), wait(9), wait(12), wait(5), *each(g2.to_diagonal, 1)],
         (8, 1): [*each(g2.to_diagonal, 0), *each(g2.to_neighbours, 3)],
         (8, 2): each(g2.to_neighbours, 2),
         (9, 0): [wait(6)],
@@ -1081,8 +1112,13 @@
                 gv_ref[3:4] += got[2]
                 gv_ref[4:5] += got[3]
 
-        w_out = lambda: w1_s[:, :, :width].reshape(width, width)
-        w_in = lambda c, n: w1_s[:, :, width + c : width + c + n].reshape(width, n)
+        half = wb_s.shape[2]
+        w_out = lambda: wa_s[:, :, :width].reshape(width, width)
+
+        def w_in(c, n):
+            part = wa_s[:, :, width + c : width + c + n] if c < half else wb_s[:, :, c - half : c - half + n]
+            return part.reshape(width, n)
+
         ga_ref[...] = mlp_back(
             gsec_s[at], gmlp_s[at], hat_ref[...], inv_ref[:, 0:1], slope_s[at], w_outer, w_out, w_in, vec, put, hook=hook
         )
@@ -1099,7 +1135,7 @@
     hook(2)
 
 
-def middle(hat, inv, cotangent, vec, act, slope, norm, att, w1, w2):
+def middle(hat, inv, cotangent, vec, act, slope, norm, att, wa, wb, w2):
     total, width = hat.shape
     ff = act.shape[1]
     tiles = total // TILE
@@ -1118,7 +1154,7 @@
             early(width),
             full(8, width),
         ]
-        + [ANY] * 6,
+        + [ANY] * 7,
         out_specs=[
             early(width),
             late(width),
@@ -1140,19 +1176,20 @@
         scratch_shapes=[
             pltpu.VMEM((total, ff), BF),
             pltpu.VMEM((total, ff), BF),
-            pltpu.VMEM(w1.shape, BF),
+            pltpu.VMEM(wa.shape, BF),
+            pltpu.VMEM(wb.shape, BF),
             pltpu.VMEM(w2.shape, BF),
             pltpu.VMEM((total, width), F),
             pltpu.VMEM((total, width), BF),
             pltpu.VMEM(w2.shape, BF),
             *Scatter.scratch(96, width, False),
-            pltpu.SemaphoreType.DMA((12,)),
+            pltpu.SemaphoreType.DMA((13,)),
             pltpu.SemaphoreType.DMA((1, 4)),
             pltpu.SemaphoreType.DMA((1, Scatter.SEMS)),
             pltpu.SemaphoreType.DMA((1, Scatter.SEMS)),
         ],
         compiler_params=pltpu.CompilerParams(collective_id=2, has_side_effects=True, vmem_limit_bytes=LIMIT),
-    )(hat, inv, cotangent, vec, act, slope, norm, att, w1, w2)
+    )(hat, inv, cotangent, vec, act, slope, norm, att, wa, wb, w2)
 
 
 def backward_fused_kernel(widths, *refs):
@@ -1288,6 +1325,38 @@
     )(seg_lengths, alignment, q, k, v, att, gatt, lse, low, gfirst, w0, gv, gib, g1)
 
 
+def deliver_kernel(count, *refs):
+    ins, sums, gib = refs[:count], refs[count], refs[count + 1]
+    outs, vecs, ib_out = refs[count + 2 : 2 * count + 2], refs[2 * count + 2 : 2 * count + 10], refs[2 * count + 10]
+    held, sem_in, sem_out = refs[2 * count + 11 : 3 * count + 11], refs[-2], refs[-1]
+    loads = [pltpu.make_async_copy(a, b, sem_in.at[i]) for i, (a, b) in enumerate(zip(ins, held))]
+    stores = [pltpu.make_async_copy(a, b, sem_out.at[i]) for i, (a, b) in enumerate(zip(held, outs))]
+    for c in loads:
+        c.start()
+    for k, out in enumerate(vecs):
+        out[...] = sums[k, :]
+    ib_out[...] = gib[0, : ib_out.shape[0]]
+    for i in range(count):
+        loads[i].wait()
+        stores[i].start()
+    for c in stores:
+        c.wait()
+
+
+def deliver(arrays, sums, gib, share):
+    n = len(arrays)
+    return pl.pallas_call(
+        functools.partial(deliver_kernel, n),
+        out_shape=[jax.ShapeDtypeStruct(a.shape, a.dtype) for a in arrays]
+        + [jax.ShapeDtypeStruct((sums.shape[1],), F)] * 8
+        + [jax.ShapeDtypeStruct((share,), F)],
+        in_specs=[ANY] * n + [VMEM] * 2,
+        out_specs=[ANY] * n + [VMEM] * 9,
+        scratch_shapes=[pltpu.VMEM(a.shape, a.dtype) for a in arrays] + [pltpu.SemaphoreType.DMA((n,))] * 2,
+        compiler_params=pltpu.CompilerParams(vmem_limit_bytes=LIMIT),
+    )(*arrays, sums, gib)
+
+
 def own_kernels(shard_rows, docs):
     return lax.axis_size("dp") == PLANES and lax.axis_size("fsdp") == 8 and shard_rows == 24 and docs == 2
 
@@ -1305,19 +1374,21 @@
     flat = lambda t: t.reshape(docs * slots, width)
     whole = lambda t: t.reshape(docs, slots, width)
     if own_kernels(rows, docs):
-        wide = lambda t: jnp.pad(t.astype(F), ((0, 128 - t.shape[0]),))
-        packed = jnp.stack([wide(t) for t in (*vectors, inner_bias)] + [jnp.zeros((128,), F)] * 7)
-        low, q, k, v, att, lse, hat, inv, norm, act, slope, vec, w0, w1, w2 = forward_fused(
+        packed = jnp.concatenate((*vectors, inner_bias)).astype(F)[None]
+        low, q, k, v, att, lse, hat, inv, norm, act, slope, vec, w0, wa, wb, w2 = forward_fused(
             seg_lengths, tokens, alignment, *weights, packed
         )
         encoded, gfirst, gatt, g1, gvec, ginner, gouter = middle(
-            hat, inv, flat(cotangent), vec, act, slope, norm, flat(att), w1, w2
+            hat, inv, flat(cotangent), vec, act, slope, norm, flat(att), wa, wb, w2
         )
         grad_tokens, gq, gk, gv, gout, ginn, sums, gib = backward_fused(
             seg_lengths, alignment, q, k, v, att, whole(gatt), lse, low, whole(gfirst), w0.reshape(width, -1), gvec,
             ginner, g1.reshape(CHIPS, 48, -1),
         )
-        sums, gib = tuple(sums[i] for i in range(8)), gib[0, : inner_bias.shape[0]]
+        whole_encoded = whole(encoded)
+        whole_encoded, grad_tokens, gq, gk, gv, gout, ginn, gouter, *sums, gib = deliver(
+            (whole_encoded, grad_tokens, gq, gk, gv, gout, ginn, gouter), sums, gib, inner_bias.shape[0]
+        )
     else:
         gather = lambda s: lax.all_gather(s, every, axis=0, tiled=True)
         owned = lambda g: lax.psum_scatter(g.astype(F), every, scatter_dimension=0, tiled=True)
@@ -1336,8 +1407,9 @@
         gout, ginn = g1[:, :width], g1[:, width:]
         sums = tuple(owned(two[i] if i < 2 else gvec[i]) for i in range(8))
         gib = owned(ginner[0])
+        whole_encoded = whole(encoded)
     return (
-        whole(encoded), grad_tokens, gq, sums[0], gk, gv, sums[1], gout, sums[2], sums[3], sums[4], ginn, gib, gouter,
+        whole_encoded, grad_tokens, gq, sums[0], gk, gv, sums[1], gout, sums[2], sums[3], sums[4], ginn, gib, gouter,
         sums[5], sums[6], sums[7],
     )
 

time: 247 us -> 230 us (0.931)
  local copies, waits for them, and re-layouts: 11.4 us -> 0.88 us
  Pallas kernels: 232 us -> 227 us
  other arithmetic: 3.36 us -> 0.57 us
    unnamed x24 -> x0, local copies, waits for them, and re-layouts: 7.51 us -> none
    pallas_call x1 -> x2, Pallas kernels: 104 us -> 99.5 us  [the longest x1 94.3 us: forward_fused(): pl.pallas_call(forward_fused_kernel, grid=(ATTEND + 2 * TILES,), in_specs...]
    another operation x5 -> x0, other arithmetic: 3.36 us -> none  [shards(): jnp.stack([wide(t) for t in (*vectors, inner_bias)] + [jnp.zeros((128,),...]
    squeeze x2 -> x0, local copies, waits for them, and re-layouts: 2.64 us -> none  [the longest x1 1.51 us: shards(): sums[i]]
where the time goes in v5:
time: 230 us
  Pallas kernels  227 us (99%)
    pallas_call x1, Pallas kernels, forward_fused(): pl.pallas_call(forward_fused_kernel, grid=(ATTEND + 2 * TILES,), in_specs...  94.3 us
    pallas_call x1, Pallas kernels, backward_fused(): pl.pallas_call(functools.partial(backward_fused_kernel, widths), grid=(qu...  72.1 us
    pallas_call x1, Pallas kernels, middle(): pl.pallas_call(middle_kernel, grid=(4 * tiles + 1,), in_specs=[pl.BlockSp...  55.9 us
    pallas_call x1, Pallas kernels, deliver(): pl.pallas_call(functools.partial(deliver_kernel, n), out_shape=[jax.Shape...  5.13 us

profile of v5, /device:TPU:0, one launch (start us, length us, event | category | flops | bytes accessed | tf_op | source)
XLA Modules:
  0.0 229.8 jit_solution(17669865346206187166)
XLA Ops:
  0.7 0.9 concatenate.37
  1.5 0.6 convert_element_type.10.vp
  2.1 94.3 %shard_map.314 = (bf16[2,640,768]{2,1,0:T(8,128)(2,1)}, bf16[2,640,768]{2,1,0:T(8,128)(2,1)}, bf16[2,640,768]{2,1,0:T(8,128)(2,1)}, bf16[2,640,768]{2,1,0:T(8,12...) custom-call(s32[2]{0:T(128)} %refs_0_.1, ...), custom_call_target="tpu_custom_call" | custom-call | tf_op jit(solution)/shard_map/pallas_call | solution.py:971
  96.5 55.9 %shard_map.315 = (bf16[1280,768]{1,0:T(8,128)(2,1)}, f32[1280,768]{1,0:T(8,128)}, bf16[1280,768]{1,0:T(8,128)(2,1)}, bf16[768,3840]{1,0:T(8,128)(2,1)}, f32[8,76...) custom-call(f32[1280,768]{1,0:T(8,128)} %get-tuple-element.65.hat_ref, f32[1280,128]{1,0:T(8,128)} %get-tuple-element.66.inv_ref, ...), custom_call_target="tpu_custom_call" | custom-call | tf_op jit(solution)/shard_map/pallas_call | solution.py:1145
  152.3 72.1 %shard_map.316 = (bf16[2,640,768]{2,1,0:T(8,128)(2,1)}, f32[24,768]{1,0:T(8,128)}, f32[24,768]{1,0:T(8,128)}, f32[24,768]{1,0:T(8,128)}, f32[24,768]{1,0:T(8,128...) custom-call(s32[2]{0:T(128)} %refs_0_.1, s32[2,512]{1,0:T(2,128)} %refs_1_.1, ...), custom_call_target="tpu_custom_call" | custom-call | tf_op jit(solution)/shard_map/pallas_call | solution.py:1276
  224.4 5.1 %shard_map.317 = (bf16[2,640,768]{2,1,0:T(8,128)(2,1)}, bf16[2,640,768]{2,1,0:T(8,128)(2,1)}, f32[24,768]{1,0:T(8,128)}, f32[24,768]{1,0:T(8,128)}, f32[24,768]{...) custom-call(bf16[2,640,768]{2,1,0:T(8,128)(2,1)} %bitcast.21, ...), custom_call_target="tpu_custom_call" | custom-call | tf_op jit(solution)/shard_map/pallas_call | solution.py:1348

commit v6 on v5

--- a/solution.py
+++ b/solution.py
@@ -300,8 +300,7 @@
         f = jnp.float32
         for k in range(3):
             self.copy(self.lz.at[k], self.lz.at[k], 20 + k, (p.z, p.f)).wait_recv()
-        c0 = self.chip(0, p.spot)
-        total = self.sums[c0].astype(f)
+        total = self.mine().astype(f)
         for k in range(3):
             total = total + self.lz[k].astype(f)
         if self.half is None:
@@ -311,6 +310,9 @@
         rows = self.rows // 2
         theirs = lambda: self.total.at[pl.ds(pl.multiple_of((1 - p.core) * rows, 8), rows)]
         self.start(lambda: self.copy(theirs(), self.last, 23, (p.z, p.sib)))
+
+    def mine(self):
+        return self.sums[self.chip(0, self.p.spot)]
 
     def finish(self):
         if self.half is None:
@@ -484,7 +486,7 @@
 
 def normal_parts(pre):
     size = jnp.abs(pre)
-    dens = jnp.exp(pre * pre * -0.5)
+    dens = jnp.exp2(pre * pre * (-0.5 * 1.4426950408889634))
     t = 1.0 / (1.0 + (0.3275911 * 0.7071067811865476) * size)
     poly = t * (
         0.5 * 0.254829592
@@ -665,11 +667,10 @@
     )(attended, base, cotangent, w1, w2, vec, inner_bias)
 
 
-def backward_body(j, b, refs, keep, gt_ref, scratch, hook=lambda at: None):
+def backward_body(j, b, refs, keep, gt_ref, scratch, hook=lambda at: None, later=None):
     len_ref, al_ref, q_ref, k_ref, v_ref, o_ref, do_ref, lse_ref, low_ref, gf_ref, w_ref = refs
     gbase_s, acc_s, vsum_s = scratch
     text, width = al_ref.shape[1], low_ref.shape[2]
-    segs = low_ref.shape[1] - text
     quads = width // QUAD
     align = al_ref[pl.ds(b, 1), :]
 
@@ -690,15 +691,19 @@
     quad_grads = [jnp.concatenate(p, axis=1) for p in parts]
     cols = pl.ds(pl.multiple_of(j * QUAD, QUAD), QUAD)
 
-    @pl.when(j == 0)
-    def _():
-        gbase_s[b] = gf_ref[0]
-
-    gbase = gbase_s[b]
-    for i in range(3):
-        at = pl.ds(pl.multiple_of(i * width + j * QUAD, QUAD), QUAD)
-        gbase = gbase + dot(quad_grads[i], w_ref[:, at], NT)
-    gbase_s[b] = gbase
+    if later is None:
+
+        @pl.when(j == 0)
+        def _():
+            gbase_s[b] = gf_ref[0]
+
+        gbase = gbase_s[b]
+        for i in range(3):
+            at = pl.ds(pl.multiple_of(i * width + j * QUAD, QUAD), QUAD)
+            gbase = gbase + dot(quad_grads[i], w_ref[:, at], NT)
+        gbase_s[b] = gbase
+    else:
+        later(quad_grads)
 
     low = low_ref[0]
     weight = [dot(low, g, TN) for g in quad_grads]
@@ -717,19 +722,24 @@
             vsum_s[i : i + 1, cols] += sums[i]
         keep(lambda i: (acc_s[i] + weight[i]).astype(BF))
 
-    @pl.when(j == quads - 1)
-    def _():
-        member = member_of(align, segs)
-        counts = jnp.maximum(jnp.sum(member, axis=1, keepdims=True), 1.0)
-        share = gbase[text:] / counts
-        high = share.astype(BF)
-        rest = (share - high.astype(F)).astype(BF)
-        sel = member.astype(BF)
-        spread = dot(sel, high, TN) + dot(sel, rest, TN)
-        gt_ref[0, :text] = (gbase[:text] + spread).astype(BF)
-        gt_ref[0, text:] = gbase[text:].astype(BF)
+    if later is None:
+
+        @pl.when(j == quads - 1)
+        def _():
+            gt_ref[0] = token_grads(gbase, align, text)
 
     hook(4)
+
+
+def token_grads(gbase, align, text):
+    member = member_of(align, gbase.shape[0] - text)
+    counts = jnp.maximum(jnp.sum(member, axis=1, keepdims=True), 1.0)
+    share = gbase[text:] / counts
+    high = share.astype(BF)
+    rest = (share - high.astype(F)).astype(BF)
+    sel = member.astype(BF)
+    spread = dot(sel, high, TN) + dot(sel, rest, TN)
+    return jnp.concatenate([gbase[:text] + spread, gbase[text:]], axis=0).astype(BF)
 
 
 def vector_cols(vsum_s, gv_ref, gib_ref, cols_s):
@@ -1051,9 +1061,10 @@
 
     plan = {
         (0, 0): [begin, wait(0), wait(1), *map(loads_start, (2, 3, 4))],
-        (1, 0): [wait(2), *map(loads_start, (9, 12, 5))],
-        (2, 0): [wait(3), *map(loads_start, (6, 7, 8))],
-        (3, 0): [wait(4)],
+        (1, 0): [wait(2)],
+        (2, 0): [wait(3)],
+        (3, 0): [wait(4), *map(loads_start, (9, 12, 5))],
+        (5, 0): [*map(loads_start, (6, 7, 8))],
         (4, 2): each(g2.from_sibling, 3),
         (5, 2): each(g2.from_sibling, 2),
         (6, 2): each(g2.from_sibling, 1),
@@ -1195,8 +1206,8 @@
 def backward_fused_kernel(widths, *refs):
     ins, (gv_ref, gib_ref, g1_ref) = refs[:11], refs[11:14]
     gt_ref, o_wide, o_inner, o_vec, o_ib = refs[14], refs[15:19], refs[19], refs[20], refs[21]
-    scratch, cols_s = refs[22:25], refs[25]
-    rest = list(refs[26:])
+    scratch, cols_s, gqkv_s, w_s, gf_sem = refs[22:25], refs[25], refs[26], refs[27], refs[28]
+    rest = list(refs[29:])
     local, send, recv = rest[-3:]
     j, b = pl.program_id(0), pl.program_id(1)
     step = 2 * j + b
@@ -1235,10 +1246,22 @@
                     both = vector_cols(scratch[2], gv_ref, gib_ref, cols_s)
                     quad_s[k][:, :, 3 * QUAD :] = both.reshape(CHIPS, 48, QUAD)
 
+    al_ref, gf_h, w_h, gf_s = ins[1], ins[9], ins[10], scratch[0]
+    load_w = lambda: pltpu.make_async_copy(w_h, w_s, gf_sem.at[1])
+    load = lambda: pltpu.make_async_copy(gf_h, gf_s, gf_sem.at[0])
+
+    def later(grads):
+        for i, grad in enumerate(grads):
+            gqkv_s[b, :, pl.ds(pl.multiple_of(i * width + j * QUAD, QUAD), QUAD)] = grad
+
+    def tokens_of(doc):
+        gbase = gf_s[doc] + dot(gqkv_s[doc], w_s[:, : 3 * width], NT)
+        gt_ref[doc] = token_grads(gbase, al_ref[doc : doc + 1, :], al_ref.shape[1])
+
     late, soon = (3, 2), (1, 0)
     all4 = late + soon
     plan = {
-        (0, 0): [place.barrier, *each(g1.from_sibling, *all4)],
+        (0, 0): [place.barrier, *each(g1.from_sibling, *all4), lambda: load().start(), lambda: load_w().start()],
         (0, 2): each(g1.to_diagonal, 3),
         (0, 4): each(g1.to_diagonal, 2, 1, 0),
         (1, 2): each(g1.to_neighbours, 3),
@@ -1251,13 +1274,14 @@
         (4, 4): [*each(q0.along_z, *all4), *each(q1.to_neighbours, *all4)],
         (5, 2): [g1.owner],
         (5, 4): [
-            *each(q2.from_sibling, *all4), *each(q1.along_z, *all4), q0.owner, *each(q2.to_diagonal, *all4),
-            give_rest, functools.partial(give_quad, 0), *each(q2.to_neighbours, *all4), q1.owner,
-            *each(q2.along_z, *all4), functools.partial(give_quad, 1), q2.owner, functools.partial(give_quad, 2),
+            *each(q2.from_sibling, *all4), lambda: load().wait(), lambda: load_w().wait(), *each(q2.to_diagonal, *all4),
+            *each(q1.along_z, *all4), functools.partial(tokens_of, 0), *each(q2.to_neighbours, *all4),
+            functools.partial(tokens_of, 1), *each(q2.along_z, *all4), q0.owner, q1.owner, give_rest,
+            functools.partial(give_quad, 0), functools.partial(give_quad, 1), q2.owner, functools.partial(give_quad, 2),
             *[g.drain for g in groups],
         ],
     }
-    backward_body(j, b, ins, keep, gt_ref, scratch, functools.partial(at_slots, plan, step))
+    backward_body(j, b, ins, keep, gt_ref, scratch, functools.partial(at_slots, plan, step), later)
 
 
 def backward_fused(seg_lengths, alignment, q, k, v, att, gatt, lse, low, gfirst, w0, gv, gib, g1):
@@ -1286,14 +1310,14 @@
             quad,
             pl.BlockSpec((1, 1, 8, slots), lambda j, b: (b, j, 0, 0)),
             doc,
-            pl.BlockSpec((1, slots, width), lambda j, b: (jnp.where(j == 0, b, 1), 0, 0)),
-            whole(*w0.shape),
+            ANY,
+            ANY,
             whole(*gv.shape),
             whole(*gib.shape),
             ANY,
         ],
         out_specs=[
-            pl.BlockSpec((1, slots, width), lambda j, b: (jnp.where(j == quads - 1, b, 0), 0, 0)),
+            whole(docs, slots, width),
             *[whole(24, width)] * 4,
             whole(24, n1 - width),
             whole(8, 24),
@@ -1314,6 +1338,9 @@
             pltpu.VMEM((3, width, QUAD), F),
             pltpu.VMEM((8, width), F),
             pltpu.VMEM((width, 128), F),
+            pltpu.VMEM((docs, slots, 3 * width), BF),
+            pltpu.VMEM(w0.shape, BF),
+            pltpu.SemaphoreType.DMA((2,)),
             *[pltpu.VMEM((CHIPS, 48, wide), BF) for wide in widths[1:]],
             pltpu.VMEM((24, n1), F),
             *bufs,

time: 230 us -> 227 us (0.987)
  Pallas kernels: 227 us -> 224 us
    pallas_call x1, Pallas kernels: 72.1 us -> 69.6 us  [backward_fused(): pl.pallas_call(functools.partial(backward_fused_kernel, widths), grid=(qu...]
where the time goes in v6:
time: 227 us
  Pallas kernels  224 us (99%)
    pallas_call x1, Pallas kernels, forward_fused(): pl.pallas_call(forward_fused_kernel, grid=(ATTEND + 2 * TILES,), in_specs...  93.9 us
    pallas_call x1, Pallas kernels, backward_fused(): pl.pallas_call(functools.partial(backward_fused_kernel, widths), grid=(qu...  69.6 us
    pallas_call x1, Pallas kernels, middle(): pl.pallas_call(middle_kernel, grid=(4 * tiles + 1,), in_specs=[pl.BlockSp...  55.8 us
    pallas_call x1, Pallas kernels, deliver(): pl.pallas_call(functools.partial(deliver_kernel, n), out_shape=[jax.Shape...  5.13 us

profile of v6, /device:TPU:0, one launch (start us, length us, event | category | flops | bytes accessed | tf_op | source)
XLA Modules:
  0.0 226.8 jit_solution(13913328751679076758)
XLA Ops:
  0.7 0.9 concatenate.37
  1.5 0.6 convert_element_type.10.vp
  2.1 93.9 %shard_map.314 = (bf16[2,640,768]{2,1,0:T(8,128)(2,1)}, bf16[2,640,768]{2,1,0:T(8,128)(2,1)}, bf16[2,640,768]{2,1,0:T(8,128)(2,1)}, bf16[2,640,768]{2,1,0:T(8,12...) custom-call(s32[2]{0:T(128)} %refs_0_.1, ...), custom_call_target="tpu_custom_call" | custom-call | tf_op jit(solution)/shard_map/pallas_call | solution.py:981
  96.0 55.8 %shard_map.315 = (bf16[1280,768]{1,0:T(8,128)(2,1)}, f32[1280,768]{1,0:T(8,128)}, bf16[1280,768]{1,0:T(8,128)(2,1)}, bf16[768,3840]{1,0:T(8,128)(2,1)}, f32[8,76...) custom-call(f32[1280,768]{1,0:T(8,128)} %get-tuple-element.65.hat_ref, f32[1280,128]{1,0:T(8,128)} %get-tuple-element.66.inv_ref, ...), custom_call_target="tpu_custom_call" | custom-call | tf_op jit(solution)/shard_map/pallas_call | solution.py:1156
  151.8 69.6 %shard_map.316 = (bf16[2,640,768]{2,1,0:T(8,128)(2,1)}, f32[24,768]{1,0:T(8,128)}, f32[24,768]{1,0:T(8,128)}, f32[24,768]{1,0:T(8,128)}, f32[24,768]{1,0:T(8,128...) custom-call(s32[2]{0:T(128)} %refs_0_.1, s32[2,512]{1,0:T(2,128)} %refs_1_.1, ...), custom_call_target="tpu_custom_call" | custom-call | tf_op jit(solution)/shard_map/pallas_call | solution.py:1300
  221.4 5.1 %shard_map.317 = (bf16[2,640,768]{2,1,0:T(8,128)(2,1)}, bf16[2,640,768]{2,1,0:T(8,128)(2,1)}, f32[24,768]{1,0:T(8,128)}, f32[24,768]{1,0:T(8,128)}, f32[24,768]{...) custom-call(bf16[2,640,768]{2,1,0:T(8,128)(2,1)} %bitcast.21, ...), custom_call_target="tpu_custom_call" | custom-call | tf_op jit(solution)/shard_map/pallas_call | solution.py:1375

commit v7 on v6

--- a/solution.py
+++ b/solution.py
@@ -37,11 +37,17 @@
     def ahead(self, step):
         return (self.z + step) % PLANES
 
-    def barrier(self):
+    def greet(self):
         bar = pltpu.get_barrier_semaphore()
         for other in self.partners():
             pl.semaphore_signal(bar, inc=1, device_id=other, device_id_type=MESH)
-        pl.semaphore_wait(bar, 3 + PLANES - 1)
+
+    def met(self):
+        pl.semaphore_wait(pltpu.get_barrier_semaphore(), 3 + PLANES - 1)
+
+    def barrier(self):
+        self.greet()
+        self.met()
 
     def partners(self):
         return [(self.z, self.sib), (self.z, self.xn), (self.z, self.yn)] + [
@@ -854,12 +860,13 @@
         for i, ref in enumerate((wq, wk, wv)):
             s0[:, i * width : (i + 1) * width] = ref[...].astype(F)
         cols_s[:128] = jnp.zeros((128, 128), F)
+        values = vp[...].astype(F)
         for k in range(8):
-            cols_s[k : k + 1, :24] = vp[:, 24 * k : 24 * k + 24]
+            cols_s[k : k + 1, :24] = values[:, 24 * k : 24 * k + 24]
         s0[:, 3 * width : 3 * width + 128] = cols_s[:128].T[:24]
         s0[:, 3 * width + 128 :] = jnp.zeros((24, 128), F)
         share = ff * 24 // width
-        s0[0:1, 3 * width + 128 : 3 * width + 128 + share] = vp[:, 192 : 192 + share]
+        s0[0:1, 3 * width + 128 : 3 * width + 128 + share] = values[:, 192 : 192 + share]
 
     def pack_rest():
         sa[:, :width] = wo[...].astype(F)
@@ -876,7 +883,7 @@
 
     attend_plan = {
         (0, -1): [
-            pack, place.barrier, pairs[0].start, pack_rest, pairs[1].start, pairs[2].start, pairs[0].done, g0.along_z,
+            place.greet, pack, place.met, pairs[0].start, pack_rest, pairs[1].start, pairs[2].start, pairs[0].done, g0.along_z,
             functools.partial(g0.to_neighbours, 0), pairs[1].done, pairs[2].done,
         ],
         (0, 0): [
@@ -1401,7 +1408,7 @@
     flat = lambda t: t.reshape(docs * slots, width)
     whole = lambda t: t.reshape(docs, slots, width)
     if own_kernels(rows, docs):
-        packed = jnp.concatenate((*vectors, inner_bias)).astype(F)[None]
+        packed = jnp.concatenate((*vectors, inner_bias))[None]
         low, q, k, v, att, lse, hat, inv, norm, act, slope, vec, w0, wa, wb, w2 = forward_fused(
             seg_lengths, tokens, alignment, *weights, packed
         )

time: 227 us -> 232 us (1.022)
  local copies, waits for them, and re-layouts: 0.88 us -> 6.67 us
    concatenate x1, local copies, waits for them, and re-layouts: 0.88 us -> 6.1 us  [shards(): packed = jnp.concatenate((*vectors, inner_bias))[None]]
where the time goes in v7:
time: 232 us
  Pallas kernels  224 us (97%)
  local copies, waits for them, and re-layouts  6.67 us (3%)
    pallas_call x1, Pallas kernels, forward_fused(): pl.pallas_call(forward_fused_kernel, grid=(ATTEND + 2 * TILES,), in_specs...  93.7 us
    pallas_call x1, Pallas kernels, backward_fused(): pl.pallas_call(functools.partial(backward_fused_kernel, widths), grid=(qu...  69.6 us
    pallas_call x1, Pallas kernels, middle(): pl.pallas_call(middle_kernel, grid=(4 * tiles + 1,), in_specs=[pl.BlockSp...  55.8 us
    concatenate x1, local copies, waits for them, and re-layouts, shards(): packed = jnp.concatenate((*vectors, inner_bias))[None]  6.1 us
    pallas_call x1, Pallas kernels, deliver(): pl.pallas_call(functools.partial(deliver_kernel, n), out_shape=[jax.Shape...  5.13 us

profile of v7, /device:TPU:0, one launch (start us, length us, event | category | flops | bytes accessed | tf_op | source)
XLA Modules:
  0.0 231.8 jit_solution(14788009639044403955)
XLA Ops:
  0.7 6.1 %concatenate.3 = bf16[288]{0:T(512)(128)(2,1)S(1)} concatenate(bf16[24]{0:T(256)(128)(2,1)} %param.24, bf16[24]{0:T(256)(128)(2,1)} %param.27, bf16[24]{0:T(256)(128)(2,1)} %param.29, bf16[24]{0:T(256)(128)(2,1)} %param.30, bf16[24]{0:T(256)(128)(2,1)} %param.31, bf16[24]{0:T(256)(128)(2,1)} %param.35, bf16[24]{0:T(256)(128)(2,1)} %param.36, bf16[24]{0:T(256)(128)(2,1)} %param.37, ...), dimensions={0} | concatenate | bytes 1152 | tf_op jit(solution)/shard_map/concatenate | solution.py:1411
  6.8 0.6 broadcast_in_dim.3.vp
  7.3 93.7 %shard_map.314 = (bf16[2,640,768]{2,1,0:T(8,128)(2,1)}, bf16[2,640,768]{2,1,0:T(8,128)(2,1)}, bf16[2,640,768]{2,1,0:T(8,128)(2,1)}, bf16[2,640,768]{2,1,0:T(8,12...) custom-call(s32[2]{0:T(128)} %refs_0_.1, ...), custom_call_target="tpu_custom_call" | custom-call | tf_op jit(solution)/shard_map/pallas_call | solution.py:988
  101.1 55.8 %shard_map.315 = (bf16[1280,768]{1,0:T(8,128)(2,1)}, f32[1280,768]{1,0:T(8,128)}, bf16[1280,768]{1,0:T(8,128)(2,1)}, bf16[768,3840]{1,0:T(8,128)(2,1)}, f32[8,76...) custom-call(f32[1280,768]{1,0:T(8,128)} %get-tuple-element.65.hat_ref, f32[1280,128]{1,0:T(8,128)} %get-tuple-element.66.inv_ref, ...), custom_call_target="tpu_custom_call" | custom-call | tf_op jit(solution)/shard_map/pallas_call | solution.py:1163
  156.9 69.6 %shard_map.316 = (bf16[2,640,768]{2,1,0:T(8,128)(2,1)}, f32[24,768]{1,0:T(8,128)}, f32[24,768]{1,0:T(8,128)}, f32[24,768]{1,0:T(8,128)}, f32[24,768]{1,0:T(8,128...) custom-call(s32[2]{0:T(128)} %refs_0_.1, s32[2,512]{1,0:T(2,128)} %refs_1_.1, ...), custom_call_target="tpu_custom_call" | custom-call | tf_op jit(solution)/shard_map/pallas_call | solution.py:1307
  226.5 5.1 %shard_map.317 = (bf16[2,640,768]{2,1,0:T(8,128)(2,1)}, bf16[2,640,768]{2,1,0:T(8,128)(2,1)}, f32[24,768]{1,0:T(8,128)}, f32[24,768]{1,0:T(8,128)}, f32[24,768]{...) custom-call(bf16[2,640,768]{2,1,0:T(8,128)(2,1)} %bitcast.12, ...), custom_call_target="tpu_custom_call" | custom-call | tf_op jit(solution)/shard_map/pallas_call | solution.py:1382
